TPU v7x, 256 devices: a whole 4x4x8 slice. The times are simulated.
256 devices in a mesh: lat: 64 (over x, z, y_hi), lon: 4 (over y_lo, core).
Axes of the slice: x: 4, y: 4 (y_hi: 2, y_lo: 2; y = y_hi * 2 + y_lo), z: 8, core: 2. Of those that a mesh axis runs over, the one named last changes fastest.
Arguments:
- inputs: bfloat16 [512, 1024, 512], P('lat', 'lon'), may hold values from -22 to 22
- cotangent: bfloat16 [512, 1024, 512], P('lat', 'lon'), may hold values from -16 to 16
- basis_values: float32 [512, 5, 9], replicated, may hold values from -0.6 to 0.6
- basis_index: int32 [512, 5, 9], replicated, may hold values from 0 to 8
- lon_reach: int32 [512, 5], replicated, may hold values from 1 to 4
- filters: float32 [512, 9], replicated, may hold values from -4 to 4
- weight_in: bfloat16 [512, 512], replicated, may hold values from -0.25 to 0.25
- weight_out: bfloat16 [512, 512], replicated, may hold values from -0.25 to 0.25
Outputs:
- output: bfloat16 [512, 1024, 512], P('lat', 'lon')
- grad_inputs: bfloat16 [512, 1024, 512], P('lat', 'lon')
- grad_weight_in: float32 [512, 512], P('lat')
- grad_weight_out: float32 [512, 512], P(None, 'lat')
- grad_filters: float32 [512, 9], P('lat')
All inputs are finite; a program needn't handle non-finite values.
Results may differ from a plain program's by a relative error of at most 0.023.
Values may be sent and summed in bfloat16 or wider, within the bound.
No kernel may reach another device: no remote copies, remote signals or barrier semaphores. Data moves between devices by JAX's collectives and lax.ppermute only.
A program may use at most 128 MiB of HBM per device.

v0:
```python
import jax
import jax.numpy as jnp
from jax import lax
from jax.sharding import PartitionSpec as P

CH = 512
BASIS = 9
REACH_LAT = 2
REACH_LON = 4


eps = 1e-06


def extended(block, sides, width, periodic):
    for axis, dim in sides:
        count = lax.axis_size(axis)
        forward = [(i, i + 1) for i in range(count - 1)]
        if periodic:
            forward.append((count - 1, 0))
        backward = [(target, source) for source, target in forward]
        low = lax.ppermute(
            lax.slice_in_dim(block, block.shape[dim] - width, None, axis=dim), axis, forward
        )
        high = lax.ppermute(lax.slice_in_dim(block, 0, width, axis=dim), axis, backward)
        block = jnp.concatenate([low, block, high], axis=dim)
    return block


def tap_tables(basis_values, basis_index, lon_reach, filters):
    lon_taps = jnp.arange(2 * REACH_LON + 1) - REACH_LON
    within = (jnp.abs(lon_taps)[None, None, :] <= lon_reach[:, :, None]).astype(jnp.float32)
    onehot = (basis_index[:, :, :, None] == jnp.arange(BASIS)[None, None, None, :]).astype(
        jnp.float32
    )
    tap_weights = onehot * (basis_values * within)[:, :, :, None]
    coeffs = jnp.einsum("rabk,ck->rabc", tap_weights, filters)
    return (tap_weights, coeffs)


def forward_taps(coeffs, wrapped, row_count, col_count):
    result = jnp.zeros((row_count, col_count, coeffs.shape[-1]), jnp.float32)
    for row_tap in range(2 * REACH_LAT + 1):
        for col_tap in range(2 * REACH_LON + 1):
            piece = wrapped[row_tap : row_tap + row_count, col_tap : col_tap + col_count].astype(
                jnp.float32
            )
            result = result + coeffs[:, row_tap, col_tap][:, None, :] * piece
    return result


def adjoint_taps(coeffs_ext, wrapped, row_count, col_count):
    result = jnp.zeros((row_count, col_count, coeffs_ext.shape[-1]), jnp.float32)
    for row_tap in range(2 * REACH_LAT + 1):
        row_first = 2 * REACH_LAT - row_tap
        for col_tap in range(2 * REACH_LON + 1):
            col_first = 2 * REACH_LON - col_tap
            piece = wrapped[
                row_first : row_first + row_count, col_first : col_first + col_count
            ].astype(jnp.float32)
            result = (
                result
                + coeffs_ext[row_first : row_first + row_count, row_tap, col_tap][:, None, :]
                * piece
            )
    return result


def tap_products(wrapped, grad_filtered, row_count, col_count):
    cotan = grad_filtered.astype(jnp.float32)
    pieces = []
    for row_tap in range(2 * REACH_LAT + 1):
        for col_tap in range(2 * REACH_LON + 1):
            piece = wrapped[row_tap : row_tap + row_count, col_tap : col_tap + col_count].astype(
                jnp.float32
            )
            pieces.append(jnp.sum(piece * cotan, axis=1))
    stacked = jnp.stack(pieces, axis=1)
    return stacked.reshape(row_count, 2 * REACH_LAT + 1, 2 * REACH_LON + 1, cotan.shape[-1])


def square_sum(grad_parts):
    return (
        jnp.sum(grad_parts[0] * grad_parts[0])
        + jnp.sum(grad_parts[1] * grad_parts[1])
        + jnp.sum(grad_parts[2] * grad_parts[2])
    )


def local(inputs, cotangent, basis_values, basis_index, lon_reach, filters, weight_in, weight_out):
    row_count, col_count, chans = inputs.shape
    band_index = lax.axis_index("lat")
    first_row = band_index * row_count
    span = row_count + 2 * REACH_LAT
    pad_rows = ((REACH_LAT, REACH_LAT), (0, 0), (0, 0))
    values_band = lax.dynamic_slice_in_dim(jnp.pad(basis_values, pad_rows), first_row, span, 0)
    index_band = lax.dynamic_slice_in_dim(jnp.pad(basis_index, pad_rows), first_row, span, 0)
    reach_band = lax.dynamic_slice_in_dim(
        jnp.pad(lon_reach, ((REACH_LAT, REACH_LAT), (0, 0))), first_row, span, 0
    )
    weights_ext, coeffs_ext = tap_tables(values_band, index_band, reach_band, filters)
    local_coeffs = coeffs_ext[REACH_LAT : REACH_LAT + row_count]
    local_weights = weights_ext[REACH_LAT : REACH_LAT + row_count]
    padded = extended(inputs, (("lat", 0),), REACH_LAT, False)
    wrapped = extended(padded, (("lon", 1),), REACH_LON, True)
    filtered = forward_taps(local_coeffs, wrapped, row_count, col_count)
    low = filtered.astype(jnp.bfloat16).reshape(-1, chans)
    hidden = jnp.dot(low, weight_in, preferred_element_type=jnp.float32)
    activated, gelu_back = jax.vjp(jax.nn.gelu, hidden)
    act_low = activated.astype(jnp.bfloat16)
    mixed_out = jnp.dot(act_low, weight_out, preferred_element_type=jnp.float32)
    output = (
        (inputs.astype(jnp.float32).reshape(-1, chans) + mixed_out)
        .astype(jnp.bfloat16)
        .reshape(inputs.shape)
    )
    cot_flat = cotangent.reshape(-1, chans)
    grad_out = jnp.dot(act_low.T, cot_flat, preferred_element_type=jnp.float32)
    grad_act = jnp.dot(cot_flat, weight_out.T, preferred_element_type=jnp.float32)
    grad_hidden = gelu_back(grad_act)[0].astype(jnp.bfloat16)
    grad_in = jnp.dot(low.T, grad_hidden, preferred_element_type=jnp.float32)
    grad_filtered = (
        jnp.dot(grad_hidden, weight_in.T, preferred_element_type=jnp.float32)
        .astype(jnp.bfloat16)
        .reshape(inputs.shape)
    )
    grad_filt = jnp.einsum(
        "rabk,rabc->ck", local_weights, tap_products(wrapped, grad_filtered, row_count, col_count)
    )
    grad_padded = extended(grad_filtered, (("lat", 0),), REACH_LAT, False)
    grad_wrapped = extended(grad_padded, (("lon", 1),), REACH_LON, True)
    back = adjoint_taps(coeffs_ext, grad_wrapped, row_count, col_count)
    grad_inputs = (cotangent.astype(jnp.float32) + back).astype(jnp.bfloat16)
    summed = lax.psum((grad_in, grad_out, grad_filt), "lon")
    shares = (
        lax.psum_scatter(summed[0], "lat", scatter_dimension=0, tiled=True),
        lax.psum_scatter(summed[1], "lat", scatter_dimension=1, tiled=True),
        lax.psum_scatter(summed[2], "lat", scatter_dimension=0, tiled=True),
    )
    grad_total = lax.psum(square_sum(shares), "lat")
    clip_scale = jnp.minimum(jnp.float32(1.0), jnp.float32(CH) / jnp.sqrt(grad_total + eps))
    return (
        output,
        grad_inputs,
        clip_scale * shares[0],
        clip_scale * shares[1],
        clip_scale * shares[2],
    )


def solution(mesh):
    placed = (P("lat", "lon", None), P("lat", "lon", None), P(), P(), P(), P(), P(), P())
    return jax.shard_map(
        local,
        mesh=mesh,
        in_specs=placed,
        out_specs=(
            P("lat", "lon", None),
            P("lat", "lon", None),
            P("lat", None),
            P(None, "lat"),
            P("lat", None),
        ),
        check_vma=False,
    )
```

profile of v0, /device:TPU:8, one launch (start us, length us, event | category | flops | bytes accessed | tf_op | source)
XLA Modules:
  0.0 1122.5 jit_solution(1312743123192925414)
XLA Ops:
  7.2 2.3 fusion.174
  9.6 5.0 collective-permute-start
  14.6 1.3 collective-permute-start.1
  15.9 0.9 pad_dynamic-slice_fusion.2
  16.8 1.0 fusion.167
  17.8 1.0 pad_dynamic-slice_fusion.1
  18.8 1.2 fusion.165
  20.0 0.7 slice_bitcast_fusion.34
  20.7 0.7 slice_bitcast_fusion.35
  21.4 3.3 fusion.177
  24.8 0.6 slice_bitcast_fusion.80
  25.7 10.8 collective-permute-done
  36.5 1.1 constant_dynamic-update-slice_fusion.2
  37.6 0.7 constant_dynamic-update-slice_fusion.1
  38.3 1.5 constant_dynamic-update-slice_fusion
  39.9 1.7 copy-done.1
  41.5 0.9 fusion.172
  42.9 0.6 slice_bitcast_fusion.78
  44.8 1.7 collective-permute-done.2
  46.6 57.7 %fusion.121 = bf16[8,256,512]{2,1,0:T(8,128)(2,1)} fusion(f32[8,512]{1,0:T(8,128)S(1)} %copy-done.17, f32[8,512]{1,0:T(8,128)S(1)} %copy-done.18, f32[8,512]{1,0:T(8,128)S(1)} %get-tuple-element.111, f32[8,512]{1,0:T(8,128)S(1)} %get-tuple-element.112, f32[8,512]{1,0:T(8,128)S(1)} %get-tuple-element.113, f32[8,512]{1,0:T(8,128)S(1)} %get-tuple-element.114, ...), kind=kLoop, calls=%fused_computation.253 | loop fusion | flops 267386880 | bytes 16564224 | tf_op jit(solution)/shard_map/convert_element_type | solution.py:107
  104.3 7.1 fusion.50
  111.4 1.3 copy-done.35
  112.7 2.3 fusion.178
  115.3 9.6 fusion.114
  125.0 1.1 fusion.173
  126.1 5.6 collective-permute-start.4
  131.6 1.3 collective-permute-start.5
  133.0 5.4 fusion.116
  138.4 6.1 fusion.119
  144.5 4.1 fusion.113
  148.7 4.9 fusion.118
  153.7 4.1 fusion.112
  157.9 5.0 fusion.117
  163.1 0.7 copy-done.33
  163.8 2.9 fusion.170
  168.0 2.0 convolution_bitcast_fusion
  170.0 370.4 %all-reduce.3 = f32[512,9]{1,0:T(8,128)S(1)} all-reduce(f32[512,9]{1,0:T(8,128)} %convolution_bitcast_fusion), channel_id=4, replica_groups=mesh['lat'=64,'lon'=4] {'lat'}, use_global_device_ids=true, to_apply=%region_52.53.clone | all-reduce | flops 4608 | bytes 36864
  540.4 6.2 fusion.120
  546.6 0.8 pad_maximum_fusion.7
  548.1 1.1 collective-permute-done.6
  549.2 2.2 collective-permute-done.7
  551.4 4.5 pad_maximum_fusion
  555.9 292.1 %reduce-scatter.5.cloned.1.call-done = f32[512,8]{0,1:T(8,128)} async-done(((f32[512,512]{0,1:T(8,128)}), f32[512,8]{0,1:T(8,128)}) %reduce-scatter.5.cloned.1.call-update) | async-done | bytes 16400 | tf_op jit(solution)/shard_map/reduce_scatter | solution.py:137
  847.9 11.3 %all-reduce.4 = (f32[8,512]{1,0:T(8,128)S(1)}, f32[512,8]{0,1:T(8,128)S(1)}, f32[8,9]{1,0:T(8,128)S(1)}) all-reduce(f32[8,512]{1,0:T(8,128)} %reduce-scatter.3.cloned.1.call-done, f32[512,8]{0,1:T(8,128)} %reduce-scatter.5.cloned.1.call-done, f32[8,9]{1,0:T(8,128)S(1)} %constant_dynamic-slice_fusion), channel_id=1, replica_groups=mesh['lat'=64,'lon'=4] {'lon'}, use_global_device_ids=true, to_apply=%region_0.1 | all-reduce | flops 8264 | bytes 66112 | tf_op jit(solution)/shard_map/psum | solution.py:134
  859.3 0.6 multiply_reduce_fusion.2
  863.2 71.6 %fusion.122 = bf16[8,256,512]{2,1,0:T(8,128)(2,1)} fusion(bf16[8,256,512]{2,1,0:T(8,128)(2,1)S(1)} %bitcast.340, bf16[8,256,512]{2,1,0:T(8,128)(2,1)} %param.9, bf16[2,256,512]{2,1,0:T(8,128)(2,1)S(1)} %collective-permute-done.4, bf16[2,256,512]{2,1,0:T(8,128)(2,1)} %collective-permute-done.5, bf16[12,260,512]{2,1,0:T(8,128)(2,1)} %get-tuple-element.60, ...), kind=kLoop, calls=%fused_computation.254 | loop fusion | flops 147849216 | bytes 91963392 | tf_op jit(solution)/shard_map/convert_element_type | solution.py:133
  934.8 178.2 %psum.31 = f32[]{:T(128)} all-reduce(f32[]{:T(128)S(6)} %add.410), channel_id=1, replica_groups=mesh['lat'=64,'lon'=4] {'lat'}, use_global_device_ids=true, to_apply=%region_54.55 | all-reduce | flops 1 | bytes 8 | tf_op jit(solution)/shard_map/psum | solution.py:140
  1114.9 0.6 broadcast_multiply_fusion.1
  (140 shorter events, 6.3 us)
Async XLA Ops:
  7.2 97.1 %copy-start = (bf16[512,512]{1,0:T(8,128)(2,1)S(1)}, bf16[512,512]{1,0:T(8,128)(2,1)}, u32[]{:S(2)}) copy-start(bf16[512,512]{1,0:T(8,128)(2,1)} %param.14) | copy-start | bytes 1572868
  7.2 14.2 %copy-start.12 = (bf16[512,512]{1,0:T(8,128)(2,1)S(1)}, bf16[512,512]{1,0:T(8,128)(2,1)}, u32[]{:S(2)}) copy-start(bf16[512,512]{1,0:T(8,128)(2,1)} %param.15) | copy-start | bytes 1572868
  7.2 548.7 %reduce-scatter.3.cloned.1.call-start = ((), (), s32[]{:S(2)}) async-start(), calls=%async_computation.2 | async-start | bytes 1064960 | tf_op jit(solution)/shard_map/reduce_scatter | solution.py:136
  9.6 26.9 %collective-permute-start = (bf16[2,256,512]{2,1,0:T(8,128)(2,1)}, bf16[2,256,512]{2,1,0:T(8,128)(2,1)}, u32[]{:S(2)}, u32[]{:S(2)}) collective-permute-start(bf16[2,256,512]{2,1,0:T(8,128)(2,1)} %get-tuple-element.70), channel_id=1, source_target_pairs={{0,4},{4,8},{8,12},{12,16},{16,20},{20,24},{24,28},{28,32},{32,36}... | collective-permute-start | bytes 1572872 | tf_op jit(solution)/shard_map/ppermute | solution.py:22
  14.6 23.7 %collective-permute-start.1 = (bf16[2,256,512]{2,1,0:T(8,128)(2,1)}, bf16[2,256,512]{2,1,0:T(8,128)(2,1)}, u32[]{:S(2)}, u32[]{:S(2)}) collective-permute-start(bf16[2,256,512]{2,1,0:T(8,128)(2,1)} %get-tuple-element.71), channel_id=1, source_target_pairs={{4,0},{8,4},{12,8},{16,12},{20,16},{24,20},{28,24},{32,28},{36,32}... | collective-permute-start | bytes 1572872 | tf_op jit(solution)/shard_map/ppermute | solution.py:25
  15.9 5.5 copy-start.9
  21.4 16.2 %copy-start.7 = (bf16[8,256,512]{2,1,0:T(8,128)(2,1)S(1)}, bf16[8,256,512]{2,1,0:T(8,128)(2,1)}, u32[]{:S(2)}) copy-start(bf16[8,256,512]{2,1,0:T(8,128)(2,1)} %param.8) | copy-start | bytes 6291460
  25.4 21.1 %copy-start.13 = (f32[8,512]{1,0:T(8,128)}, f32[8,512]{1,0:T(8,128)S(1)}, u32[]{:S(2)}) copy-start(f32[8,512]{1,0:T(8,128)S(1)} %get-tuple-element.127) | copy-start | bytes 49156
  25.4 21.1 %copy-start.15 = (f32[8,512]{1,0:T(8,128)}, f32[8,512]{1,0:T(8,128)S(1)}, u32[]{:S(2)}) copy-start(f32[8,512]{1,0:T(8,128)S(1)} %get-tuple-element.128) | copy-start | bytes 49156
  37.6 5.9 copy-start.34
  37.6 8.9 copy-start.17
  37.6 8.9 copy-start.18
  38.3 4.1 copy-start.5
  39.9 1.7 copy-start.1
  39.9 2.5 copy-start.3
  42.4 2.4 collective-permute-start.3
  42.4 4.1 collective-permute-start.2
  104.2 8.5 copy-start.11
  111.4 1.3 copy-start.35
  115.0 733.0 %reduce-scatter.5.cloned.1.call-start = ((), (), s32[]{:S(2)}) async-start(), calls=%async_computation.3 | async-start | bytes 1064960 | tf_op jit(solution)/shard_map/reduce_scatter | solution.py:137
  115.3 17.7 %copy-start.2 = (bf16[12,256,512]{2,1,0:T(8,128)(2,1)S(1)}, bf16[12,256,512]{2,1,0:T(8,128)(2,1)}, u32[]{:S(2)}) copy-start(bf16[12,256,512]{2,1,0:T(8,128)(2,1)} %copy-done.1) | copy-start | bytes 9437188
  115.3 17.7 %copy-start.4 = (bf16[10,256,512]{2,1,0:T(8,128)(2,1)S(1)}, bf16[10,256,512]{2,1,0:T(8,128)(2,1)}, u32[]{:S(2)}) copy-start(bf16[10,256,512]{2,1,0:T(8,128)(2,1)} %copy-done.3) | copy-start | bytes 7864324
  115.3 17.7 %copy-start.6 = (bf16[10,256,512]{2,1,0:T(8,128)(2,1)S(1)}, bf16[10,256,512]{2,1,0:T(8,128)(2,1)}, u32[]{:S(2)}) copy-start(bf16[10,256,512]{2,1,0:T(8,128)(2,1)} %copy-done.5) | copy-start | bytes 7864324
  126.1 420.5 %collective-permute-start.4 = (bf16[2,256,512]{2,1,0:T(8,128)(2,1)}, bf16[2,256,512]{2,1,0:T(8,128)(2,1)S(1)}, u32[]{:S(2)}, u32[]{:S(2)}) collective-permute-start(bf16[2,256,512]{2,1,0:T(8,128)(2,1)} %bitcast.52), channel_id=1, source_target_pairs={{0,4},{4,8},{8,12},{12,16},{16,20},{20,24},{24,28},{28,32},{32,36}... | collective-permute-start | bytes 1572872 | tf_op jit(solution)/shard_map/ppermute | solution.py:22
  131.6 414.9 %collective-permute-start.5 = (bf16[2,256,512]{2,1,0:T(8,128)(2,1)}, bf16[2,256,512]{2,1,0:T(8,128)(2,1)}, u32[]{:S(2)}, u32[]{:S(2)}) collective-permute-start(bf16[2,256,512]{2,1,0:T(8,128)(2,1)} %bitcast.54), channel_id=1, source_target_pairs={{4,0},{8,4},{12,8},{16,12},{20,16},{24,20},{28,24},{32,28},{36,32}... | collective-permute-start | bytes 1572872 | tf_op jit(solution)/shard_map/ppermute | solution.py:25
  133.0 5.4 copy-start.8
  153.7 10.1 copy-start.36
  157.9 6.0 copy-start.10
  163.1 0.7 copy-start.33
  163.8 3.5 copy-start.32
  547.3 1.8 collective-permute-start.6
  547.4 4.0 collective-permute-start.7
  547.9 315.1 %copy-start.14 = (f32[8,512]{1,0:T(8,128)S(1)}, f32[8,512]{1,0:T(8,128)}, u32[]{:S(2)}) copy-start(f32[8,512]{1,0:T(8,128)} %copy-done.13) | copy-start | bytes 49156
  547.9 315.1 %copy-start.16 = (f32[8,512]{1,0:T(8,128)S(1)}, f32[8,512]{1,0:T(8,128)}, u32[]{:S(2)}) copy-start(f32[8,512]{1,0:T(8,128)} %copy-done.15) | copy-start | bytes 49156
  547.9 315.1 %copy-start.19 = (f32[8,512]{1,0:T(8,128)S(1)}, f32[8,512]{1,0:T(8,128)}, u32[]{:S(2)}) copy-start(f32[8,512]{1,0:T(8,128)} %get-tuple-element.91) | copy-start | bytes 49156
  547.9 315.1 %copy-start.20 = (f32[8,512]{1,0:T(8,128)S(1)}, f32[8,512]{1,0:T(8,128)}, u32[]{:S(2)}) copy-start(f32[8,512]{1,0:T(8,128)} %get-tuple-element.92) | copy-start | bytes 49156
  547.9 315.1 %copy-start.21 = (f32[8,512]{1,0:T(8,128)S(1)}, f32[8,512]{1,0:T(8,128)}, u32[]{:S(2)}) copy-start(f32[8,512]{1,0:T(8,128)} %get-tuple-element.93) | copy-start | bytes 49156
  548.0 315.1 %copy-start.22 = (f32[8,512]{1,0:T(8,128)S(1)}, f32[8,512]{1,0:T(8,128)}, u32[]{:S(2)}) copy-start(f32[8,512]{1,0:T(8,128)} %get-tuple-element.94) | copy-start | bytes 49156
  548.0 315.1 %copy-start.23 = (f32[8,512]{1,0:T(8,128)S(1)}, f32[8,512]{1,0:T(8,128)}, u32[]{:S(2)}) copy-start(f32[8,512]{1,0:T(8,128)} %get-tuple-element.95) | copy-start | bytes 49156
  548.0 315.1 %copy-start.24 = (f32[8,512]{1,0:T(8,128)S(1)}, f32[8,512]{1,0:T(8,128)}, u32[]{:S(2)}) copy-start(f32[8,512]{1,0:T(8,128)} %get-tuple-element.96) | copy-start | bytes 49156
  548.0 315.1 %copy-start.25 = (f32[8,512]{1,0:T(8,128)S(1)}, f32[8,512]{1,0:T(8,128)}, u32[]{:S(2)}) copy-start(f32[8,512]{1,0:T(8,128)} %get-tuple-element.97) | copy-start | bytes 49156
  548.0 315.1 %copy-start.26 = (f32[8,512]{1,0:T(8,128)S(1)}, f32[8,512]{1,0:T(8,128)}, u32[]{:S(2)}) copy-start(f32[8,512]{1,0:T(8,128)} %get-tuple-element.98) | copy-start | bytes 49156
  548.0 315.1 %copy-start.27 = (f32[8,512]{1,0:T(8,128)S(1)}, f32[8,512]{1,0:T(8,128)}, u32[]{:S(2)}) copy-start(f32[8,512]{1,0:T(8,128)} %get-tuple-element.99) | copy-start | bytes 49156
  548.0 315.1 %copy-start.28 = (f32[8,512]{1,0:T(8,128)S(1)}, f32[8,512]{1,0:T(8,128)}, u32[]{:S(2)}) copy-start(f32[8,512]{1,0:T(8,128)} %get-tuple-element.100) | copy-start | bytes 49156
  548.0 315.1 %copy-start.29 = (f32[8,512]{1,0:T(8,128)S(1)}, f32[8,512]{1,0:T(8,128)}, u32[]{:S(2)}) copy-start(f32[8,512]{1,0:T(8,128)} %get-tuple-element.101) | copy-start | bytes 49156
  548.0 315.1 %copy-start.30 = (f32[8,512]{1,0:T(8,128)S(1)}, f32[8,512]{1,0:T(8,128)}, u32[]{:S(2)}) copy-start(f32[8,512]{1,0:T(8,128)} %get-tuple-element.102) | copy-start | bytes 49156
  548.0 315.1 %copy-start.31 = (f32[8,512]{1,0:T(8,128)S(1)}, f32[8,512]{1,0:T(8,128)}, u32[]{:S(2)}) copy-start(f32[8,512]{1,0:T(8,128)} %get-tuple-element.103) | copy-start | bytes 49156
Sparse Core Ops, SparseCore 0:
  115.1 371.6 reduce-scatter.2
  489.5 358.4 reduce-scatter.4
where the time goes:
time: 1130 us; the launch traced here: 1120 us
  blocking collectives  560 us (50%)
  waiting for transfers between devices  308 us (27%)
  other arithmetic  169 us (15%)
  matrix products  34.6 us (3%)
  between operations  18.4 us (2%)
  local copies, waits for them, and re-layouts  18 us (2%)
  starting transfers between devices  14.6 us (1%)
    unnamed x1, blocking collectives  370 us
    reduce_scatter x1, waiting for transfers between devices, local(): lax.psum_scatter(summed[1], 'lat', scatter_dimension=1, tiled=True)  292 us
    psum x1, blocking collectives, local(): grad_total = lax.psum(square_sum(shares), 'lat')  178 us
    convert_element_type x1, other arithmetic, local(): grad_inputs = (cotangent.astype(jnp.float32) + back).astype(jnp.bfloat16)  71.6 us
    convert_element_type x1, other arithmetic, local(): low = filtered.astype(jnp.bfloat16).reshape(-1, chans)  57.7 us
    reduce_sum x6, other arithmetic, tap_products(): pieces.append(jnp.sum(piece * cotan, axis=1))  29.6 us
  transfers between devices with their start and end apart: 10, of which 5 were waited for; matrix products, arithmetic and copies ran while one was open for 6% of the time, Pallas kernels for 0%

commit v1 on v0

v1 whole, which is shorter than its diff:
```python
import functools
import math

import jax
import jax.numpy as jnp
import numpy as np
from jax import lax
from jax.experimental import pallas as pl
from jax.experimental.pallas import tpu as pltpu
from jax.sharding import PartitionSpec as P

BASIS = 9
REACH_LAT = 2
REACH_LON = 4
ROW_TAPS = 2 * REACH_LAT + 1
COL_TAPS = 2 * REACH_LON + 1
PAIR = 2
WIN = PAIR + 2 * REACH_LAT
TILE = 16
HALF = TILE // 2
SPAN = 2 * TILE
CLIP = 512.0
EPS = 1e-06
BF = jnp.bfloat16
F32 = jnp.float32
VMEM_LIMIT = 56 * 1024 * 1024


def column_offsets():
    w = np.arange(SPAN)
    return np.where(w < HALF, w + TILE, w - TILE)


def band_constants(pairs):
    off = column_offsets()
    b = np.arange(COL_TAPS)[:, None, None]
    j = np.arange(TILE)[None, :, None]
    fwd = off[None, None, :] == j + b - REACH_LON
    adj = off[None, None, :] == j - b + REACH_LON
    ext = PAIR * pairs + 2 * REACH_LAT
    shape = (pairs, PAIR, WIN, ext, ROW_TAPS)
    pick_f, pick_a = np.zeros(shape), np.zeros(shape)
    for p in range(pairs):
        for r in range(PAIR):
            for a in range(WIN):
                if 0 <= a - r < ROW_TAPS:
                    pick_f[p, r, a, PAIR * p + r + REACH_LAT, a - r] = 1
                    pick_a[p, r, a, PAIR * p + a, r - a + 2 * REACH_LAT] = 1
    return fwd, adj, pick_f, pick_a


def band_matrices(tap_weights, pairs):
    fwd, adj, pick_f, pick_a = band_constants(pairs)
    taps = tap_weights.astype(BF)
    ext = taps.shape[0]
    pick = jnp.asarray(np.stack([pick_f, pick_a]).reshape(-1, ext * ROW_TAPS), BF)
    rows = jnp.dot(pick, taps.reshape(ext * ROW_TAPS, -1), preferred_element_type=F32).astype(BF)
    rows = rows.reshape(2, pairs, PAIR, WIN, COL_TAPS, BASIS)
    out = []
    for which, band in enumerate((fwd, adj)):
        full = jnp.einsum(
            "prabk,bjw->pkrjaw", rows[which], jnp.asarray(band, BF), preferred_element_type=F32
        )
        out.append(full.astype(BF).reshape(pairs, BASIS * PAIR * TILE, WIN * SPAN))
    return out


def dot(a, b, ca, cb):
    return lax.dot_general(a, b, (((ca,), (cb,)), ((), ())), preferred_element_type=F32)


def window(rows, sides, m, tiles):
    parts = []
    for row, side in zip(rows, sides):
        if m + 1 < tiles:
            right = row[(m + 1) * TILE : (m + 2) * TILE, :].astype(F32)[:HALF]
        else:
            right = side[...].astype(F32)[:HALF]
        if m > 0:
            left = row[(m - 1) * TILE : m * TILE, :].astype(F32)[HALF:]
        else:
            left = side[...].astype(F32)[HALF:]
        parts.append(jnp.concatenate([right, left], axis=0).astype(BF))
        parts.append(row[m * TILE : (m + 1) * TILE, :])
    return jnp.concatenate(parts, axis=0)


def mixer_body(
    rows, sides, band, filt, w_in, w_out, cot, out, gf, edge, gin, gout, gfilt, prev,
    y, low, hid, gact, act, gh,
):
    cols, chans = cot.shape[1:]
    tiles = cols // TILE
    cells = PAIR * cols
    for m in range(tiles):
        full = jnp.dot(band[0], window(rows, sides, m, tiles), preferred_element_type=F32)
        for r in range(PAIR):
            at = pl.ds(r * cols + m * TILE, TILE)
            total = None
            for k in range(BASIS):
                first = (k * PAIR + r) * TILE
                piece = full[first : first + TILE]
                y[k, at, :] = piece
                term = filt[k : k + 1, :] * piece
                total = term if total is None else total + term
            low[at, :] = total.astype(BF)
    cot_flat = cot[...].reshape(cells, chans)
    hid[...] = dot(low[...], w_in[...], 1, 0)
    gact[...] = dot(cot_flat, w_out[...], 1, 1)
    root = math.sqrt(2.0 / math.pi)
    step = 2 * TILE

    def pointwise(n, carry):
        at = pl.ds(pl.multiple_of(n * step, step), step)
        v = hid[at, :]
        sq = v * v
        t = jnp.tanh(v * (root + (root * 0.044715) * sq))
        half = 0.5 + 0.5 * t
        act[at, :] = (v * half).astype(BF)
        slope = half + (0.5 * v) * (1.0 - t * t) * (root + (3 * root * 0.044715) * sq)
        gh[at, :] = (gact[at, :] * slope).astype(BF)
        return carry

    lax.fori_loop(0, cells // step, pointwise, 0)
    mixed = dot(act[...], w_out[...], 1, 0)
    back = dot(gh[...], w_in[...], 1, 1)
    for r in range(PAIR):
        part = slice(r * cols, (r + 1) * cols)
        out[r] = (rows[REACH_LAT + r][...].astype(F32) + mixed[part]).astype(BF)
        gf[r] = back[part].astype(BF)
        edge[r] = jnp.concatenate(
            [back[r * cols : r * cols + HALF], back[(r + 1) * cols - HALF : (r + 1) * cols]], axis=0
        ).astype(BF)
    more_out = dot(cot_flat, act[...], 0, 0)
    more_in = dot(low[...], gh[...], 0, 0)
    if prev is None:
        first = pl.program_id(0) == 0

        @pl.when(first)
        def _():
            gin[...] = more_in
            gout[...] = more_out
            gfilt[...] = jnp.zeros_like(gfilt)

        @pl.when(jnp.logical_not(first))
        def _():
            gin[...] += more_in
            gout[...] += more_out

    else:
        gin[...] = prev[0][...] + more_in
        gout[...] = prev[1][...] + more_out
        gfilt[...] = prev[2][...]
    lanes = 128
    for c in range(chans // lanes):
        at_c = pl.ds(c * lanes, lanes)

        def correlate(n, sums, at_c=at_c):
            for r in range(PAIR):
                g = gf[r, pl.ds(pl.multiple_of(n * TILE, TILE), TILE), at_c].astype(F32)
                cell = pl.ds(pl.multiple_of(r * cols + n * TILE, TILE), TILE)
                new = []
                for k in range(BASIS):
                    prod = g * y[k, cell, at_c]
                    new.append(sums[k] + (prod[:8] + prod[8:]))
                sums = tuple(new)
            return sums

        zero = tuple(jnp.zeros((8, lanes), F32) for _ in range(BASIS))
        sums = lax.fori_loop(0, tiles, correlate, zero)
        for k in range(BASIS):
            gfilt[8 * k : 8 * k + 8, at_c] += sums[k]


def inner_kernel(x, side, band, filt, w_in, w_out, cot, out, gf, edge, gin, gout, gfilt, *scratch):
    i = pl.program_id(0)
    rows = [x.at[PAIR * i + a] for a in range(WIN)]
    sides = [side.at[PAIR * i + a] for a in range(WIN)]
    mixer_body(
        rows, sides, band, filt, w_in, w_out, cot, out, gf, edge, gin, gout, gfilt, None, *scratch
    )


def outer_kernel(
    low_end, x, side, halo, halo_side, band, filt, w_in, w_out, cot, keep, gin0, gout0, gfilt0,
    out, gf, edge, gin, gout, gfilt, *scratch,
):
    near = range(WIN - REACH_LAT)
    far = range(REACH_LAT)
    rows, sides = [x.at[a] for a in near], [side.at[a] for a in near]
    more_rows, more_sides = [halo.at[a] for a in far], [halo_side.at[a] for a in far]
    if low_end:
        rows, sides = more_rows + rows, more_sides + sides
    else:
        rows, sides = rows + more_rows, sides + more_sides
    mixer_body(
        rows, sides, band, filt, w_in, w_out, cot, out, gf, edge, gin, gout, gfilt,
        (gin0, gout0, gfilt0), *scratch,
    )


def adjoint_body(rows, sides, band, filt, cot, out):
    cols = cot.shape[1]
    tiles = cols // TILE
    for m in range(tiles):
        full = jnp.dot(band[0], window(rows, sides, m, tiles), preferred_element_type=F32)
        at = slice(m * TILE, (m + 1) * TILE)
        for r in range(PAIR):
            total = cot[r, at, :].astype(F32)
            for k in range(BASIS):
                first = (k * PAIR + r) * TILE
                total = total + filt[k : k + 1, :] * full[first : first + TILE]
            out[r, at, :] = total.astype(BF)


def inner_adjoint(top, mid, bottom, side, band, filt, cot, out):
    i = pl.program_id(0)
    for step in range(2):

        @pl.when(i == step)
        def _(step=step):
            every = [top.at[0], top.at[1]] + [mid.at[a] for a in range(4)]
            every = every + [bottom.at[0], bottom.at[1]]
            rows = every[PAIR * step : PAIR * step + WIN]
            sides = [side.at[PAIR * step + a] for a in range(WIN)]
            adjoint_body(rows, sides, band, filt, cot, out)


def outer_adjoint(low_end, end, mid, side, halo, halo_side, band, filt, cot, keep, out):
    far = range(REACH_LAT)
    more_rows, more_sides = [halo.at[a] for a in far], [halo_side.at[a] for a in far]
    own_sides = [side.at[a] for a in range(WIN - REACH_LAT)]
    if low_end:
        rows = more_rows + [end.at[a] for a in far] + [mid.at[a] for a in far]
        sides = more_sides + own_sides
    else:
        rows = [mid.at[a] for a in far] + [end.at[a] for a in far] + more_rows
        sides = own_sides + more_sides
    adjoint_body(rows, sides, band, filt, cot, out)


def whole(shape):
    return pl.BlockSpec(shape, lambda i: (0,) * len(shape))


def pair_block(shape, first):
    return pl.BlockSpec((PAIR,) + shape[1:], lambda i: (first + i,) + (0,) * (len(shape) - 1))


def params():
    return pltpu.CompilerParams(vmem_limit_bytes=VMEM_LIMIT)


def mixer_scratch(cols, chans):
    cells = PAIR * cols
    return [
        pltpu.VMEM((BASIS, cells, chans), F32),
        pltpu.VMEM((cells, chans), BF),
        pltpu.VMEM((cells, chans), F32),
        pltpu.VMEM((cells, chans), F32),
        pltpu.VMEM((cells, chans), BF),
        pltpu.VMEM((cells, chans), BF),
    ]


def mixer_outs(n, cols, chans):
    shapes = (
        jax.ShapeDtypeStruct((n * PAIR, cols, chans), BF),
        jax.ShapeDtypeStruct((n * PAIR, TILE, chans), BF),
        jax.ShapeDtypeStruct((chans, chans), F32),
        jax.ShapeDtypeStruct((chans, chans), F32),
        jax.ShapeDtypeStruct((8 * BASIS, chans), F32),
    )
    specs = [
        pair_block(shapes[0].shape, 0),
        pair_block(shapes[1].shape, 0),
        whole((chans, chans)),
        whole((chans, chans)),
        whole((8 * BASIS, chans)),
    ]
    return shapes, specs


def mixer_cost(n, cols, chans):
    cells = n * PAIR * cols
    flops = 2 * cells * chans * (6 * chans + BASIS * WIN * SPAN)
    return pl.CostEstimate(
        flops=flops, bytes_accessed=10 * cells * chans, transcendentals=cells * chans
    )


def mixer_inner(x, side, band, filt, w_in, w_out, cot):
    rows, cols, chans = x.shape
    shapes, specs = mixer_outs(2, cols, chans)
    return pl.pallas_call(
        inner_kernel,
        grid=(2,),
        in_specs=[
            whole(x.shape), whole(side.shape),
            pl.BlockSpec((1,) + band.shape[1:], lambda i: (1 + i, 0, 0)),
            whole(filt.shape), whole(w_in.shape), whole(w_out.shape), pair_block(cot.shape, 1),
        ],
        out_specs=[pair_block(x.shape, 1)] + specs,
        out_shape=(jax.ShapeDtypeStruct(x.shape, BF),) + shapes,
        scratch_shapes=mixer_scratch(cols, chans),
        compiler_params=params(),
        cost_estimate=mixer_cost(2, cols, chans),
        name="mixer_inner",
    )(x, side, band, filt, w_in, w_out, cot)


def mixer_outer(low_end, x, side, halo, halo_side, band, filt, w_in, w_out, cot, keep, sums):
    rows, cols, chans = x.shape
    pair = 0 if low_end else rows // PAIR - 1
    near = WIN - REACH_LAT
    at = 0 if low_end else rows // near - 1
    shapes, specs = mixer_outs(1, cols, chans)
    return pl.pallas_call(
        functools.partial(outer_kernel, low_end),
        grid=(1,),
        in_specs=[
            pl.BlockSpec((near, cols, chans), lambda i: (at, 0, 0)),
            pl.BlockSpec((near, TILE, chans), lambda i: (at, 0, 0)),
            whole(halo.shape), whole(halo_side.shape),
            pl.BlockSpec((1,) + band.shape[1:], lambda i: (pair, 0, 0)),
            whole(filt.shape), whole(w_in.shape), whole(w_out.shape), pair_block(cot.shape, pair),
            pl.BlockSpec(memory_space=pl.ANY),
        ] + [whole(s.shape) for s in sums],
        out_specs=[pair_block(x.shape, pair)] + specs,
        out_shape=(jax.ShapeDtypeStruct(x.shape, BF),) + shapes,
        scratch_shapes=mixer_scratch(cols, chans),
        input_output_aliases={9: 0, 10: 3, 11: 4, 12: 5},
        compiler_params=params(),
        cost_estimate=mixer_cost(1, cols, chans),
        name="mixer_low" if low_end else "mixer_high",
    )(x, side, halo, halo_side, band, filt, w_in, w_out, cot, keep, *sums)


def adjoint_cost(n, cols, chans):
    cells = n * PAIR * cols
    return pl.CostEstimate(
        flops=2 * cells * chans * BASIS * WIN * SPAN, bytes_accessed=6 * cells * chans,
        transcendentals=0,
    )


def adjoint_inner(top, mid, bottom, side, band, filt, cot):
    rows, cols, chans = cot.shape
    return pl.pallas_call(
        inner_adjoint,
        grid=(2,),
        in_specs=[
            whole(top.shape), whole(mid.shape), whole(bottom.shape), whole(side.shape),
            pl.BlockSpec((1,) + band.shape[1:], lambda i: (1 + i, 0, 0)),
            whole(filt.shape), pair_block(cot.shape, 1),
        ],
        out_specs=pair_block(cot.shape, 1),
        out_shape=jax.ShapeDtypeStruct(cot.shape, BF),
        compiler_params=params(),
        cost_estimate=adjoint_cost(2, cols, chans),
        name="adjoint_inner",
    )(top, mid, bottom, side, band, filt, cot)


def adjoint_outer(low_end, end, mid, side, halo, halo_side, band, filt, cot, keep):
    rows, cols, chans = cot.shape
    pair = 0 if low_end else rows // PAIR - 1
    near = WIN - REACH_LAT
    at = 0 if low_end else rows // near - 1
    return pl.pallas_call(
        functools.partial(outer_adjoint, low_end),
        grid=(1,),
        in_specs=[
            whole(end.shape),
            pl.BlockSpec((REACH_LAT, cols, chans), lambda i: (0 if low_end else 1, 0, 0)),
            pl.BlockSpec((near, TILE, chans), lambda i: (at, 0, 0)),
            whole(halo.shape), whole(halo_side.shape),
            pl.BlockSpec((1,) + band.shape[1:], lambda i: (pair, 0, 0)),
            whole(filt.shape), pair_block(cot.shape, pair),
            pl.BlockSpec(memory_space=pl.ANY),
        ],
        out_specs=pair_block(cot.shape, pair),
        out_shape=jax.ShapeDtypeStruct(cot.shape, BF),
        input_output_aliases={8: 0},
        compiler_params=params(),
        cost_estimate=adjoint_cost(1, cols, chans),
        name="adjoint_low" if low_end else "adjoint_high",
    )(end, mid, side, halo, halo_side, band, filt, cot, keep)


def exchange_columns(first, last):
    count = lax.axis_size("lon")
    up = [(i, (i + 1) % count) for i in range(count)]
    down = [(i, (i - 1) % count) for i in range(count)]
    right = lax.ppermute(first, "lon", down)
    left = lax.ppermute(last, "lon", up)
    return jnp.concatenate([right, left], axis=1)


def to_next(a):
    return lax.ppermute(a, "lat", [(i, i + 1) for i in range(lax.axis_size("lat") - 1)])


def to_last(a):
    return lax.ppermute(a, "lat", [(i + 1, i) for i in range(lax.axis_size("lat") - 1)])


def swap(a, bit):
    count = lax.axis_size("lon")
    return lax.ppermute(a, "lon", [(i, i ^ bit) for i in range(count)])


def reduce_grads(sums, chans):
    bands = lax.axis_size("lat")
    here = lax.axis_index("lon")
    per = chans // bands
    lanes = 128
    gin, gout, gfilt = sums
    filt = gfilt.reshape(BASIS, 8, bands, per).sum(1).transpose(1, 0, 2).reshape(bands, 1, -1)
    beside = jnp.broadcast_to(jnp.pad(filt, ((0, 0), (0, 0), (0, lanes - BASIS * per))), (bands, per, lanes))
    full_in = jnp.concatenate([gin.reshape(bands, per, chans), beside], axis=2)
    full_out = jnp.concatenate([gout.reshape(bands, per, chans), beside], axis=2)
    odd = here % 2 == 1
    keep = jnp.where(odd, full_out, full_in)
    give = jnp.where(odd, full_in, full_out).astype(BF)
    total = keep + swap(give, 1).astype(F32)
    upper = here // 2 == 1
    half = per // 2
    keep = jnp.where(upper, total[:, half:], total[:, :half])
    give = jnp.where(upper, total[:, :half], total[:, half:]).astype(BF)
    part = (keep + swap(give, 2).astype(F32)).astype(BF)
    share = jnp.sum(lax.all_to_all(part, "lat", 0, 0).astype(F32), axis=0)
    mats, filt_row = share[:, :chans], share[:1, chans : chans + BASIS * per]
    count = lax.axis_size("lon")
    square = jnp.sum(mats * mats) + jnp.sum(filt_row * filt_row) / count
    devices = bands * count
    spread = jnp.broadcast_to(square, (devices, 1, lanes))
    every = lax.all_to_all(spread, ("lat", "lon"), 0, 0)
    grad_total = jnp.sum(every[:, 0, 0])
    scale = jnp.minimum(jnp.float32(1.0), jnp.float32(CLIP) / jnp.sqrt(grad_total + EPS))
    other = swap(mats, 2)
    rows = jnp.concatenate(
        [jnp.where(upper, other, mats), jnp.where(upper, mats, other)], axis=0
    )
    across = swap(rows, 1)
    share_in = jnp.where(odd, across, rows)
    share_out = jnp.where(odd, rows, across)
    return (
        scale * share_in,
        (scale * share_out).T,
        scale * filt_row.reshape(BASIS, per).T,
    )


def local(inputs, cotangent, basis_values, basis_index, lon_reach, filters, weight_in, weight_out):
    rows, cols, chans = inputs.shape
    pairs = rows // PAIR
    band_at = lax.axis_index("lat")
    first_row = band_at * rows
    ext = rows + 2 * REACH_LAT
    with jax.named_scope("input_halo"):
        lo = to_next(inputs[rows - REACH_LAT :])
        hi = to_last(inputs[:REACH_LAT])
        side = exchange_columns(inputs[:, :HALF], inputs[:, cols - HALF :])
        lo_side = to_next(side[rows - REACH_LAT :])
        hi_side = to_last(side[:REACH_LAT])
    with jax.named_scope("bands"):
        lat_pad = (REACH_LAT, REACH_LAT)

        def cut(a):
            padded = jnp.pad(a, (lat_pad,) + ((0, 0),) * (a.ndim - 1))
            return lax.dynamic_slice_in_dim(padded, first_row, ext, 0)

        values, index, reach = cut(basis_values), cut(basis_index), cut(lon_reach)
        lon_taps = jnp.abs(jnp.arange(COL_TAPS) - REACH_LON)
        within = lon_taps[None, None, :] <= reach[:, :, None]
        onehot = index[:, :, :, None] == jnp.arange(BASIS)
        taps = jnp.where(onehot & within[..., None], values[..., None], 0.0)
        band, band_adj = band_matrices(taps, pairs)
        filt = jnp.pad(filters.T, ((0, 16 - BASIS), (0, 0)))
    out, gf_mid, edge_mid, *sums = mixer_inner(
        inputs, side, band, filt, weight_in, weight_out, cotangent
    )
    out, gf_lo, edge_lo, *sums = mixer_outer(
        True, inputs, side, lo, lo_side, band, filt, weight_in, weight_out, cotangent, out, sums
    )
    gf_up = to_last(gf_lo)
    out, gf_hi, edge_hi, *sums = mixer_outer(
        False, inputs, side, hi, hi_side, band, filt, weight_in, weight_out, cotangent, out, sums
    )
    with jax.named_scope("grad_halo"):
        gf_down = to_next(gf_hi)
        edge = jnp.concatenate([edge_lo, edge_mid, edge_hi], axis=0)
        gside = exchange_columns(edge[:, :HALF], edge[:, HALF:])
        glo_side = to_next(gside[rows - REACH_LAT :])
        ghi_side = to_last(gside[:REACH_LAT])
    back = adjoint_inner(gf_lo, gf_mid, gf_hi, gside, band_adj, filt, cotangent)
    shares = reduce_grads(sums, chans)
    back = adjoint_outer(
        True, gf_lo, gf_mid, gside, gf_down, glo_side, band_adj, filt, cotangent, back
    )
    back = adjoint_outer(
        False, gf_hi, gf_mid, gside, gf_up, ghi_side, band_adj, filt, cotangent, back
    )
    return (out, back) + shares


def solution(mesh):
    placed = (P("lat", "lon", None), P("lat", "lon", None), P(), P(), P(), P(), P(), P())
    return jax.shard_map(
        local,
        mesh=mesh,
        in_specs=placed,
        out_specs=(
            P("lat", "lon", None),
            P("lat", "lon", None),
            P("lat", None),
            P(None, "lat"),
            P("lat", None),
        ),
        check_vma=False,
    )
```

time: 1130 us -> 175 us (0.15)
  the two profiles are of different devices: /device:TPU:8 before, /device:TPU:2 now
where the time goes in v1:
time: 175 us; the launch traced here: 173 us
  starting transfers between devices  69.3 us (40%)
  Pallas kernels  48.5 us (28%)
  local copies, waits for them, and re-layouts  28.7 us (16%)
  waiting for transfers between devices  11.4 us (7%)
  other arithmetic  8.61 us (5%)
  between operations  3.21 us (2%)
  matrix products  2.93 us (2%)
    ppermute x4, starting transfers between devices, to_last(): lax.ppermute(a, 'lat', [(i + 1, i) for i in range(lax.axis_size('lat') -...  29.7 us
    pallas_call x2, Pallas kernels, mixer_outer(): pl.pallas_call(functools.partial(outer_kernel, low_end), grid=(1,), in_sp...  19.9 us
    pallas_call x1, Pallas kernels, mixer_inner(): pl.pallas_call(inner_kernel, grid=(2,), in_specs=[whole(x.shape), whole(s...  15.6 us
    ppermute x4, starting transfers between devices, to_next(): lax.ppermute(a, 'lat', [(i, i + 1) for i in range(lax.axis_size('lat') -...  13.5 us
    all_to_all x1, starting transfers between devices, reduce_grads(): every = lax.all_to_all(spread, ('lat', 'lon'), 0, 0)  13.4 us
    ppermute x4, waiting for transfers between devices, swap(): return lax.ppermute(a, 'lon', [(i, i ^ bit) for i in range(count)])  10.1 us
    all_to_all x1, starting transfers between devices, reduce_grads(): share = jnp.sum(lax.all_to_all(part, 'lat', 0, 0).astype(F32), axis=0)  8.76 us
    pallas_call x2, Pallas kernels, adjoint_outer(): pl.pallas_call(functools.partial(outer_adjoint, low_end), grid=(1,), in_s...  7.59 us
  transfers between devices with their start and end apart: 18, of which 4 were waited for; matrix products, arithmetic and copies ran while one was open for 15% of the time, Pallas kernels for 22%

profile of v1, /device:TPU:2, one launch (start us, length us, event | category | flops | bytes accessed | tf_op | source)
XLA Modules:
  0.0 172.6 jit_solution(3347339835192044948)
XLA Ops:
  0.7 1.6 fusion.5
  2.2 1.0 collective-permute-start
  3.2 2.3 %fusion.4 = (bf16[2,256,512]{2,1,0:T(8,128)(2,1)}, bf16[2,256,512]{2,1,0:T(8,128)(2,1)}) fusion(bf16[8,256,512]{2,1,0:T(8,128)(2,1)} %x.15), kind=kLoop, calls=%fused_computation.37 | loop fusion | bytes 2097152 | tf_op jit(solution)/shard_map/input_halo/slice | solution.py:462
  5.5 4.8 %collective-permute-start.4 = (bf16[2,256,512]{2,1,0:T(8,128)(2,1)}, bf16[2,256,512]{2,1,0:T(8,128)(2,1)}, u32[]{:S(2)}, u32[]{:S(2)}) collective-permute-start(bf16[2,256,512]{2,1,0:T(8,128)(2,1)} %get-tuple-element.66), channel_id=1, source_target_pairs={{0,4},{4,8},{8,12},{12,16},{16,20},{20,24},{24,28},{28,32},{32,36}... | collective-permute-start | bytes 1572872 | tf_op jit(solution)/shard_map/input_halo/ppermute | solution.py:401
  10.3 7.2 %collective-permute-start.2 = (bf16[2,256,512]{2,1,0:T(8,128)(2,1)}, bf16[2,256,512]{2,1,0:T(8,128)(2,1)}, u32[]{:S(2)}, u32[]{:S(2)}) collective-permute-start(bf16[2,256,512]{2,1,0:T(8,128)(2,1)} %get-tuple-element.67), channel_id=1, source_target_pairs={{4,0},{8,4},{12,8},{16,12},{20,16},{24,20},{28,24},{32,28},{36,32}... | collective-permute-start | bytes 1572872 | tf_op jit(solution)/shard_map/input_halo/ppermute | solution.py:405
  20.0 1.0 copy.74
  21.0 1.8 %convert_bitcast_fusion.1 = bf16[4,9,2,16,6,32]{5,1,3,4,2,0:T(8,128)(2,1)S(1)} fusion(bf16[4,2,6,9,9,1]{3,4,5,2,1,0:T(8,128)(2,1)S(1)} %copy.74, bf16[9,16,32,1,1,1]{2,0,1,5,4,3:T(8,128)(2,1)} %constant.75), kind=kOutput, calls=%fused_computation.1 | convolution fusion | flops 4202496 | bytes 459360 | tf_op jit(solution)/shard_map/bands/prabk,bjw->pkrjaw/dot_general | solution.py:61
  22.8 2.8 %copy.67 = bf16[4,9,2,16,6,32]{5,4,3,2,1,0:T(8,128)(2,1)} copy(bf16[4,9,2,16,6,32]{5,1,3,4,2,0:T(8,128)(2,1)S(1)} %convert_bitcast_fusion.1) | data formatting | bytes 884736 | tf_op jit(solution)/shard_map/bands/convert_element_type | solution.py:64
  25.5 4.0 %reshape.50.band = bf16[4,288,192]{2,1,0:T(8,128)(2,1)} reshape(bf16[4,9,2,16,6,32]{5,4,3,2,1,0:T(8,128)(2,1)} %copy.67) | data formatting | bytes 884736 | tf_op jit(solution)/shard_map/bands/reshape | solution.py:64
  29.5 0.6 pad.23.filt
  30.2 1.9 %collective-permute-start.5 = (bf16[2,16,512]{2,1,0:T(8,128)(2,1)S(1)}, bf16[2,16,512]{2,1,0:T(8,128)(2,1)S(1)}, u32[]{:S(2)}, u32[]{:S(2)}) collective-permute-start(bf16[2,16,512]{2,1,0:T(8,128)(2,1)S(1)} %get-tuple-element.74), channel_id=1, source_target_pairs={{0,4},{4,8},{8,12},{12,16},{16,20},{20,24},{24,28},{28,32},{32,36}... | collective-permute-start | bytes 98312 | tf_op jit(solution)/shard_map/input_halo/ppermute | solution.py:401
  32.1 8.6 %collective-permute-start.3 = (bf16[2,16,512]{2,1,0:T(8,128)(2,1)S(1)}, bf16[2,16,512]{2,1,0:T(8,128)(2,1)S(1)}, u32[]{:S(2)}, u32[]{:S(2)}) collective-permute-start(bf16[2,16,512]{2,1,0:T(8,128)(2,1)S(1)} %get-tuple-element.75), channel_id=1, source_target_pairs={{4,0},{8,4},{12,8},{16,12},{20,16},{24,20},{28,24},{32,28},{36,32}... | collective-permute-start | bytes 98312 | tf_op jit(solution)/shard_map/input_halo/ppermute | solution.py:405
  40.7 15.6 %mixer_inner.1 = (bf16[8,256,512]{2,1,0:T(8,128)(2,1)}, bf16[4,256,512]{2,1,0:T(8,128)(2,1)}, bf16[4,16,512]{2,1,0:T(8,128)(2,1)}, f32[512,512]{1,0:T(8,128)}, f32[512,512]{1,0:T(8,128)}, /*index=5*/f32[72,512]{1,0:T(8,128)}) custom-call(bf16[8,256,512]{2,1,0:T(8,128)(2,1)} %x.15, bf16[8,16,512]{2,1,0:T(8,128)(2,1)} %copy-done.5, ...), custom_call_target="tpu_custom_call" | custom-call | flops 5033164800 | bytes 5242880 | tf_op jit(solution)/shard_map/mixer_inner/pallas_call | solution.py:295
  56.9 9.9 %mixer_low.1 = (bf16[8,256,512]{2,1,0:T(8,128)(2,1)}, bf16[2,256,512]{2,1,0:T(8,128)(2,1)}, bf16[2,16,512]{2,1,0:T(8,128)(2,1)}, f32[512,512]{1,0:T(8,128)}, f32[512,512]{1,0:T(8,128)}, /*index=5*/f32[72,512]{1,0:T(8,128)}) custom-call(bf16[8,256,512]{2,1,0:T(8,128)(2,1)} %x.15, ...), custom_call_target="tpu_custom_call", output_to_operand_aliasing={{0}: (9, {}), {3}: (10, {}), {4}: (11, {}), {5}: (12, {})} | custom-call | flops 2516582400 | bytes 2621440 | tf_op jit(solution)/shard_map/mixer_low/pallas_call | solution.py:318
  67.5 9.9 %mixer_high.1 = (bf16[8,256,512]{2,1,0:T(8,128)(2,1)}, bf16[2,256,512]{2,1,0:T(8,128)(2,1)}, bf16[2,16,512]{2,1,0:T(8,128)(2,1)}, f32[512,512]{1,0:T(8,128)}, f32[512,512]{1,0:T(8,128)}, /*index=5*/f32[72,512]{1,0:T(8,128)}) custom-call(bf16[8,256,512]{2,1,0:T(8,128)(2,1)} %x.15, ...), custom_call_target="tpu_custom_call", output_to_operand_aliasing={{0}: (9, {}), {3}: (10, {}), {4}: (11, {}), {5}: (12, {})} | custom-call | flops 2516582400 | bytes 2621440 | tf_op jit(solution)/shard_map/mixer_high/pallas_call | solution.py:318
  77.4 3.5 %reshape.53 = f32[9,8,64,8]{3,2,1,0:T(8,128)} reshape(f32[72,512]{1,0:T(8,128)} %get-tuple-element.39) | data formatting | bytes 294912 | tf_op jit(solution)/shard_map/reshape | solution.py:419
  80.9 2.1 %reduce_sum.45 = f32[9,64,8]{2,1,0:T(8,128)S(1)} reduce(f32[9,8,64,8]{3,2,1,0:T(8,128)} %reshape.53, f32[]{:T(128)} %constant.51.clone.1), dimensions={1}, to_apply=%region_0.1 | reduce | flops 32256 | bytes 165892 | tf_op jit(solution)/shard_map/reduce_sum | solution.py:419
  83.3 1.1 select_convert_fusion
  84.5 1.0 copy.76
  85.5 1.1 collective-permute-done.12
  87.7 0.6 fusion.7
  88.3 1.1 collective-permute-start.6
  89.4 7.6 %collective-permute-done.13 = bf16[64,4,640]{2,1,0:T(4,128)(2,1)S(1)} collective-permute-done((bf16[64,4,640]{2,1,0:T(4,128)(2,1)S(1)}, bf16[64,4,640]{2,1,0:T(4,128)(2,1)S(1)}, u32[]{:S(2)}, u32[]{:S(2)}) %collective-permute-start.13) | collective-permute-done | bytes 327712 | tf_op jit(solution)/shard_map/ppermute | solution.py:410
  97.0 1.0 add_convert_fusion
  98.0 8.8 %all-to-all-start = ((bf16[64,4,640]{2,1,0:T(4,128)(2,1)}), bf16[64,4,640]{2,1,0:T(4,128)(2,1)}, u32[]{:S(2)}, u32[]{:S(2)}) async-start(bf16[64,4,640]{2,1,0:T(4,128)(2,1)} %add_convert_fusion), calls=%async_computation | async-start | bytes 655360 | tf_op jit(solution)/shard_map/all_to_all | solution.py:432
  106.8 1.0 convert_bitcast_fusion
  107.7 1.3 copy.69
  109.1 2.1 %reshape.51.band = bf16[4,288,192]{2,1,0:T(8,128)(2,1)} reshape(bf16[4,9,2,16,6,32]{5,4,3,2,1,0:T(8,128)(2,1)S(1)} %copy.69) | data formatting | bytes 884736 | tf_op jit(solution)/shard_map/bands/reshape | solution.py:64
  111.2 4.9 %collective-permute-start.10 = (bf16[2,256,512]{2,1,0:T(8,128)(2,1)S(1)}, bf16[2,256,512]{2,1,0:T(8,128)(2,1)S(1)}, u32[]{:S(2)}, u32[]{:S(2)}) collective-permute-start(bf16[2,256,512]{2,1,0:T(8,128)(2,1)S(1)} %copy-done.4), channel_id=1, source_target_pairs={{0,4},{4,8},{8,12},{12,16},{16,20},{20,24},{24,28},{28,32},{32,36}... | collective-permute-start | bytes 1572872 | tf_op jit(solution)/shard_map/grad_halo/ppermute | solution.py:401
  116.1 5.5 %collective-permute-start.8 = (bf16[2,256,512]{2,1,0:T(8,128)(2,1)S(1)}, bf16[2,256,512]{2,1,0:T(8,128)(2,1)S(1)}, u32[]{:S(2)}, u32[]{:S(2)}) collective-permute-start(bf16[2,256,512]{2,1,0:T(8,128)(2,1)S(1)} %copy-done.3), channel_id=1, source_target_pairs={{4,0},{8,4},{12,8},{16,12},{20,16},{24,20},{28,24},{32,28},{36,32}... | collective-permute-start | bytes 1572872 | tf_op jit(solution)/shard_map/ppermute | solution.py:405
  121.6 1.9 %collective-permute-start.11 = (bf16[2,16,512]{2,1,0:T(8,128)(2,1)S(1)}, bf16[2,16,512]{2,1,0:T(8,128)(2,1)S(1)}, u32[]{:S(2)}, u32[]{:S(2)}) collective-permute-start(bf16[2,16,512]{2,1,0:T(8,128)(2,1)S(1)} %get-tuple-element.70), channel_id=1, source_target_pairs={{0,4},{4,8},{8,12},{12,16},{16,20},{20,24},{24,28},{28,32},{32,36}... | collective-permute-start | bytes 98312 | tf_op jit(solution)/shard_map/grad_halo/ppermute | solution.py:401
  123.6 8.4 %collective-permute-start.9 = (bf16[2,16,512]{2,1,0:T(8,128)(2,1)S(1)}, bf16[2,16,512]{2,1,0:T(8,128)(2,1)S(1)}, u32[]{:S(2)}, u32[]{:S(2)}) collective-permute-start(bf16[2,16,512]{2,1,0:T(8,128)(2,1)S(1)} %get-tuple-element.71), channel_id=1, source_target_pairs={{4,0},{8,4},{12,8},{16,12},{20,16},{24,20},{28,24},{32,28},{36,32}... | collective-permute-start | bytes 98312 | tf_op jit(solution)/shard_map/grad_halo/ppermute | solution.py:405
  132.0 5.5 %adjoint_inner.1.keep = bf16[8,256,512]{2,1,0:T(8,128)(2,1)} custom-call(bf16[2,256,512]{2,1,0:T(8,128)(2,1)} %get-tuple-element.37.top.end, bf16[4,256,512]{2,1,0:T(8,128)(2,1)} %get-tuple-element.33.mid, bf16[2,256,512]{2,1,0:T(8,128)(2,1)} %get-tuple-element.32.bottom.end, bf16[8,16,512]{2,1,0:T(8,128)(2,1)} %copy-done.2, ...), custom_call_target="tpu_custom_call" | custom-call | flops 1811939328 | bytes 3145728 | tf_op jit(solution)/shard_map/adjoint_inner/pallas_call | solution.py:349
  137.5 1.1 convert_reduce_fusion
  138.6 1.1 collective-permute-start.14
  141.0 1.4 collective-permute-done.14
  142.4 0.6 broadcast_select_fusion.1
  143.6 0.7 broadcast_in_dim.35
  144.3 13.4 %all-to-all-start.1 = ((f32[256,1,128]{2,1,0:T(1,128)}), f32[256,1,128]{2,1,0:T(1,128)S(1)}, u32[]{:S(2)}, u32[]{:S(2)}) async-start(f32[256,1,128]{2,1,0:T(1,128)} %broadcast_in_dim.35), calls=%async_computation.1 | async-start | bytes 262144 | tf_op jit(solution)/shard_map/all_to_all | solution.py:438
  158.4 0.8 copy-done.7
  159.2 3.8 %adjoint_low.1.keep = bf16[8,256,512]{2,1,0:T(8,128)(2,1)} custom-call(bf16[2,256,512]{2,1,0:T(8,128)(2,1)} %get-tuple-element.37.top.end, bf16[4,256,512]{2,1,0:T(8,128)(2,1)} %get-tuple-element.33.mid, bf16[8,16,512]{2,1,0:T(8,128)(2,1)} %copy-done.2, bf16[2,256,512]{2,1,0:T(8,128)(2,1)} %copy-done.7, ...), custom_call_target="tpu_custom_call", output_to_operand_aliasing={{}: (8, {})} | custom-call | flops 905969664 | bytes 1572864 | tf_op jit(solution)/shard_map/adjoint_low/pallas_call | solution.py:370
  163.0 0.6 copy-done.12
  163.6 0.8 copy-done.6
  164.4 3.8 %adjoint_high.1 = bf16[8,256,512]{2,1,0:T(8,128)(2,1)} custom-call(bf16[2,256,512]{2,1,0:T(8,128)(2,1)} %get-tuple-element.32.bottom.end, bf16[4,256,512]{2,1,0:T(8,128)(2,1)} %get-tuple-element.33.mid, bf16[8,16,512]{2,1,0:T(8,128)(2,1)} %copy-done.2, bf16[2,256,512]{2,1,0:T(8,128)(2,1)} %copy-done.6, ...), custom_call_target="tpu_custom_call", output_to_operand_aliasing={{}: (8, {})} | custom-call | flops 905969664 | bytes 1572864 | tf_op jit(solution)/shard_map/adjoint_high/pallas_call | solution.py:370
  168.4 1.3 all-to-all-done.1
  169.7 0.9 slice_reduce_fusion
  171.3 0.7 copy.73
  172.0 0.6 multiply_bitcast_fusion
  (98 shorter events, 6.7 us)
Async XLA Ops:
  0.6 16.9 %copy-start.8 = (s32[512,5,9]{0,1,2:T(8,128)S(1)}, s32[512,5,9]{0,1,2:T(8,128)}, u32[]{:S(2)}) copy-start(s32[512,5,9]{0,1,2:T(8,128)} %param.14) | copy-start | bytes 276484
  0.6 17.5 %copy-start.9 = (f32[512,5,9]{0,1,2:T(8,128)S(1)}, f32[512,5,9]{0,1,2:T(8,128)}, u32[]{:S(2)}) copy-start(f32[512,5,9]{0,1,2:T(8,128)} %param.13) | copy-start | bytes 276484
  2.2 27.9 %collective-permute-start = (bf16[8,8,512]{2,1,0:T(8,128)(2,1)}, bf16[8,8,512]{2,1,0:T(8,128)(2,1)S(1)}, u32[]{:S(2)}, u32[]{:S(2)}) collective-permute-start(bf16[8,8,512]{2,1,0:T(8,128)(2,1)} %get-tuple-element.69), channel_id=1, source_target_pairs={{0,3},{1,0},{2,1},{3,2},{4,7},{5,4},{6,5},{7,6},{8,11},{9,8},{10,9... | collective-permute-start | bytes 196616 | tf_op jit(solution)/shard_map/input_halo/ppermute | solution.py:395
  3.2 15.5 %copy-start.20 = (s32[512,5]{0,1:T(8,128)S(1)}, s32[512,5]{0,1:T(8,128)}, u32[]{:S(2)}) copy-start(s32[512,5]{0,1:T(8,128)} %param.15) | copy-start | bytes 30724
  3.2 16.3 %copy-start.19 = (bf16[96,60]{1,0:T(8,128)(2,1)S(1)}, bf16[96,60]{1,0:T(8,128)(2,1)}, u32[]{:S(2)}) copy-start(bf16[96,60]{1,0:T(8,128)(2,1)} %constant.60.clone) | copy-start | bytes 34564
  3.2 26.9 %collective-permute-start.1 = (bf16[8,8,512]{2,1,0:T(8,128)(2,1)}, bf16[8,8,512]{2,1,0:T(8,128)(2,1)S(1)}, u32[]{:S(2)}, u32[]{:S(2)}) collective-permute-start(bf16[8,8,512]{2,1,0:T(8,128)(2,1)} %get-tuple-element.68), channel_id=1, source_target_pairs={{0,1},{1,2},{2,3},{3,0},{4,5},{5,6},{6,7},{7,4},{8,9},{9,10},{10,1... | collective-permute-start | bytes 196616 | tf_op jit(solution)/shard_map/input_halo/ppermute | solution.py:396
  5.5 50.8 %collective-permute-start.4 = (bf16[2,256,512]{2,1,0:T(8,128)(2,1)}, bf16[2,256,512]{2,1,0:T(8,128)(2,1)}, u32[]{:S(2)}, u32[]{:S(2)}) collective-permute-start(bf16[2,256,512]{2,1,0:T(8,128)(2,1)} %get-tuple-element.66), channel_id=1, source_target_pairs={{0,4},{4,8},{8,12},{12,16},{16,20},{20,24},{24,28},{28,32},{32,36}... | collective-permute-start | bytes 1572872 | tf_op jit(solution)/shard_map/input_halo/ppermute | solution.py:401
  10.3 56.5 %collective-permute-start.2 = (bf16[2,256,512]{2,1,0:T(8,128)(2,1)}, bf16[2,256,512]{2,1,0:T(8,128)(2,1)}, u32[]{:S(2)}, u32[]{:S(2)}) collective-permute-start(bf16[2,256,512]{2,1,0:T(8,128)(2,1)} %get-tuple-element.67), channel_id=1, source_target_pairs={{4,0},{8,4},{12,8},{16,12},{20,16},{24,20},{28,24},{32,28},{36,32}... | collective-permute-start | bytes 1572872 | tf_op jit(solution)/shard_map/input_halo/ppermute | solution.py:405
  25.5 4.0 %copy-start.16 = (f32[512,9]{0,1:T(8,128)S(1)}, f32[512,9]{0,1:T(8,128)}, u32[]{:S(2)}) copy-start(f32[512,9]{0,1:T(8,128)} %param.16) | copy-start | bytes 55300
  30.2 10.6 %copy-start.5 = (bf16[8,16,512]{2,1,0:T(8,128)(2,1)}, bf16[8,16,512]{2,1,0:T(8,128)(2,1)S(1)}, u32[]{:S(2)}) copy-start(bf16[8,16,512]{2,1,0:T(8,128)(2,1)S(1)} %constant_dynamic-update-slice_fusion.side) | copy-start | bytes 393220
  30.2 26.1 %collective-permute-start.5 = (bf16[2,16,512]{2,1,0:T(8,128)(2,1)S(1)}, bf16[2,16,512]{2,1,0:T(8,128)(2,1)S(1)}, u32[]{:S(2)}, u32[]{:S(2)}) collective-permute-start(bf16[2,16,512]{2,1,0:T(8,128)(2,1)S(1)} %get-tuple-element.74), channel_id=1, source_target_pairs={{0,4},{4,8},{8,12},{12,16},{16,20},{20,24},{24,28},{28,32},{32,36}... | collective-permute-start | bytes 98312 | tf_op jit(solution)/shard_map/input_halo/ppermute | solution.py:401
  32.1 34.8 %collective-permute-start.3 = (bf16[2,16,512]{2,1,0:T(8,128)(2,1)S(1)}, bf16[2,16,512]{2,1,0:T(8,128)(2,1)S(1)}, u32[]{:S(2)}, u32[]{:S(2)}) collective-permute-start(bf16[2,16,512]{2,1,0:T(8,128)(2,1)S(1)} %get-tuple-element.75), channel_id=1, source_target_pairs={{4,0},{8,4},{12,8},{16,12},{20,16},{24,20},{28,24},{32,28},{36,32}... | collective-permute-start | bytes 98312 | tf_op jit(solution)/shard_map/input_halo/ppermute | solution.py:405
  56.3 0.6 copy-start.15
  66.9 0.6 copy-start.14
  80.9 2.4 %copy-start = (f32[512,512]{1,0:T(8,128)S(1)}, f32[512,512]{1,0:T(8,128)}, u32[]{:S(2)}) copy-start(f32[512,512]{1,0:T(8,128)} %get-tuple-element.40) | copy-start | bytes 3145732
  80.9 2.4 %copy-start.1 = (f32[512,512]{1,0:T(8,128)S(1)}, f32[512,512]{1,0:T(8,128)}, u32[]{:S(2)}) copy-start(f32[512,512]{1,0:T(8,128)} %get-tuple-element.38) | copy-start | bytes 3145732
  83.1 2.4 %copy-start.17 = (bf16[2,16,512]{2,1,0:T(8,128)(2,1)S(1)}, bf16[2,16,512]{2,1,0:T(8,128)(2,1)}, u32[]{:S(2)}) copy-start(bf16[2,16,512]{2,1,0:T(8,128)(2,1)} %get-tuple-element.34) | copy-start | bytes 98308
  83.1 2.4 %copy-start.10 = (bf16[4,16,512]{2,1,0:T(8,128)(2,1)S(1)}, bf16[4,16,512]{2,1,0:T(8,128)(2,1)}, u32[]{:S(2)}) copy-start(bf16[4,16,512]{2,1,0:T(8,128)(2,1)} %get-tuple-element.35) | copy-start | bytes 196612
  84.3 2.3 %collective-permute-start.12 = (bf16[64,8,640]{2,1,0:T(8,128)(2,1)}, bf16[64,8,640]{2,1,0:T(8,128)(2,1)S(1)}, u32[]{:S(2)}, u32[]{:S(2)}) collective-permute-start(bf16[64,8,640]{2,1,0:T(8,128)(2,1)} %select_convert_fusion), channel_id=1, source_target_pairs={{0,1},{1,0},{2,3},{3,2},{4,5},{5,4},{6,7},{7,6},{8,9},{9,8},{10,11... | collective-permute-start | bytes 1966088 | tf_op jit(solution)/shard_map/ppermute | solution.py:410
  85.5 2.2 %copy-start.18 = (bf16[2,16,512]{2,1,0:T(8,128)(2,1)S(1)}, bf16[2,16,512]{2,1,0:T(8,128)(2,1)}, u32[]{:S(2)}) copy-start(bf16[2,16,512]{2,1,0:T(8,128)(2,1)} %get-tuple-element.36) | copy-start | bytes 98308
  86.9 19.8 %copy-start.11 = (bf16[9,16,32,1,1,1]{2,0,1,5,4,3:T(8,128)(2,1)S(1)}, bf16[9,16,32,1,1,1]{2,0,1,5,4,3:T(8,128)(2,1)}, u32[]{:S(2)}) copy-start(bf16[9,16,32,1,1,1]{2,0,1,5,4,3:T(8,128)(2,1)} %constant.76) | copy-start | bytes 27652
  87.2 9.8 %collective-permute-start.13 = (bf16[64,4,640]{2,1,0:T(4,128)(2,1)S(1)}, bf16[64,4,640]{2,1,0:T(4,128)(2,1)S(1)}, u32[]{:S(2)}, u32[]{:S(2)}) collective-permute-start(bf16[64,4,640]{2,1,0:T(4,128)(2,1)S(1)} %select_convert_fusion.1), channel_id=1, source_target_pairs={{0,2},{1,3},{2,0},{3,1},{4,6},{5,7},{6,4},{7,5},{8,10},{9,11},{10,... | collective-permute-start | bytes 983048 | tf_op jit(solution)/shard_map/ppermute | solution.py:410
  88.3 33.2 %collective-permute-start.6 = (bf16[8,8,512]{2,1,0:T(8,128)(2,1)}, bf16[8,8,512]{2,1,0:T(8,128)(2,1)S(1)}, u32[]{:S(2)}, u32[]{:S(2)}) collective-permute-start(bf16[8,8,512]{2,1,0:T(8,128)(2,1)} %get-tuple-element.73), channel_id=1, source_target_pairs={{0,3},{1,0},{2,1},{3,2},{4,7},{5,4},{6,5},{7,6},{8,11},{9,8},{10,9... | collective-permute-start | bytes 196616 | tf_op jit(solution)/shard_map/grad_halo/ppermute | solution.py:395
  98.0 39.5 %all-to-all-start = ((bf16[64,4,640]{2,1,0:T(4,128)(2,1)}), bf16[64,4,640]{2,1,0:T(4,128)(2,1)}, u32[]{:S(2)}, u32[]{:S(2)}) async-start(bf16[64,4,640]{2,1,0:T(4,128)(2,1)} %add_convert_fusion), calls=%async_computation | async-start | bytes 655360 | tf_op jit(solution)/shard_map/all_to_all | solution.py:432
  109.1 2.1 %copy-start.4 = (bf16[2,256,512]{2,1,0:T(8,128)(2,1)S(1)}, bf16[2,256,512]{2,1,0:T(8,128)(2,1)}, u32[]{:S(2)}) copy-start(bf16[2,256,512]{2,1,0:T(8,128)(2,1)} %get-tuple-element.32.bottom.end) | copy-start | bytes 1572868
  109.1 7.0 %copy-start.3 = (bf16[2,256,512]{2,1,0:T(8,128)(2,1)S(1)}, bf16[2,256,512]{2,1,0:T(8,128)(2,1)}, u32[]{:S(2)}) copy-start(bf16[2,256,512]{2,1,0:T(8,128)(2,1)} %get-tuple-element.37.top.end) | copy-start | bytes 1572868
  111.2 10.4 %collective-permute-start.7 = (bf16[8,8,512]{2,1,0:T(8,128)(2,1)S(1)}, bf16[8,8,512]{2,1,0:T(8,128)(2,1)S(1)}, u32[]{:S(2)}, u32[]{:S(2)}) collective-permute-start(bf16[8,8,512]{2,1,0:T(8,128)(2,1)S(1)} %get-tuple-element.72), channel_id=1, source_target_pairs={{0,1},{1,2},{2,3},{3,0},{4,5},{5,6},{6,7},{7,4},{8,9},{9,10},{10,1... | collective-permute-start | bytes 196616 | tf_op jit(solution)/shard_map/grad_halo/ppermute | solution.py:396
  111.2 46.6 %collective-permute-start.10 = (bf16[2,256,512]{2,1,0:T(8,128)(2,1)S(1)}, bf16[2,256,512]{2,1,0:T(8,128)(2,1)S(1)}, u32[]{:S(2)}, u32[]{:S(2)}) collective-permute-start(bf16[2,256,512]{2,1,0:T(8,128)(2,1)S(1)} %copy-done.4), channel_id=1, source_target_pairs={{0,4},{4,8},{8,12},{12,16},{16,20},{20,24},{24,28},{28,32},{32,36}... | collective-permute-start | bytes 1572872 | tf_op jit(solution)/shard_map/grad_halo/ppermute | solution.py:401
  116.1 46.9 %collective-permute-start.8 = (bf16[2,256,512]{2,1,0:T(8,128)(2,1)S(1)}, bf16[2,256,512]{2,1,0:T(8,128)(2,1)S(1)}, u32[]{:S(2)}, u32[]{:S(2)}) collective-permute-start(bf16[2,256,512]{2,1,0:T(8,128)(2,1)S(1)} %copy-done.3), channel_id=1, source_target_pairs={{4,0},{8,4},{12,8},{16,12},{20,16},{24,20},{28,24},{32,28},{36,32}... | collective-permute-start | bytes 1572872 | tf_op jit(solution)/shard_map/ppermute | solution.py:405
  121.6 10.4 %copy-start.2 = (bf16[8,16,512]{2,1,0:T(8,128)(2,1)}, bf16[8,16,512]{2,1,0:T(8,128)(2,1)S(1)}, u32[]{:S(2)}) copy-start(bf16[8,16,512]{2,1,0:T(8,128)(2,1)S(1)} %constant_dynamic-update-slice_fusion.5.side) | copy-start | bytes 393220
  121.6 36.1 %collective-permute-start.11 = (bf16[2,16,512]{2,1,0:T(8,128)(2,1)S(1)}, bf16[2,16,512]{2,1,0:T(8,128)(2,1)S(1)}, u32[]{:S(2)}, u32[]{:S(2)}) collective-permute-start(bf16[2,16,512]{2,1,0:T(8,128)(2,1)S(1)} %get-tuple-element.70), channel_id=1, source_target_pairs={{0,4},{4,8},{8,12},{12,16},{16,20},{20,24},{24,28},{28,32},{32,36}... | collective-permute-start | bytes 98312 | tf_op jit(solution)/shard_map/grad_halo/ppermute | solution.py:401
  123.6 39.4 %collective-permute-start.9 = (bf16[2,16,512]{2,1,0:T(8,128)(2,1)S(1)}, bf16[2,16,512]{2,1,0:T(8,128)(2,1)S(1)}, u32[]{:S(2)}, u32[]{:S(2)}) collective-permute-start(bf16[2,16,512]{2,1,0:T(8,128)(2,1)S(1)} %get-tuple-element.71), channel_id=1, source_target_pairs={{4,0},{8,4},{12,8},{16,12},{20,16},{24,20},{28,24},{32,28},{36,32}... | collective-permute-start | bytes 98312 | tf_op jit(solution)/shard_map/grad_halo/ppermute | solution.py:405
  138.6 3.7 %collective-permute-start.14 = (f32[4,512]{1,0:T(4,128)S(1)}, f32[4,512]{1,0:T(4,128)S(1)}, u32[]{:S(2)}, u32[]{:S(2)}) collective-permute-start(f32[4,512]{1,0:T(4,128)S(1)} %slice.82), channel_id=1, source_target_pairs={{0,2},{1,3},{2,0},{3,1},{4,6},{5,7},{6,4},{7,5},{8,10},{9,11},{10,... | collective-permute-start | bytes 24584 | tf_op jit(solution)/shard_map/ppermute | solution.py:410
  144.3 25.3 %all-to-all-start.1 = ((f32[256,1,128]{2,1,0:T(1,128)}), f32[256,1,128]{2,1,0:T(1,128)S(1)}, u32[]{:S(2)}, u32[]{:S(2)}) async-start(f32[256,1,128]{2,1,0:T(1,128)} %broadcast_in_dim.35), calls=%async_computation.1 | async-start | bytes 262144 | tf_op jit(solution)/shard_map/all_to_all | solution.py:438
  157.7 0.6 copy-start.13
  158.4 0.8 copy-start.7
  163.0 0.6 copy-start.12
  163.6 0.8 copy-start.6
  168.2 3.8 %collective-permute-start.15 = (f32[8,512]{1,0:T(8,128)S(1)}, f32[8,512]{1,0:T(8,128)S(1)}, u32[]{:S(2)}, u32[]{:S(2)}) collective-permute-start(f32[8,512]{1,0:T(8,128)S(1)} %pad_maximum_fusion.2), channel_id=1, source_target_pairs={{0,1},{1,0},{2,3},{3,2},{4,5},{5,4},{6,7},{7,6},{8,9},{9,8},{10,11... | collective-permute-start | bytes 49160 | tf_op jit(solution)/shard_map/ppermute | solution.py:410

commit v2 on v1

v2 whole, which is shorter than its diff:
```python
import functools
import math

import jax
import jax.numpy as jnp
import numpy as np
from jax import lax
from jax.experimental import pallas as pl
from jax.experimental.pallas import tpu as pltpu
from jax.sharding import PartitionSpec as P

BASIS = 9
REACH_LAT = 2
REACH_LON = 4
ROW_TAPS = 2 * REACH_LAT + 1
COL_TAPS = 2 * REACH_LON + 1
PAIR = 2
WIN = PAIR + 2 * REACH_LAT
TILE = 16
HALF = TILE // 2
SPAN = 2 * TILE
LANES_K = 256
CLIP = 512.0
EPS = 1e-06
BF = jnp.bfloat16
F32 = jnp.float32
VMEM_LIMIT = 56 * 1024 * 1024
MIDDLE_LIMIT = 42 * 1024 * 1024
SMALL_LIMIT = 24 * 1024 * 1024


def band_picks(pairs):
    ext = PAIR * pairs + 2 * REACH_LAT
    pick = np.zeros((ext, ROW_TAPS, 2, pairs, PAIR, LANES_K // SPAN, SPAN))
    for p in range(pairs):
        for r in range(PAIR):
            for a in range(WIN):
                if 0 <= a - r < ROW_TAPS:
                    pick[PAIR * p + r + REACH_LAT, a - r, 0, p, r, a] = 1
                    pick[PAIR * p + a, r - a + 2 * REACH_LAT, 1, p, r, a] = 1
    return pick.reshape(ext * ROW_TAPS, 2, -1)


def band_kernel(pairs, which, values, index, reach, pick, out):
    lane = lax.broadcasted_iota(jnp.int32, (TILE, LANES_K), 1)
    j = lax.broadcasted_iota(jnp.int32, (TILE, LANES_K), 0)
    w = lane % SPAN
    ahead = jnp.where(w < HALF, w + TILE, w - TILE) - j
    tap = lax.broadcasted_iota(jnp.int32, values.shape, 0) - REACH_LON
    kept = jnp.where(jnp.abs(tap) <= reach[...], values[...], 0.0)
    for k in range(BASIS):
        taps = jnp.where(index[...] == k, kept, 0.0).astype(BF)
        spread = jnp.dot(taps, pick[...], preferred_element_type=F32)
        for p in range(pairs):
            for r in range(PAIR):
                first = (p * PAIR + r) * LANES_K
                block = jnp.zeros((TILE, LANES_K), F32)
                for b in range(COL_TAPS):
                    at = b - REACH_LON if which == 0 else REACH_LON - b
                    row = spread[b : b + 1, first : first + LANES_K]
                    block = jnp.where(ahead == at, row, block)
                at = (k * PAIR + r) * TILE
                out[p, at : at + TILE, :] = block[:, : WIN * SPAN].astype(BF)


def band_matrix(which, values, index, reach, pairs):
    return pl.pallas_call(
        functools.partial(band_kernel, pairs, which),
        out_shape=jax.ShapeDtypeStruct((pairs, BASIS * PAIR * TILE, WIN * SPAN), BF),
        compiler_params=params(SMALL_LIMIT),
        name="band_adjoint" if which else "band_forward",
    )(values, index, reach, jnp.asarray(band_picks(pairs)[:, which].reshape(values.shape[1], -1), BF))


def dot(a, b, ca, cb):
    return lax.dot_general(a, b, (((ca,), (cb,)), ((), ())), preferred_element_type=F32)


def window(rows, sides, m, tiles):
    parts = []
    for row, side in zip(rows, sides):
        if m + 1 < tiles:
            right = row[(m + 1) * TILE : (m + 2) * TILE, :].astype(F32)[:HALF]
        else:
            right = side[...].astype(F32)[:HALF]
        if m > 0:
            left = row[(m - 1) * TILE : m * TILE, :].astype(F32)[HALF:]
        else:
            left = side[...].astype(F32)[HALF:]
        parts.append(jnp.concatenate([right, left], axis=0).astype(BF))
        parts.append(row[m * TILE : (m + 1) * TILE, :])
    return jnp.concatenate(parts, axis=0)


def mixer_body(
    rows, sides, band, filt, w_in, w_out, cot, out, gf, edge, gin, gout, gfilt,
    y, low, hid, gact, act, gh,
):
    cols, chans = cot.shape[1:]
    tiles = cols // TILE
    cells = PAIR * cols
    for m in range(tiles):
        full = jnp.dot(band[0], window(rows, sides, m, tiles), preferred_element_type=F32)
        for r in range(PAIR):
            at = pl.ds(r * cols + m * TILE, TILE)
            total = None
            for k in range(BASIS):
                first = (k * PAIR + r) * TILE
                piece = full[first : first + TILE]
                y[k, at, :] = piece
                term = filt[k : k + 1, :] * piece
                total = term if total is None else total + term
            low[at, :] = total.astype(BF)
    cot_flat = cot[...].reshape(cells, chans)
    hid[...] = dot(low[...], w_in[...], 1, 0)
    gact[...] = dot(cot_flat, w_out[...], 1, 1)
    root = math.sqrt(2.0 / math.pi)
    for n in range(cells // TILE):
        at = pl.ds(n * TILE, TILE)
        v = hid[at, :]
        sq = v * v
        t = jnp.tanh(v * (root + (root * 0.044715) * sq))
        half = 0.5 + 0.5 * t
        act[at, :] = (v * half).astype(BF)
        slope = half + (0.5 * v) * (1.0 - t * t) * (root + (3 * root * 0.044715) * sq)
        gh[at, :] = (gact[at, :] * slope).astype(BF)
    back = dot(gh[...], w_in[...], 1, 1)
    mixed = dot(act[...], w_out[...], 1, 0)
    for r in range(PAIR):
        part = slice(r * cols, (r + 1) * cols)
        gf[r] = back[part].astype(BF)
        edge[r] = jnp.concatenate(
            [back[r * cols : r * cols + HALF], back[(r + 1) * cols - HALF : (r + 1) * cols]], axis=0
        ).astype(BF)
        out[r] = (rows[REACH_LAT + r][:cols, :].astype(F32) + mixed[part]).astype(BF)
    gout[...] += dot(cot_flat, act[...], 0, 0)
    gin[...] += dot(low[...], gh[...], 0, 0)
    lanes = 128
    for c in range(chans // lanes):
        at_c = pl.ds(c * lanes, lanes)
        sums = [gfilt[8 * k : 8 * k + 8, at_c] for k in range(BASIS)]
        for n in range(tiles):
            for r in range(PAIR):
                g = gf[r, pl.ds(n * TILE, TILE), at_c].astype(F32)
                for k in range(BASIS):
                    prod = g * y[k, pl.ds(r * cols + n * TILE, TILE), at_c]
                    sums[k] = sums[k] + (prod[:8] + prod[8:])
        for k in range(BASIS):
            gfilt[8 * k : 8 * k + 8, at_c] = sums[k]


def inner_kernel(x, side, band, filt, w_in, w_out, cot, out, gf, edge, gin, gout, gfilt, *scratch):
    i = pl.program_id(0)

    @pl.when(i == 0)
    def _():
        gin[...] = jnp.zeros_like(gin)
        gout[...] = jnp.zeros_like(gout)
        gfilt[...] = jnp.zeros_like(gfilt)

    rows = [x.at[PAIR * i + a] for a in range(WIN)]
    sides = [side.at[PAIR * i + a] for a in range(WIN)]
    mixer_body(rows, sides, band, filt, w_in, w_out, cot, out, gf, edge, gin, gout, gfilt, *scratch)


def place(win, at, part, side=None):
    n, cols = part.shape[:2]
    win[at : at + n, :cols, :] = part[...]
    if side is not None:
        win[at : at + n, cols:, :] = side[...]


def views(win):
    cols = win.shape[1] - TILE
    rows = [win.at[a] for a in range(WIN)]
    return rows, [win.at[a, pl.ds(cols, TILE)] for a in range(WIN)]


def beside_rows(gfilt, chans, per):
    bands, lanes = chans // per, 128
    mine = lax.broadcasted_iota(jnp.int32, (bands, chans), 1) // per == lax.broadcasted_iota(
        jnp.int32, (bands, chans), 0
    )
    lane = lax.broadcasted_iota(jnp.int32, (chans, lanes), 1)
    chan = lax.broadcasted_iota(jnp.int32, (chans, lanes), 0)
    packed = jnp.zeros((bands, lanes), F32)
    for k in range(BASIS):
        sums = jnp.sum(gfilt[8 * k : 8 * k + 8, :], axis=0, keepdims=True)
        spread = jnp.where(mine, sums, 0.0).astype(BF)
        fold = jnp.where((lane // per == k) & (lane % per == chan % per), 1.0, 0.0).astype(BF)
        packed = packed + jnp.dot(spread, fold, preferred_element_type=F32)
    row = lax.broadcasted_iota(jnp.int32, (chans, bands), 0) // per
    repeat = jnp.where(row == lax.broadcasted_iota(jnp.int32, (chans, bands), 1), 1.0, 0.0)
    return jnp.dot(repeat.astype(BF), packed.astype(BF), preferred_element_type=F32)


def outer_kernel(
    per, odd, x, side, lo, hi, band, filt, w_in, w_out, cot, partial_out, gin0, gout0, gfilt0,
    out, gf, edge, keep, give, win, gin, gout, gfilt, *scratch,
):
    i = pl.program_id(0)
    chans = gin.shape[0]

    @pl.when(i == 0)
    def _():
        gin[...] = gin0[...]
        gout[...] = gout0[...]
        gfilt[...] = gfilt0[...]
        place(win, 0, lo)
        place(win, REACH_LAT, x, side)

    @pl.when(i == 1)
    def _():
        place(win, 0, x, side)
        place(win, WIN - REACH_LAT, hi)

    rows, sides = views(win)
    mixer_body(rows, sides, band, filt, w_in, w_out, cot, out, gf, edge, gin, gout, gfilt, *scratch)

    @pl.when(i == 1)
    def _():
        beside = beside_rows(gfilt, chans, per)
        keep[:, chans:] = beside
        give[:, chans:] = beside.astype(BF)

    @pl.when((i == 1) & (odd[0] == 0))
    def _():
        keep[:, :chans] = gin[...]
        give[:, :chans] = gout[...].astype(BF)

    @pl.when((i == 1) & (odd[0] == 1))
    def _():
        keep[:, :chans] = gout[...]
        give[:, :chans] = gin[...].astype(BF)


def adjoint_body(rows, sides, band, filt, cot, out):
    cols = cot.shape[1]
    tiles = cols // TILE
    for m in range(tiles):
        full = jnp.dot(band[0], window(rows, sides, m, tiles), preferred_element_type=F32)
        at = slice(m * TILE, (m + 1) * TILE)
        for r in range(PAIR):
            total = cot[r, at, :].astype(F32)
            for k in range(BASIS):
                first = (k * PAIR + r) * TILE
                total = total + filt[k : k + 1, :] * full[first : first + TILE]
            out[r, at, :] = total.astype(BF)


def inner_adjoint(mid, mid_side, end, end_side, band, filt, cot, out, win):
    i = pl.program_id(0)

    @pl.when(i == 0)
    def _():
        place(win, 0, end, end_side)
        place(win, REACH_LAT, mid, mid_side)

    @pl.when(i == 1)
    def _():
        place(win, 0, mid, mid_side)
        place(win, WIN - REACH_LAT, end, end_side)

    adjoint_body(*views(win), band, filt, cot, out)


def outer_adjoint(mid, mid_side, end, end_side, lo, hi, band, filt, cot, partial_out, out, win):
    i = pl.program_id(0)
    place(win, REACH_LAT, end, end_side)

    @pl.when(i == 0)
    def _():
        place(win, 0, lo)
        place(win, WIN - REACH_LAT, mid, mid_side)

    @pl.when(i == 1)
    def _():
        place(win, 0, mid, mid_side)
        place(win, WIN - REACH_LAT, hi)

    adjoint_body(*views(win), band, filt, cot, out)


def blocks(n, shape, step=None):
    step = step or (lambda i: i)
    return pl.BlockSpec((n,) + shape[1:], lambda i: (step(i),) + (0,) * (len(shape) - 1))


def whole(shape):
    return pl.BlockSpec(shape, lambda i: (0,) * len(shape))


def params(limit=VMEM_LIMIT):
    return pltpu.CompilerParams(vmem_limit_bytes=limit)


def mixer_scratch(cols, chans):
    cells = PAIR * cols
    return [
        pltpu.VMEM((BASIS, cells, chans), F32),
        pltpu.VMEM((cells, chans), BF),
        pltpu.VMEM((cells, chans), F32),
        pltpu.VMEM((cells, chans), F32),
        pltpu.VMEM((cells, chans), BF),
        pltpu.VMEM((cells, chans), BF),
    ]


def mixer_cost(cols, chans):
    cells = 2 * PAIR * cols
    flops = 2 * cells * chans * (6 * chans + BASIS * WIN * SPAN)
    return pl.CostEstimate(
        flops=flops, bytes_accessed=10 * cells * chans, transcendentals=cells * chans
    )


def inner_pair(i):
    return 1 + i


def outer_pair(i):
    return 3 * i


def mixer_inner(x, side, band, filt, w_in, w_out, cot):
    rows, cols, chans = x.shape
    gf = jax.ShapeDtypeStruct((2 * PAIR, cols, chans), BF)
    edge = jax.ShapeDtypeStruct((2 * PAIR, TILE, chans), BF)
    matrix = jax.ShapeDtypeStruct((chans, chans), F32)
    small = jax.ShapeDtypeStruct((8 * BASIS, chans), F32)
    return pl.pallas_call(
        inner_kernel,
        grid=(2,),
        in_specs=[
            whole(x.shape), whole(side.shape), blocks(1, band.shape, inner_pair),
            whole(filt.shape), whole(w_in.shape), whole(w_out.shape),
            blocks(PAIR, cot.shape, inner_pair),
        ],
        out_specs=[
            blocks(PAIR, x.shape, inner_pair), blocks(PAIR, gf.shape), blocks(PAIR, edge.shape),
            whole(matrix.shape), whole(matrix.shape), whole(small.shape),
        ],
        out_shape=(jax.ShapeDtypeStruct(x.shape, BF), gf, edge, matrix, matrix, small),
        scratch_shapes=mixer_scratch(cols, chans),
        compiler_params=params(),
        cost_estimate=mixer_cost(cols, chans),
        name="mixer_inner",
    )(x, side, band, filt, w_in, w_out, cot)


def mixer_outer(
    odd, per, x, side, lo, hi, band, filt, w_in, w_out, cot, partial_out, sums
):
    rows, cols, chans = x.shape
    near = WIN - REACH_LAT
    gf = jax.ShapeDtypeStruct((2 * PAIR, cols, chans), BF)
    edge = jax.ShapeDtypeStruct((2 * PAIR, TILE, chans), BF)
    keep = jax.ShapeDtypeStruct((chans, chans + 128), F32)
    give = jax.ShapeDtypeStruct((chans, chans + 128), BF)
    return pl.pallas_call(
        functools.partial(outer_kernel, per),
        grid=(2,),
        in_specs=[
            pl.BlockSpec(memory_space=pltpu.SMEM),
            blocks(near, x.shape), blocks(near, side.shape),
            whole(lo.shape), whole(hi.shape),
            blocks(1, band.shape, outer_pair),
            whole(filt.shape), whole(w_in.shape), whole(w_out.shape),
            blocks(PAIR, cot.shape, outer_pair),
            pl.BlockSpec(memory_space=pl.ANY),
        ] + [whole(s.shape) for s in sums],
        out_specs=[
            blocks(PAIR, x.shape, outer_pair), blocks(PAIR, gf.shape), blocks(PAIR, edge.shape),
            whole(keep.shape), whole(give.shape),
        ],
        out_shape=(jax.ShapeDtypeStruct(x.shape, BF), gf, edge, keep, give),
        scratch_shapes=[
            pltpu.VMEM((WIN, cols + TILE, chans), BF),
            pltpu.VMEM((chans, chans), F32),
            pltpu.VMEM((chans, chans), F32),
            pltpu.VMEM((8 * BASIS, chans), F32),
        ] + mixer_scratch(cols, chans),
        input_output_aliases={10: 0},
        compiler_params=params(MIDDLE_LIMIT),
        cost_estimate=mixer_cost(cols, chans),
        name="mixer_outer",
    )(odd, x, side, lo, hi, band, filt, w_in, w_out, cot, partial_out, *sums)


def adjoint_cost(cols, chans):
    cells = 2 * PAIR * cols
    return pl.CostEstimate(
        flops=2 * cells * chans * BASIS * WIN * SPAN, bytes_accessed=6 * cells * chans,
        transcendentals=0,
    )


def adjoint_inner(mid, mid_side, end, end_side, band, filt, cot):
    rows, cols, chans = cot.shape
    return pl.pallas_call(
        inner_adjoint,
        grid=(2,),
        in_specs=[
            whole(mid.shape), whole(mid_side.shape),
            blocks(PAIR, end.shape), blocks(PAIR, end_side.shape),
            blocks(1, band.shape, inner_pair), whole(filt.shape),
            blocks(PAIR, cot.shape, inner_pair),
        ],
        out_specs=blocks(PAIR, cot.shape, inner_pair),
        out_shape=jax.ShapeDtypeStruct(cot.shape, BF),
        scratch_shapes=[pltpu.VMEM((WIN, cols + TILE, chans), BF)],
        compiler_params=params(SMALL_LIMIT),
        cost_estimate=adjoint_cost(cols, chans),
        name="adjoint_inner",
    )(mid, mid_side, end, end_side, band, filt, cot)


def adjoint_outer(mid, mid_side, end, end_side, lo, hi, band, filt, cot, partial_out):
    rows, cols, chans = cot.shape
    return pl.pallas_call(
        outer_adjoint,
        grid=(2,),
        in_specs=[
            blocks(PAIR, mid.shape), blocks(PAIR, mid_side.shape),
            blocks(PAIR, end.shape), blocks(PAIR, end_side.shape),
            whole(lo.shape), whole(hi.shape),
            blocks(1, band.shape, outer_pair), whole(filt.shape),
            blocks(PAIR, cot.shape, outer_pair),
            pl.BlockSpec(memory_space=pl.ANY),
        ],
        out_specs=blocks(PAIR, cot.shape, outer_pair),
        out_shape=jax.ShapeDtypeStruct(cot.shape, BF),
        scratch_shapes=[pltpu.VMEM((WIN, cols + TILE, chans), BF)],
        input_output_aliases={9: 0},
        compiler_params=params(),
        cost_estimate=adjoint_cost(cols, chans),
        name="adjoint_outer",
    )(mid, mid_side, end, end_side, lo, hi, band, filt, cot, partial_out)


def exchange_columns(first, last, count):
    up = [(i, (i + 1) % count) for i in range(count)]
    down = [(i, (i - 1) % count) for i in range(count)]
    right = lax.ppermute(first, "lon", down)
    left = lax.ppermute(last, "lon", up)
    return jnp.concatenate([right, left], axis=1)


def beside(rows, side):
    return jnp.concatenate([rows, side], axis=1)


def exchange_rows(first, last, count):
    up = [(i, i + 1) for i in range(count - 1)]
    down = [(i + 1, i) for i in range(count - 1)]
    return lax.ppermute(last, "lat", up), lax.ppermute(first, "lat", down)


def swap(a, count, bits):
    return lax.ppermute(a, "lon", [(i, i ^ bits) for i in range(count)])


def sum_kernel(chans, filters, copies, spread, share, square):
    total = jnp.sum(spread[...].astype(F32), axis=0)
    share[...] = total
    sq = total * total
    lane = lax.broadcasted_iota(jnp.int32, sq.shape, 1)
    row = lax.broadcasted_iota(jnp.int32, sq.shape, 0)
    beside = jnp.where((row == 0) & (lane < chans + filters), sq / copies, 0.0)
    square[...] = jnp.full(square.shape, jnp.sum(jnp.where(lane < chans, sq, beside)), F32)


def sum_shares(spread, chans, filters, copies):
    return pl.pallas_call(
        functools.partial(sum_kernel, chans, filters, copies),
        out_shape=(
            jax.ShapeDtypeStruct(spread.shape[1:], F32),
            jax.ShapeDtypeStruct((1, 128), F32),
        ),
        compiler_params=params(SMALL_LIMIT),
        name="sum_shares",
    )(spread)


def local(
    bands, panels,
    inputs, cotangent, basis_values, basis_index, lon_reach, filters, weight_in, weight_out,
):
    rows, cols, chans = inputs.shape
    pairs = rows // PAIR
    per = chans // bands
    first_row = lax.axis_index("lat") * rows
    ext = rows + 2 * REACH_LAT
    with jax.named_scope("input_halo"):
        side = exchange_columns(inputs[:, :HALF], inputs[:, cols - HALF :], panels)
        lo, hi = exchange_rows(
            beside(inputs[:REACH_LAT], side[:REACH_LAT]),
            beside(inputs[rows - REACH_LAT :], side[rows - REACH_LAT :]), bands,
        )
    with jax.named_scope("bands"):

        def cut(a):
            padded = jnp.pad(a, ((REACH_LAT, REACH_LAT),) + ((0, 0),) * (a.ndim - 1))
            return lax.dynamic_slice_in_dim(padded, first_row, ext, 0)

        tables = (
            cut(basis_values).reshape(-1, COL_TAPS).T,
            cut(basis_index).reshape(-1, COL_TAPS).T,
            cut(lon_reach).reshape(1, -1),
        )
        band = band_matrix(0, *tables, pairs)
        filt = filters.T
    out, gf_mid, edge_mid, *sums = mixer_inner(
        inputs, side, band, filt, weight_in, weight_out, cotangent
    )
    tables, out = lax.optimization_barrier((tables, out))
    band_adj = band_matrix(1, *tables, pairs)
    core = lax.axis_index("lon") % 2
    out, gf_end, edge_end, keep, give = mixer_outer(
        core.astype(jnp.int32).reshape(1), per, inputs, side, lo, hi, band, filt,
        weight_in, weight_out, cotangent, out, sums,
    )
    with jax.named_scope("grad_halo"):
        edge = jnp.concatenate([edge_end, edge_mid], axis=0)
        gside = exchange_columns(edge[:, :HALF], edge[:, HALF:], panels)
        end_side, mid_side = gside[: 2 * PAIR], gside[2 * PAIR :]
        ends = beside(gf_end[:PAIR], end_side[:PAIR]), beside(gf_end[PAIR:], end_side[PAIR:])
    back = adjoint_inner(gf_mid, mid_side, gf_end, end_side, band_adj, filt, cotangent)
    with jax.named_scope("reduce"):
        lanes, half = chans + 128, per // 2
        total = (keep + swap(give, panels, 1).astype(F32)).reshape(bands, per, lanes)
        upper = lax.axis_index("lon") // 2 == 1
        kept = jnp.where(upper, total[:, half:], total[:, :half])
        give = jnp.where(upper, total[:, :half], total[:, half:]).astype(BF)
        part = (kept + swap(give, panels, 2).astype(F32)).astype(BF)
        part, back, ends = lax.optimization_barrier((part, back, ends))
        halos = exchange_rows(*ends, bands)
        spread = lax.all_to_all(part, "lat", 0, 0)
    with jax.named_scope("norm"):
        share, square = sum_shares(spread, chans, BASIS * per, panels)
        mats, filt_row = share[:, :chans], share[:1, chans : chans + BASIS * per]
        near, across, far = (swap(mats, panels, bits) for bits in (2, 1, 3))
        every = lax.all_to_all(
            jnp.broadcast_to(square, (bands * panels, 1, 128)), ("lat", "lon"), 0, 0
        )
        near, across, far, every = lax.optimization_barrier((near, across, far, every))
        grad_total = jnp.sum(every[:, 0, 0])
        scale = jnp.minimum(jnp.float32(1.0), jnp.float32(CLIP) / jnp.sqrt(grad_total + EPS))

        def stack(own, other):
            return jnp.concatenate(
                [jnp.where(upper, other, own), jnp.where(upper, own, other)], axis=0
            )

        own, other = stack(mats, near), stack(across, far)
        odd = core == 1
        shares = (
            scale * jnp.where(odd, other, own),
            (scale * jnp.where(odd, own, other)).T,
            scale * filt_row.reshape(BASIS, per).T,
        )
    back = adjoint_outer(
        gf_mid, mid_side, gf_end, end_side, *halos, band_adj, filt, cotangent, back
    )
    return (out, back) + shares


def solution(mesh):
    bands, panels = mesh.shape["lat"], mesh.shape["lon"]
    field = P("lat", "lon", None)
    return jax.shard_map(
        functools.partial(local, bands, panels),
        mesh=mesh,
        in_specs=(field, field, P(), P(), P(), P(), P(), P()),
        out_specs=(field, field, P("lat", None), P(None, "lat"), P("lat", None)),
        check_vma=False,
    )
```

time: 175 us -> 130 us (0.74); the launches traced: 173 us -> 130 us
  starting transfers between devices: 69.3 us -> 45.6 us
  waiting for transfers between devices: 11.4 us -> 29.6 us
  local copies, waits for them, and re-layouts: 28.7 us -> 11.7 us
  Pallas kernels: 48.5 us -> 34.7 us
  matrix products: 2.93 us -> 0 us
  other arithmetic: 8.61 us -> 6.32 us
    ppermute x12 -> x9, starting transfers between devices: 45.1 us -> 25.6 us  [the longest x4 22.6 us: exchange_rows(): return (lax.ppermute(last, 'lat', up), lax.ppermute(first, 'lat', down))]
    ppermute x12 -> x9, waiting for transfers between devices: 10.1 us -> 22.3 us  [the longest x4 18.1 us: exchange_rows(): return (lax.ppermute(last, 'lat', up), lax.ppermute(first, 'lat', down))]
    pallas_call x5 -> x6, Pallas kernels: 32.9 us -> 22.8 us  [the longest x1 11.1 us: mixer_outer(): pl.pallas_call(functools.partial(outer_kernel, per), grid=(2,), in_specs=...]
    reshape x3 -> x5, local copies, waits for them, and re-layouts: 9.56 us -> 0.56 us  [the longest x2 0.24 us: local(): cut(basis_index).reshape(-1, COL_TAPS)]
    all_to_all x2, starting transfers between devices: 22.1 us -> 16.4 us  [the longest x1 9.84 us: local(): spread = lax.all_to_all(part, 'lat', 0, 0)]
    all_to_all x2, waiting for transfers between devices: 1.26 us -> 5.35 us  [the longest x1 5.35 us: local(): spread = lax.all_to_all(part, 'lat', 0, 0)]
    convert_element_type x2 -> x0, local copies, waits for them, and re-layouts: 4.08 us -> none  [band_matrices(): out.append(full.astype(BF).reshape(pairs, BASIS * PAIR * TILE, WIN * SPAN))]
    reduce_sum x4 -> x1, other arithmetic: 4.7 us -> 0.87 us  [local(): grad_total = jnp.sum(every[:, 0, 0])]
  transfers between devices with their start and end apart: 18 -> 15, of which waited for: 4 -> 8; matrix products, arithmetic and copies ran while one was open for 15% -> 4% of each run, Pallas kernels for 22% -> 18%
where the time goes in v2:
time: 130 us
  starting transfers between devices  45.6 us (35%)
  Pallas kernels  34.7 us (27%)
  waiting for transfers between devices  29.6 us (23%)
  local copies, waits for them, and re-layouts  11.7 us (9%)
  other arithmetic  6.32 us (5%)
  between operations  1.85 us (1%)
    ppermute x4, starting transfers between devices, exchange_rows(): return (lax.ppermute(last, 'lat', up), lax.ppermute(first, 'lat', down))  22.6 us
    ppermute x4, waiting for transfers between devices, exchange_rows(): return (lax.ppermute(last, 'lat', up), lax.ppermute(first, 'lat', down))  18.1 us
    pallas_call x1, Pallas kernels, mixer_inner(): pl.pallas_call(inner_kernel, grid=(2,), in_specs=[whole(x.shape), whole(s...  11.9 us
    pallas_call x1, Pallas kernels, mixer_outer(): pl.pallas_call(functools.partial(outer_kernel, per), grid=(2,), in_specs=...  11.1 us
    all_to_all x1, starting transfers between devices, local(): spread = lax.all_to_all(part, 'lat', 0, 0)  9.84 us
    unnamed x62, local copies, waits for them, and re-layouts  7.64 us
    all_to_all x1, starting transfers between devices, local(): lax.all_to_all(jnp.broadcast_to(square, (bands * panels, 1, 128)), ('lat'...  6.56 us
    pallas_call x1, Pallas kernels, adjoint_outer(): pl.pallas_call(outer_adjoint, grid=(2,), in_specs=[blocks(PAIR, mid.shape...  5.65 us
  transfers between devices with their start and end apart: 15, of which 8 were waited for; matrix products, arithmetic and copies ran while one was open for 4% of the time, Pallas kernels for 18%

profile of v2, /device:TPU:2, one launch (start us, length us, event | category | flops | bytes accessed | tf_op | source)
XLA Modules:
  0.0 129.8 jit_solution(9092564975590058576)
XLA Ops:
  0.7 0.9 fusion.1
  1.7 1.7 %collective-permute-start = (bf16[8,8,512]{2,1,0:T(8,128)(2,1)S(1)}, bf16[8,8,512]{2,1,0:T(8,128)(2,1)S(1)}, u32[]{:S(2)}, u32[]{:S(2)}) collective-permute-start(bf16[8,8,512]{2,1,0:T(8,128)(2,1)S(1)} %get-tuple-element.78), channel_id=1, source_target_pairs={{0,3},{1,0},{2,1},{3,2},{4,7},{5,4},{6,5},{7,6},{8,11},{9,8},{10,9... | collective-permute-start | bytes 196616 | tf_op jit(solution)/shard_map/input_halo/ppermute | solution.py:444
  3.4 1.3 fusion
  5.1 0.1 copy.41
  5.4 0.9 pad_maximum_fusion
  6.3 5.1 %collective-permute-start.2 = (bf16[2,272,512]{2,1,0:T(8,128)(2,1)}, bf16[2,272,512]{2,1,0:T(8,128)(2,1)S(1)}, u32[]{:S(2)}, u32[]{:S(2)}) collective-permute-start(bf16[2,272,512]{2,1,0:T(8,128)(2,1)} %pad_maximum_fusion), channel_id=1, source_target_pairs={{0,4},{4,8},{8,12},{12,16},{16,20},{20,24},{24,28},{28,32},{32,36}... | collective-permute-start | bytes 1671176 | tf_op jit(solution)/shard_map/input_halo/ppermute | solution.py:456
  11.4 0.9 pad_maximum_fusion.1
  12.3 7.2 %collective-permute-start.3 = (bf16[2,272,512]{2,1,0:T(8,128)(2,1)}, bf16[2,272,512]{2,1,0:T(8,128)(2,1)}, u32[]{:S(2)}, u32[]{:S(2)}) collective-permute-start(bf16[2,272,512]{2,1,0:T(8,128)(2,1)} %pad_maximum_fusion.1), channel_id=1, source_target_pairs={{4,0},{8,4},{12,8},{16,12},{20,16},{24,20},{28,24},{32,28},{36,32}... | collective-permute-start | bytes 1671176 | tf_op jit(solution)/shard_map/input_halo/ppermute | solution.py:456
  19.8 1.0 band_forward.1.band
  20.8 0.8 copy-done.7
  21.7 11.9 %mixer_inner.1 = (bf16[8,256,512]{2,1,0:T(8,128)(2,1)}, bf16[4,256,512]{2,1,0:T(8,128)(2,1)}, bf16[4,16,512]{2,1,0:T(8,128)(2,1)}, f32[512,512]{1,0:T(8,128)}, f32[512,512]{1,0:T(8,128)}, /*index=5*/f32[72,512]{1,0:T(8,128)}) custom-call(bf16[8,256,512]{2,1,0:T(8,128)(2,1)} %x.9, bf16[8,16,512]{2,1,0:T(8,128)(2,1)} %copy-done.12, ...), custom_call_target="tpu_custom_call" | custom-call | flops 5033164800 | bytes 5242880 | tf_op jit(solution)/shard_map/mixer_inner/pallas_call | solution.py:331
  33.6 1.0 band_adjoint.1.band
  34.6 1.7 %collective-permute-done.2.lo = bf16[2,272,512]{2,1,0:T(8,128)(2,1)S(1)} collective-permute-done((bf16[2,272,512]{2,1,0:T(8,128)(2,1)}, bf16[2,272,512]{2,1,0:T(8,128)(2,1)S(1)}, u32[]{:S(2)}, u32[]{:S(2)}) %collective-permute-start.2) | collective-permute-done | bytes 557088 | tf_op jit(solution)/shard_map/input_halo/ppermute | solution.py:456
  36.3 0.8 copy-done.14
  37.1 5.2 %collective-permute-done.3.hi = bf16[2,272,512]{2,1,0:T(8,128)(2,1)} collective-permute-done((bf16[2,272,512]{2,1,0:T(8,128)(2,1)}, bf16[2,272,512]{2,1,0:T(8,128)(2,1)}, u32[]{:S(2)}, u32[]{:S(2)}) %collective-permute-start.3) | collective-permute-done | bytes 557088 | tf_op jit(solution)/shard_map/input_halo/ppermute | solution.py:456
  42.4 1.0 copy-done.15
  43.5 1.2 copy-done.18
  44.7 1.2 copy-done.19
  45.9 0.9 copy-done.20
  46.8 11.1 %mixer_outer.1 = (bf16[8,256,512]{2,1,0:T(8,128)(2,1)}, bf16[4,256,512]{2,1,0:T(8,128)(2,1)S(1)}, bf16[4,16,512]{2,1,0:T(8,128)(2,1)S(1)}, f32[512,640]{1,0:T(8,128)S(1)}, bf16[512,640]{1,0:T(8,128)(2,1)S(1)}) custom-call(s32[1]{0:T(128)} %bitcast.odd, bf16[8,256,512]{2,1,0:T(8,128)(2,1)S(1)} %copy-done.4, ...), custom_call_target="tpu_custom_call", output_to_operand_aliasing={{0}: (10, {})} | custom-call | flops 5033164800 | bytes 5242880 | tf_op jit(solution)/shard_map/mixer_outer/pallas_call | solution.py:360
  58.0 0.2 collective-permute-start.5
  58.2 1.7 %collective-permute-start.4 = (bf16[8,8,512]{2,1,0:T(8,128)(2,1)S(1)}, bf16[8,8,512]{2,1,0:T(8,128)(2,1)S(1)}, u32[]{:S(2)}, u32[]{:S(2)}) collective-permute-start(bf16[8,8,512]{2,1,0:T(8,128)(2,1)S(1)} %get-tuple-element.86), channel_id=1, source_target_pairs={{0,3},{1,0},{2,1},{3,2},{4,7},{5,4},{6,5},{7,6},{8,11},{9,8},{10,9... | collective-permute-start | bytes 196616 | tf_op jit(solution)/shard_map/grad_halo/ppermute | solution.py:444
  59.9 1.8 %collective-permute-done.4 = bf16[8,8,512]{2,1,0:T(8,128)(2,1)S(1)} collective-permute-done((bf16[8,8,512]{2,1,0:T(8,128)(2,1)S(1)}, bf16[8,8,512]{2,1,0:T(8,128)(2,1)S(1)}, u32[]{:S(2)}, u32[]{:S(2)}) %collective-permute-start.4) | collective-permute-done | bytes 65568 | tf_op jit(solution)/shard_map/grad_halo/ppermute | solution.py:444
  61.9 0.2 add_bitcast_fusion
  62.1 0.2 select_convert_fusion
  62.3 0.7 collective-permute-start.7
  63.1 0.8 pad_maximum_fusion.3
  63.9 0.8 pad_maximum_fusion.2
  64.8 3.8 %adjoint_inner.1.partial_out = bf16[8,256,512]{2,1,0:T(8,128)(2,1)} custom-call(bf16[4,256,512]{2,1,0:T(8,128)(2,1)S(1)} %copy-done.3, bf16[4,16,512]{2,1,0:T(8,128)(2,1)S(1)} %get-tuple-element.84.mid_side, bf16[4,256,512]{2,1,0:T(8,128)(2,1)S(1)} %get-tuple-element.39.end, bf16[4,16,512]{2,1,0:T(8,128)(2,1)S(1)} %get-tuple-element.83.end_side, ...), custom_call_target="tpu_custom_call" | custom-call | flops 1811939328 | bytes 3145728 | tf_op jit(solution)/shard_map/adjoint_inner/pallas_call | solution.py:400
  68.6 4.1 %collective-permute-done.7 = bf16[64,4,640]{2,1,0:T(4,128)(2,1)S(1)} collective-permute-done((bf16[64,4,640]{2,1,0:T(4,128)(2,1)S(1)}, bf16[64,4,640]{2,1,0:T(4,128)(2,1)S(1)}, u32[]{:S(2)}, u32[]{:S(2)}) %collective-permute-start.7) | collective-permute-done | bytes 327712 | tf_op jit(solution)/shard_map/reduce/ppermute | solution.py:460
  72.7 1.0 add_convert_fusion
  73.7 9.8 %all-to-all-start = ((bf16[64,4,640]{2,1,0:T(4,128)(2,1)}), bf16[64,4,640]{2,1,0:T(4,128)(2,1)S(1)}, u32[]{:S(2)}, u32[]{:S(2)}) async-start(bf16[64,4,640]{2,1,0:T(4,128)(2,1)} %add_convert_fusion), calls=%async_computation | async-start | bytes 655360 | tf_op jit(solution)/shard_map/reduce/all_to_all | solution.py:538
  83.6 4.9 %collective-permute-start.8 = (bf16[2,272,512]{2,1,0:T(8,128)(2,1)S(1)}, bf16[2,272,512]{2,1,0:T(8,128)(2,1)S(1)}, u32[]{:S(2)}, u32[]{:S(2)}) collective-permute-start(bf16[2,272,512]{2,1,0:T(8,128)(2,1)S(1)} %copy-done.23), channel_id=1, source_target_pairs={{0,4},{4,8},{8,12},{12,16},{16,20},{20,24},{24,28},{28,32},{32,36}... | collective-permute-start | bytes 1671176 | tf_op jit(solution)/shard_map/reduce/ppermute | solution.py:456
  88.5 5.5 %collective-permute-start.9 = (bf16[2,272,512]{2,1,0:T(8,128)(2,1)S(1)}, bf16[2,272,512]{2,1,0:T(8,128)(2,1)S(1)}, u32[]{:S(2)}, u32[]{:S(2)}) collective-permute-start(bf16[2,272,512]{2,1,0:T(8,128)(2,1)S(1)} %copy-done.24), channel_id=1, source_target_pairs={{4,0},{8,4},{12,8},{16,12},{20,16},{24,20},{28,24},{32,28},{36,32}... | collective-permute-start | bytes 1671176 | tf_op jit(solution)/shard_map/reduce/ppermute | solution.py:456
  94.0 5.3 %all-to-all-done.spread = bf16[64,4,640]{2,1,0:T(4,128)(2,1)S(1)} async-done(((bf16[64,4,640]{2,1,0:T(4,128)(2,1)}), bf16[64,4,640]{2,1,0:T(4,128)(2,1)S(1)}, u32[]{:S(2)}, u32[]{:S(2)}) %all-to-all-start) | async-done | bytes 327712 | tf_op jit(solution)/shard_map/reduce/all_to_all | solution.py:538
  99.3 0.3 sum_shares.1
  99.6 0.7 broadcast_in_dim.3
  100.3 6.6 %all-to-all-start.1 = ((f32[256,1,128]{2,1,0:T(1,128)}), f32[256,1,128]{2,1,0:T(1,128)S(1)}, u32[]{:S(2)}, u32[]{:S(2)}) async-start(f32[256,1,128]{2,1,0:T(1,128)} %broadcast_in_dim.3), calls=%async_computation.1 | async-start | bytes 262144 | tf_op jit(solution)/shard_map/norm/all_to_all | solution.py:543
  106.9 1.4 %collective-permute-start.12 = (f32[4,512]{1,0:T(4,128)S(1)}, f32[4,512]{1,0:T(4,128)S(1)}, u32[]{:S(2)}, u32[]{:S(2)}) collective-permute-start(f32[4,512]{1,0:T(4,128)S(1)} %slice.77), channel_id=1, source_target_pairs={{0,3},{1,2},{2,1},{3,0},{4,7},{5,6},{6,5},{7,4},{8,11},{9,10},{10,... | collective-permute-start | bytes 24584 | tf_op jit(solution)/shard_map/norm/ppermute | solution.py:460
  108.3 0.4 collective-permute-start.11
  108.7 0.5 collective-permute-start.10
  109.2 6.9 %collective-permute-done.8.lo = bf16[2,272,512]{2,1,0:T(8,128)(2,1)S(1)} collective-permute-done((bf16[2,272,512]{2,1,0:T(8,128)(2,1)S(1)}, bf16[2,272,512]{2,1,0:T(8,128)(2,1)S(1)}, u32[]{:S(2)}, u32[]{:S(2)}) %collective-permute-start.8) | collective-permute-done | bytes 557088 | tf_op jit(solution)/shard_map/reduce/ppermute | solution.py:456
  116.1 4.2 %collective-permute-done.9.hi = bf16[2,272,512]{2,1,0:T(8,128)(2,1)S(1)} collective-permute-done((bf16[2,272,512]{2,1,0:T(8,128)(2,1)S(1)}, bf16[2,272,512]{2,1,0:T(8,128)(2,1)S(1)}, u32[]{:S(2)}, u32[]{:S(2)}) %collective-permute-start.9) | collective-permute-done | bytes 557088 | tf_op jit(solution)/shard_map/reduce/ppermute | solution.py:456
  120.3 0.8 copy-done.22
  121.1 5.6 %adjoint_outer.1 = bf16[8,256,512]{2,1,0:T(8,128)(2,1)} custom-call(bf16[4,256,512]{2,1,0:T(8,128)(2,1)} %get-tuple-element.36.mid, bf16[4,16,512]{2,1,0:T(8,128)(2,1)} %copy-done.6, bf16[4,256,512]{2,1,0:T(8,128)(2,1)} %copy-done, bf16[4,16,512]{2,1,0:T(8,128)(2,1)} %copy-done.5, bf16[2,272,512]{2,1,0:T(8,128)(2,1)} %copy-done.21, ...), custom_call_target="tpu_custom_call", output_to_operand_aliasing={{}: (9, {})} | custom-call | flops 1811939328 | bytes 3145728 | tf_op jit(solution)/shard_map/adjoint_outer/pallas_call | solution.py:420
  126.8 0.9 slice_reduce_fusion
  128.4 0.7 copy.39
  129.1 0.6 multiply_bitcast_fusion
  (84 shorter events, 1.4 us)
Async XLA Ops:
  0.6 4.1 %copy-start.28 = (s32[512,5]{0,1:T(8,128)S(1)}, s32[512,5]{0,1:T(8,128)}, u32[]{:S(2)}) copy-start(s32[512,5]{0,1:T(8,128)} %param.14) | copy-start | bytes 30724
  0.6 4.3 %copy-start.25 = (s32[512,5,9]{0,1,2:T(8,128)S(1)}, s32[512,5,9]{0,1,2:T(8,128)}, u32[]{:S(2)}) copy-start(s32[512,5,9]{0,1,2:T(8,128)} %param.13) | copy-start | bytes 276484
  1.6 3.8 %collective-permute-start.1 = (bf16[8,8,512]{2,1,0:T(8,128)(2,1)S(1)}, bf16[8,8,512]{2,1,0:T(8,128)(2,1)S(1)}, u32[]{:S(2)}, u32[]{:S(2)}) collective-permute-start(bf16[8,8,512]{2,1,0:T(8,128)(2,1)S(1)} %get-tuple-element.77), channel_id=1, source_target_pairs={{0,1},{1,2},{2,3},{3,0},{4,5},{5,6},{6,7},{7,4},{8,9},{9,10},{10,1... | collective-permute-start | bytes 196616 | tf_op jit(solution)/shard_map/input_halo/ppermute | solution.py:445
  1.7 3.7 %collective-permute-start = (bf16[8,8,512]{2,1,0:T(8,128)(2,1)S(1)}, bf16[8,8,512]{2,1,0:T(8,128)(2,1)S(1)}, u32[]{:S(2)}, u32[]{:S(2)}) collective-permute-start(bf16[8,8,512]{2,1,0:T(8,128)(2,1)S(1)} %get-tuple-element.78), channel_id=1, source_target_pairs={{0,3},{1,0},{2,1},{3,2},{4,7},{5,4},{6,5},{7,6},{8,11},{9,8},{10,9... | collective-permute-start | bytes 196616 | tf_op jit(solution)/shard_map/input_halo/ppermute | solution.py:444
  5.3 14.1 %copy-start.26 = (f32[512,5,9]{0,1,2:T(8,128)S(1)}, f32[512,5,9]{0,1,2:T(8,128)}, u32[]{:S(2)}) copy-start(f32[512,5,9]{0,1,2:T(8,128)} %param.12) | copy-start | bytes 276484
  5.4 14.3 %copy-start.12 = (bf16[8,16,512]{2,1,0:T(8,128)(2,1)}, bf16[8,16,512]{2,1,0:T(8,128)(2,1)S(1)}, u32[]{:S(2)}) copy-start(bf16[8,16,512]{2,1,0:T(8,128)(2,1)S(1)} %constant_dynamic-update-slice_fusion.side) | copy-start | bytes 393220
  5.4 14.4 %copy-start.10 = (bf16[60,2048]{1,0:T(8,128)(2,1)S(1)}, bf16[60,2048]{1,0:T(8,128)(2,1)}, u32[]{:S(2)}) copy-start(bf16[60,2048]{1,0:T(8,128)(2,1)} %constant.52.clone.pick) | copy-start | bytes 737284
  6.3 30.0 %collective-permute-start.2 = (bf16[2,272,512]{2,1,0:T(8,128)(2,1)}, bf16[2,272,512]{2,1,0:T(8,128)(2,1)S(1)}, u32[]{:S(2)}, u32[]{:S(2)}) collective-permute-start(bf16[2,272,512]{2,1,0:T(8,128)(2,1)} %pad_maximum_fusion), channel_id=1, source_target_pairs={{0,4},{4,8},{8,12},{12,16},{16,20},{20,24},{24,28},{28,32},{32,36}... | collective-permute-start | bytes 1671176 | tf_op jit(solution)/shard_map/input_halo/ppermute | solution.py:456
  12.3 30.1 %collective-permute-start.3 = (bf16[2,272,512]{2,1,0:T(8,128)(2,1)}, bf16[2,272,512]{2,1,0:T(8,128)(2,1)}, u32[]{:S(2)}, u32[]{:S(2)}) collective-permute-start(bf16[2,272,512]{2,1,0:T(8,128)(2,1)} %pad_maximum_fusion.1), channel_id=1, source_target_pairs={{4,0},{8,4},{12,8},{16,12},{20,16},{24,20},{28,24},{32,28},{36,32}... | collective-permute-start | bytes 1671176 | tf_op jit(solution)/shard_map/input_halo/ppermute | solution.py:456
  20.8 0.8 copy-start.7
  21.6 12.0 %copy-start.9 = (bf16[60,2048]{1,0:T(8,128)(2,1)S(1)}, bf16[60,2048]{1,0:T(8,128)(2,1)}, u32[]{:S(2)}) copy-start(bf16[60,2048]{1,0:T(8,128)(2,1)} %constant.53.clone.pick) | copy-start | bytes 737284
  21.6 20.8 %copy-start.1 = (bf16[8,256,512]{2,1,0:T(8,128)(2,1)S(1)}, bf16[8,256,512]{2,1,0:T(8,128)(2,1)}, u32[]{:S(2)}) copy-start(bf16[8,256,512]{2,1,0:T(8,128)(2,1)} %cot.7) | copy-start | bytes 6291460
  21.6 20.8 %copy-start.4 = (bf16[8,256,512]{2,1,0:T(8,128)(2,1)S(1)}, bf16[8,256,512]{2,1,0:T(8,128)(2,1)}, u32[]{:S(2)}) copy-start(bf16[8,256,512]{2,1,0:T(8,128)(2,1)} %x.9) | copy-start | bytes 6291460
  21.6 20.8 %copy-start.8 = (bf16[4,288,192]{2,1,0:T(8,128)(2,1)S(1)}, bf16[4,288,192]{2,1,0:T(8,128)(2,1)}, u32[]{:S(2)}) copy-start(bf16[4,288,192]{2,1,0:T(8,128)(2,1)} %copy-done.7) | copy-start | bytes 1327108
  21.6 20.8 %copy-start.11 = (f32[512,9]{0,1:T(8,128)S(1)}, f32[512,9]{0,1:T(8,128)}, u32[]{:S(2)}) copy-start(f32[512,9]{0,1:T(8,128)} %param.15) | copy-start | bytes 55300
  21.6 20.8 %copy-start.13 = (bf16[8,16,512]{2,1,0:T(8,128)(2,1)S(1)}, bf16[8,16,512]{2,1,0:T(8,128)(2,1)}, u32[]{:S(2)}) copy-start(bf16[8,16,512]{2,1,0:T(8,128)(2,1)} %copy-done.12) | copy-start | bytes 393220
  21.6 20.8 %copy-start.16 = (bf16[512,512]{1,0:T(8,128)(2,1)S(1)}, bf16[512,512]{1,0:T(8,128)(2,1)}, u32[]{:S(2)}) copy-start(bf16[512,512]{1,0:T(8,128)(2,1)} %w_in.3) | copy-start | bytes 1572868
  21.6 20.8 %copy-start.17 = (bf16[512,512]{1,0:T(8,128)(2,1)S(1)}, bf16[512,512]{1,0:T(8,128)(2,1)}, u32[]{:S(2)}) copy-start(bf16[512,512]{1,0:T(8,128)(2,1)} %w_out.3) | copy-start | bytes 1572868
  34.5 30.2 %copy-start.2 = (bf16[4,288,192]{2,1,0:T(8,128)(2,1)}, bf16[4,288,192]{2,1,0:T(8,128)(2,1)S(1)}, u32[]{:S(2)}) copy-start(bf16[4,288,192]{2,1,0:T(8,128)(2,1)S(1)} %band_adjoint.1.band) | copy-start | bytes 1327108
  36.3 0.8 copy-start.14
  42.4 1.1 copy-start.15
  43.5 1.2 copy-start.18
  44.7 1.2 copy-start.19
  45.9 0.9 copy-start.20
  46.8 11.1 %copy-start.27 = (bf16[4,16,512]{2,1,0:T(8,128)(2,1)S(1)}, bf16[4,16,512]{2,1,0:T(8,128)(2,1)}, u32[]{:S(2)}) copy-start(bf16[4,16,512]{2,1,0:T(8,128)(2,1)} %get-tuple-element.38) | copy-start | bytes 196612
  57.9 6.8 %copy-start = (bf16[4,256,512]{2,1,0:T(8,128)(2,1)}, bf16[4,256,512]{2,1,0:T(8,128)(2,1)S(1)}, u32[]{:S(2)}) copy-start(bf16[4,256,512]{2,1,0:T(8,128)(2,1)S(1)} %get-tuple-element.39.end) | copy-start | bytes 3145732
  58.0 3.8 %collective-permute-start.5 = (bf16[8,8,512]{2,1,0:T(8,128)(2,1)S(1)}, bf16[8,8,512]{2,1,0:T(8,128)(2,1)S(1)}, u32[]{:S(2)}, u32[]{:S(2)}) collective-permute-start(bf16[8,8,512]{2,1,0:T(8,128)(2,1)S(1)} %get-tuple-element.85), channel_id=1, source_target_pairs={{0,1},{1,2},{2,3},{3,0},{4,5},{5,6},{6,7},{7,4},{8,9},{9,10},{10,1... | collective-permute-start | bytes 196616 | tf_op jit(solution)/shard_map/grad_halo/ppermute | solution.py:445
  58.2 3.6 %collective-permute-start.4 = (bf16[8,8,512]{2,1,0:T(8,128)(2,1)S(1)}, bf16[8,8,512]{2,1,0:T(8,128)(2,1)S(1)}, u32[]{:S(2)}, u32[]{:S(2)}) collective-permute-start(bf16[8,8,512]{2,1,0:T(8,128)(2,1)S(1)} %get-tuple-element.86), channel_id=1, source_target_pairs={{0,3},{1,0},{2,1},{3,2},{4,7},{5,4},{6,5},{7,6},{8,11},{9,8},{10,9... | collective-permute-start | bytes 196616 | tf_op jit(solution)/shard_map/grad_halo/ppermute | solution.py:444
  59.8 2.1 %collective-permute-start.6 = (bf16[512,640]{1,0:T(8,128)(2,1)S(1)}, bf16[512,640]{1,0:T(8,128)(2,1)S(1)}, u32[]{:S(2)}, u32[]{:S(2)}) collective-permute-start(bf16[512,640]{1,0:T(8,128)(2,1)S(1)} %get-tuple-element.41), channel_id=1, source_target_pairs={{0,1},{1,0},{2,3},{3,2},{4,5},{5,4},{6,7},{7,6},{8,9},{9,8},{10,11... | collective-permute-start | bytes 1966088 | tf_op jit(solution)/shard_map/reduce/ppermute | solution.py:460
  61.8 3.0 %copy-start.5 = (bf16[4,16,512]{2,1,0:T(8,128)(2,1)}, bf16[4,16,512]{2,1,0:T(8,128)(2,1)S(1)}, u32[]{:S(2)}) copy-start(bf16[4,16,512]{2,1,0:T(8,128)(2,1)S(1)} %get-tuple-element.83.end_side) | copy-start | bytes 196612
  61.8 3.0 %copy-start.6 = (bf16[4,16,512]{2,1,0:T(8,128)(2,1)}, bf16[4,16,512]{2,1,0:T(8,128)(2,1)S(1)}, u32[]{:S(2)}) copy-start(bf16[4,16,512]{2,1,0:T(8,128)(2,1)S(1)} %get-tuple-element.84.mid_side) | copy-start | bytes 196612
  62.3 2.4 %copy-start.3 = (bf16[4,256,512]{2,1,0:T(8,128)(2,1)S(1)}, bf16[4,256,512]{2,1,0:T(8,128)(2,1)}, u32[]{:S(2)}) copy-start(bf16[4,256,512]{2,1,0:T(8,128)(2,1)} %get-tuple-element.36.mid) | copy-start | bytes 3145732
  62.3 10.4 %collective-permute-start.7 = (bf16[64,4,640]{2,1,0:T(4,128)(2,1)S(1)}, bf16[64,4,640]{2,1,0:T(4,128)(2,1)S(1)}, u32[]{:S(2)}, u32[]{:S(2)}) collective-permute-start(bf16[64,4,640]{2,1,0:T(4,128)(2,1)S(1)} %select_convert_fusion), channel_id=1, source_target_pairs={{0,2},{1,3},{2,0},{3,1},{4,6},{5,7},{6,4},{7,5},{8,10},{9,11},{10,... | collective-permute-start | bytes 983048 | tf_op jit(solution)/shard_map/reduce/ppermute | solution.py:460
  68.6 15.0 %copy-start.23 = (bf16[2,272,512]{2,1,0:T(8,128)(2,1)S(1)}, bf16[2,272,512]{2,1,0:T(8,128)(2,1)}, u32[]{:S(2)}) copy-start(bf16[2,272,512]{2,1,0:T(8,128)(2,1)} %pad_maximum_fusion.3) | copy-start | bytes 1671172
  68.6 19.9 %copy-start.24 = (bf16[2,272,512]{2,1,0:T(8,128)(2,1)S(1)}, bf16[2,272,512]{2,1,0:T(8,128)(2,1)}, u32[]{:S(2)}) copy-start(bf16[2,272,512]{2,1,0:T(8,128)(2,1)} %pad_maximum_fusion.2) | copy-start | bytes 1671172
  73.7 25.6 %all-to-all-start = ((bf16[64,4,640]{2,1,0:T(4,128)(2,1)}), bf16[64,4,640]{2,1,0:T(4,128)(2,1)S(1)}, u32[]{:S(2)}, u32[]{:S(2)}) async-start(bf16[64,4,640]{2,1,0:T(4,128)(2,1)} %add_convert_fusion), calls=%async_computation | async-start | bytes 655360 | tf_op jit(solution)/shard_map/reduce/all_to_all | solution.py:538
  83.6 32.5 %collective-permute-start.8 = (bf16[2,272,512]{2,1,0:T(8,128)(2,1)S(1)}, bf16[2,272,512]{2,1,0:T(8,128)(2,1)S(1)}, u32[]{:S(2)}, u32[]{:S(2)}) collective-permute-start(bf16[2,272,512]{2,1,0:T(8,128)(2,1)S(1)} %copy-done.23), channel_id=1, source_target_pairs={{0,4},{4,8},{8,12},{12,16},{16,20},{20,24},{24,28},{28,32},{32,36}... | collective-permute-start | bytes 1671176 | tf_op jit(solution)/shard_map/reduce/ppermute | solution.py:456
  88.5 31.8 %collective-permute-start.9 = (bf16[2,272,512]{2,1,0:T(8,128)(2,1)S(1)}, bf16[2,272,512]{2,1,0:T(8,128)(2,1)S(1)}, u32[]{:S(2)}, u32[]{:S(2)}) collective-permute-start(bf16[2,272,512]{2,1,0:T(8,128)(2,1)S(1)} %copy-done.24), channel_id=1, source_target_pairs={{4,0},{8,4},{12,8},{16,12},{20,16},{24,20},{28,24},{32,28},{36,32}... | collective-permute-start | bytes 1671176 | tf_op jit(solution)/shard_map/reduce/ppermute | solution.py:456
  100.3 26.4 %all-to-all-start.1 = ((f32[256,1,128]{2,1,0:T(1,128)}), f32[256,1,128]{2,1,0:T(1,128)S(1)}, u32[]{:S(2)}, u32[]{:S(2)}) async-start(f32[256,1,128]{2,1,0:T(1,128)} %broadcast_in_dim.3), calls=%async_computation.1 | async-start | bytes 262144 | tf_op jit(solution)/shard_map/norm/all_to_all | solution.py:543
  106.9 19.8 %collective-permute-start.12 = (f32[4,512]{1,0:T(4,128)S(1)}, f32[4,512]{1,0:T(4,128)S(1)}, u32[]{:S(2)}, u32[]{:S(2)}) collective-permute-start(f32[4,512]{1,0:T(4,128)S(1)} %slice.77), channel_id=1, source_target_pairs={{0,3},{1,2},{2,1},{3,0},{4,7},{5,6},{6,5},{7,4},{8,11},{9,10},{10,... | collective-permute-start | bytes 24584 | tf_op jit(solution)/shard_map/norm/ppermute | solution.py:460
  108.3 18.5 %collective-permute-start.11 = (f32[4,512]{1,0:T(4,128)S(1)}, f32[4,512]{1,0:T(4,128)S(1)}, u32[]{:S(2)}, u32[]{:S(2)}) collective-permute-start(f32[4,512]{1,0:T(4,128)S(1)} %slice.77), channel_id=1, source_target_pairs={{0,1},{1,0},{2,3},{3,2},{4,5},{5,4},{6,7},{7,6},{8,9},{9,8},{10,11... | collective-permute-start | bytes 24584 | tf_op jit(solution)/shard_map/norm/ppermute | solution.py:460
  108.7 18.1 %collective-permute-start.10 = (f32[4,512]{1,0:T(4,128)S(1)}, f32[4,512]{1,0:T(4,128)S(1)}, u32[]{:S(2)}, u32[]{:S(2)}) collective-permute-start(f32[4,512]{1,0:T(4,128)S(1)} %slice.77), channel_id=1, source_target_pairs={{0,2},{1,3},{2,0},{3,1},{4,6},{5,7},{6,4},{7,5},{8,10},{9,11},{10,... | collective-permute-start | bytes 24584 | tf_op jit(solution)/shard_map/norm/ppermute | solution.py:460
  116.1 4.2 %copy-start.21 = (bf16[2,272,512]{2,1,0:T(8,128)(2,1)}, bf16[2,272,512]{2,1,0:T(8,128)(2,1)S(1)}, u32[]{:S(2)}) copy-start(bf16[2,272,512]{2,1,0:T(8,128)(2,1)S(1)} %collective-permute-done.8.lo) | copy-start | bytes 1671172
  120.3 0.8 copy-start.22

commit v3 on v2

--- a/solution.py
+++ b/solution.py
@@ -25,7 +25,6 @@
 BF = jnp.bfloat16
 F32 = jnp.float32
 VMEM_LIMIT = 56 * 1024 * 1024
-MIDDLE_LIMIT = 42 * 1024 * 1024
 SMALL_LIMIT = 24 * 1024 * 1024
 
 
@@ -381,7 +380,7 @@
             pltpu.VMEM((8 * BASIS, chans), F32),
         ] + mixer_scratch(cols, chans),
         input_output_aliases={10: 0},
-        compiler_params=params(MIDDLE_LIMIT),
+        compiler_params=params(),
         cost_estimate=mixer_cost(cols, chans),
         name="mixer_outer",
     )(odd, x, side, lo, hi, band, filt, w_in, w_out, cot, partial_out, *sums)
@@ -480,6 +479,45 @@
         compiler_params=params(SMALL_LIMIT),
         name="sum_shares",
     )(spread)
+
+
+def scale_kernel(per, flags, every, mats, near, across, far, beside, w_in, w_out, filters, work):
+    total = jnp.sum(every[...], axis=0)
+    scale = jnp.minimum(1.0, CLIP / jnp.sqrt(total + EPS))[:, :1]
+    half = mats.shape[0]
+    upper = jnp.full(mats.shape, flags[1], jnp.int32) == 1
+    for n, (own, other) in enumerate(((mats, near), (across, far))):
+        work[n, :half, :] = jnp.where(upper, other[...], own[...]) * scale
+        work[n, half:, :] = jnp.where(upper, own[...], other[...]) * scale
+    odd = jnp.full(w_in.shape, flags[0], jnp.int32) == 1
+    w_in[...] = jnp.where(odd, work[1], work[0])
+    w_out[...] = jnp.where(odd, work[0], work[1]).T
+    lanes = beside.shape[1]
+    lane = lax.broadcasted_iota(jnp.int32, (per, lanes), 1)
+    chan = lax.broadcasted_iota(jnp.int32, (per, lanes), 0)
+    spread = jnp.where(lane % per == chan, beside[...], 0.0)
+    at = lax.broadcasted_iota(jnp.int32, (lanes, BASIS), 0) // per
+    fold = jnp.where(at == lax.broadcasted_iota(jnp.int32, (lanes, BASIS), 1), 1.0, 0.0)
+    sums = jnp.dot(spread, fold, precision=lax.Precision.HIGHEST, preferred_element_type=F32)
+    filters[...] = sums * scale
+
+
+def scaled(flags, every, mats, near, across, far, beside, per):
+    chans = mats.shape[1]
+    blocks_in = [pl.BlockSpec(memory_space=pltpu.SMEM)]
+    blocks_in += [pl.BlockSpec(memory_space=pltpu.VMEM)] * 6
+    return pl.pallas_call(
+        functools.partial(scale_kernel, per),
+        in_specs=blocks_in,
+        out_shape=(
+            jax.ShapeDtypeStruct((per, chans), F32),
+            jax.ShapeDtypeStruct((chans, per), F32),
+            jax.ShapeDtypeStruct((per, BASIS), F32),
+        ),
+        scratch_shapes=[pltpu.VMEM((2, per, chans), F32)],
+        compiler_params=params(SMALL_LIMIT),
+        name="scaled",
+    )(flags, every, mats, near, across, far, beside)
 
 
 def local(
@@ -538,31 +576,18 @@
         spread = lax.all_to_all(part, "lat", 0, 0)
     with jax.named_scope("norm"):
         share, square = sum_shares(spread, chans, BASIS * per, panels)
-        mats, filt_row = share[:, :chans], share[:1, chans : chans + BASIS * per]
+        mats = share[:, :chans]
         near, across, far = (swap(mats, panels, bits) for bits in (2, 1, 3))
         every = lax.all_to_all(
             jnp.broadcast_to(square, (bands * panels, 1, 128)), ("lat", "lon"), 0, 0
         )
         near, across, far, every = lax.optimization_barrier((near, across, far, every))
-        grad_total = jnp.sum(every[:, 0, 0])
-        scale = jnp.minimum(jnp.float32(1.0), jnp.float32(CLIP) / jnp.sqrt(grad_total + EPS))
-
-        def stack(own, other):
-            return jnp.concatenate(
-                [jnp.where(upper, other, own), jnp.where(upper, own, other)], axis=0
-            )
-
-        own, other = stack(mats, near), stack(across, far)
-        odd = core == 1
-        shares = (
-            scale * jnp.where(odd, other, own),
-            (scale * jnp.where(odd, own, other)).T,
-            scale * filt_row.reshape(BASIS, per).T,
-        )
+        flags = jnp.stack([core, lax.axis_index("lon") // 2]).astype(jnp.int32)
+        shares = scaled(flags, every, mats, near, across, far, share[:1, chans:], per)
     back = adjoint_outer(
         gf_mid, mid_side, gf_end, end_side, *halos, band_adj, filt, cotangent, back
     )
-    return (out, back) + shares
+    return (out, back, *shares)
 
 
 def solution(mesh):

time: 130 us -> 128 us (0.985)
  Pallas kernels: 34.7 us -> 38.9 us
  other arithmetic: 6.32 us -> 2.56 us
  local copies, waits for them, and re-layouts: 11.7 us -> 9.89 us
    unnamed x62 -> x48, local copies, waits for them, and re-layouts: 7.64 us -> 4.61 us
    pallas_call x1, Pallas kernels: 11.1 us -> 13.9 us  [mixer_outer(): pl.pallas_call(functools.partial(outer_kernel, per), grid=(2,), in_specs=...]
    concatenate x4 -> x3, other arithmetic: 3.41 us -> 1.16 us  [beside(): return jnp.concatenate([rows, side], axis=1)]
    pallas_call x0 -> x1, Pallas kernels: none -> 1.53 us  [scaled(): pl.pallas_call(functools.partial(scale_kernel, per), in_specs=blocks_in,...]
    ppermute x4, waiting for transfers between devices: 18.1 us -> 19.5 us  [exchange_rows(): return (lax.ppermute(last, 'lat', up), lax.ppermute(first, 'lat', down))]
    ppermute x2, waiting for transfers between devices: 1.83 us -> 0.53 us  [exchange_columns(): right = lax.ppermute(first, 'lon', down)]
    slice x1, local copies, waits for them, and re-layouts: 0.07 us -> 1.37 us  [local(): gf_end[PAIR:]]
where the time goes in v3:
time: 128 us
  starting transfers between devices  45.7 us (36%)
  Pallas kernels  38.9 us (30%)
  waiting for transfers between devices  29.6 us (23%)
  local copies, waits for them, and re-layouts  9.89 us (8%)
  other arithmetic  2.56 us (2%)
    ppermute x4, starting transfers between devices, exchange_rows(): return (lax.ppermute(last, 'lat', up), lax.ppermute(first, 'lat', down))  22.8 us
    ppermute x4, waiting for transfers between devices, exchange_rows(): return (lax.ppermute(last, 'lat', up), lax.ppermute(first, 'lat', down))  19.5 us
    pallas_call x1, Pallas kernels, mixer_outer(): pl.pallas_call(functools.partial(outer_kernel, per), grid=(2,), in_specs=...  13.9 us
    pallas_call x1, Pallas kernels, mixer_inner(): pl.pallas_call(inner_kernel, grid=(2,), in_specs=[whole(x.shape), whole(s...  11.8 us
    all_to_all x1, starting transfers between devices, local(): spread = lax.all_to_all(part, 'lat', 0, 0)  9.92 us
    all_to_all x1, starting transfers between devices, local(): lax.all_to_all(jnp.broadcast_to(square, (bands * panels, 1, 128)), ('lat'...  6.57 us
    pallas_call x1, Pallas kernels, adjoint_outer(): pl.pallas_call(outer_adjoint, grid=(2,), in_specs=[blocks(PAIR, mid.shape...  5.64 us
    all_to_all x1, waiting for transfers between devices, local(): spread = lax.all_to_all(part, 'lat', 0, 0)  5.22 us
  transfers between devices with their start and end apart: 15, of which 8 were waited for; matrix products, arithmetic and copies ran while one was open for 4% of the time, Pallas kernels for 18%

profile of v3, /device:TPU:2, one launch (start us, length us, event | category | flops | bytes accessed | tf_op | source)
XLA Modules:
  0.0 127.8 jit_solution(10653483493697345026)
XLA Ops:
  0.7 0.9 fusion.1
  1.7 1.7 %collective-permute-start = (bf16[8,8,512]{2,1,0:T(8,128)(2,1)S(1)}, bf16[8,8,512]{2,1,0:T(8,128)(2,1)S(1)}, u32[]{:S(2)}, u32[]{:S(2)}) collective-permute-start(bf16[8,8,512]{2,1,0:T(8,128)(2,1)S(1)} %get-tuple-element.74), channel_id=1, source_target_pairs={{0,3},{1,0},{2,1},{3,2},{4,7},{5,4},{6,5},{7,6},{8,11},{9,8},{10,9... | collective-permute-start | bytes 196616 | tf_op jit(solution)/shard_map/input_halo/ppermute | solution.py:443
  3.4 1.3 fusion
  4.8 0.1 copy.25
  5.1 0.1 copy.28
  5.2 0.1 reshape.32
  5.5 5.2 %collective-permute-start.2 = (bf16[2,272,512]{2,1,0:T(8,128)(2,1)S(1)}, bf16[2,272,512]{2,1,0:T(8,128)(2,1)S(1)}, u32[]{:S(2)}, u32[]{:S(2)}) collective-permute-start(bf16[2,272,512]{2,1,0:T(8,128)(2,1)S(1)} %pad_maximum_fusion), channel_id=1, source_target_pairs={{0,4},{4,8},{8,12},{12,16},{16,20},{20,24},{24,28},{28,32},{32,36}... | collective-permute-start | bytes 1671176 | tf_op jit(solution)/shard_map/input_halo/ppermute | solution.py:455
  10.8 7.2 %collective-permute-start.3 = (bf16[2,272,512]{2,1,0:T(8,128)(2,1)S(1)}, bf16[2,272,512]{2,1,0:T(8,128)(2,1)S(1)}, u32[]{:S(2)}, u32[]{:S(2)}) collective-permute-start(bf16[2,272,512]{2,1,0:T(8,128)(2,1)S(1)} %pad_maximum_fusion.1), channel_id=1, source_target_pairs={{4,0},{8,4},{12,8},{16,12},{20,16},{24,20},{28,24},{32,28},{36,32}... | collective-permute-start | bytes 1671176 | tf_op jit(solution)/shard_map/input_halo/ppermute | solution.py:455
  18.0 0.1 copy.27
  18.2 0.1 reshape.31
  18.3 1.0 band_forward.1.band
  19.3 0.8 copy-done.6
  20.1 11.8 %mixer_inner.1 = (bf16[8,256,512]{2,1,0:T(8,128)(2,1)}, bf16[4,256,512]{2,1,0:T(8,128)(2,1)}, bf16[4,16,512]{2,1,0:T(8,128)(2,1)}, f32[512,512]{1,0:T(8,128)}, f32[512,512]{1,0:T(8,128)}, /*index=5*/f32[72,512]{1,0:T(8,128)}) custom-call(bf16[8,256,512]{2,1,0:T(8,128)(2,1)} %x.9, bf16[8,16,512]{2,1,0:T(8,128)(2,1)} %copy-done.17, ...), custom_call_target="tpu_custom_call" | custom-call | flops 5033164800 | bytes 5242880 | tf_op jit(solution)/shard_map/mixer_inner/pallas_call | solution.py:330
  31.9 1.0 band_adjoint.1.band
  32.9 2.4 %collective-permute-done.2.lo = bf16[2,272,512]{2,1,0:T(8,128)(2,1)S(1)} collective-permute-done((bf16[2,272,512]{2,1,0:T(8,128)(2,1)S(1)}, bf16[2,272,512]{2,1,0:T(8,128)(2,1)S(1)}, u32[]{:S(2)}, u32[]{:S(2)}) %collective-permute-start.2) | collective-permute-done | bytes 557088 | tf_op jit(solution)/shard_map/input_halo/ppermute | solution.py:455
  35.3 6.1 %collective-permute-done.3.hi = bf16[2,272,512]{2,1,0:T(8,128)(2,1)S(1)} collective-permute-done((bf16[2,272,512]{2,1,0:T(8,128)(2,1)S(1)}, bf16[2,272,512]{2,1,0:T(8,128)(2,1)S(1)}, u32[]{:S(2)}, u32[]{:S(2)}) %collective-permute-start.3) | collective-permute-done | bytes 557088 | tf_op jit(solution)/shard_map/input_halo/ppermute | solution.py:455
  41.4 0.8 copy-done.21
  42.2 13.9 %mixer_outer.1 = (bf16[8,256,512]{2,1,0:T(8,128)(2,1)}, bf16[4,256,512]{2,1,0:T(8,128)(2,1)}, bf16[4,16,512]{2,1,0:T(8,128)(2,1)}, f32[512,640]{1,0:T(8,128)}, bf16[512,640]{1,0:T(8,128)(2,1)}) custom-call(s32[1]{0:T(128)} %bitcast.odd, bf16[8,256,512]{2,1,0:T(8,128)(2,1)} %x.9, bf16[8,16,512]{2,1,0:T(8,128)(2,1)} %copy-done.17, ...), custom_call_target="tpu_custom_call", output_to_operand_aliasing={{0}: (10, {})} | custom-call | flops 5033164800 | bytes 5242880 | tf_op jit(solution)/shard_map/mixer_outer/pallas_call | solution.py:359
  56.1 0.8 constant_dynamic-update-slice_fusion.3
  57.0 0.2 collective-permute-start.5
  57.2 1.6 %collective-permute-start.4 = (bf16[8,8,512]{2,1,0:T(8,128)(2,1)S(1)}, bf16[8,8,512]{2,1,0:T(8,128)(2,1)S(1)}, u32[]{:S(2)}, u32[]{:S(2)}) collective-permute-start(bf16[8,8,512]{2,1,0:T(8,128)(2,1)S(1)} %get-tuple-element.82), channel_id=1, source_target_pairs={{0,3},{1,0},{2,1},{3,2},{4,7},{5,4},{6,5},{7,6},{8,11},{9,8},{10,9... | collective-permute-start | bytes 196616 | tf_op jit(solution)/shard_map/grad_halo/ppermute | solution.py:443
  58.8 1.4 %fusion.2 = (bf16[2,256,512]{2,1,0:T(8,128)(2,1)S(1)}, bf16[2,256,512]{2,1,0:T(8,128)(2,1)S(1)}) fusion(bf16[4,256,512]{2,1,0:T(8,128)(2,1)} %get-tuple-element.42.end), kind=kLoop, calls=%fused_computation.19 | loop fusion | bytes 2097152 | tf_op jit(solution)/shard_map/grad_halo/slice | solution.py:565
  60.2 0.5 collective-permute-done.4
  60.8 0.3 collective-permute-done.6
  61.1 0.1 add_bitcast_fusion
  61.2 0.2 select_convert_fusion
  61.5 0.6 collective-permute-start.7
  62.1 1.1 pad_maximum_fusion.2
  63.2 0.6 copy-done
  63.8 3.8 %adjoint_inner.1.partial_out = bf16[8,256,512]{2,1,0:T(8,128)(2,1)} custom-call(bf16[4,256,512]{2,1,0:T(8,128)(2,1)S(1)} %copy-done.3, bf16[4,16,512]{2,1,0:T(8,128)(2,1)S(1)} %get-tuple-element.80.mid_side, bf16[4,256,512]{2,1,0:T(8,128)(2,1)S(1)} %copy-done, bf16[4,16,512]{2,1,0:T(8,128)(2,1)S(1)} %get-tuple-element.79.end_side, ...), custom_call_target="tpu_custom_call" | custom-call | flops 1811939328 | bytes 3145728 | tf_op jit(solution)/shard_map/adjoint_inner/pallas_call | solution.py:399
  67.6 4.0 %collective-permute-done.7 = bf16[64,4,640]{2,1,0:T(4,128)(2,1)S(1)} collective-permute-done((bf16[64,4,640]{2,1,0:T(4,128)(2,1)S(1)}, bf16[64,4,640]{2,1,0:T(4,128)(2,1)S(1)}, u32[]{:S(2)}, u32[]{:S(2)}) %collective-permute-start.7) | collective-permute-done | bytes 327712 | tf_op jit(solution)/shard_map/reduce/ppermute | solution.py:459
  71.6 1.0 add_convert_fusion
  72.5 9.9 %all-to-all-start = ((bf16[64,4,640]{2,1,0:T(4,128)(2,1)}), bf16[64,4,640]{2,1,0:T(4,128)(2,1)S(1)}, u32[]{:S(2)}, u32[]{:S(2)}) async-start(bf16[64,4,640]{2,1,0:T(4,128)(2,1)} %add_convert_fusion), calls=%async_computation | async-start | bytes 655360 | tf_op jit(solution)/shard_map/reduce/all_to_all | solution.py:576
  82.5 4.9 %collective-permute-start.8 = (bf16[2,272,512]{2,1,0:T(8,128)(2,1)S(1)}, bf16[2,272,512]{2,1,0:T(8,128)(2,1)S(1)}, u32[]{:S(2)}, u32[]{:S(2)}) collective-permute-start(bf16[2,272,512]{2,1,0:T(8,128)(2,1)S(1)} %copy-done.14), channel_id=1, source_target_pairs={{0,4},{4,8},{8,12},{12,16},{16,20},{20,24},{24,28},{28,32},{32,36}... | collective-permute-start | bytes 1671176 | tf_op jit(solution)/shard_map/reduce/ppermute | solution.py:455
  87.4 5.5 %collective-permute-start.9 = (bf16[2,272,512]{2,1,0:T(8,128)(2,1)S(1)}, bf16[2,272,512]{2,1,0:T(8,128)(2,1)S(1)}, u32[]{:S(2)}, u32[]{:S(2)}) collective-permute-start(bf16[2,272,512]{2,1,0:T(8,128)(2,1)S(1)} %copy-done.13), channel_id=1, source_target_pairs={{4,0},{8,4},{12,8},{16,12},{20,16},{24,20},{28,24},{32,28},{36,32}... | collective-permute-start | bytes 1671176 | tf_op jit(solution)/shard_map/reduce/ppermute | solution.py:455
  92.8 5.2 %all-to-all-done.spread = bf16[64,4,640]{2,1,0:T(4,128)(2,1)S(1)} async-done(((bf16[64,4,640]{2,1,0:T(4,128)(2,1)}), bf16[64,4,640]{2,1,0:T(4,128)(2,1)S(1)}, u32[]{:S(2)}, u32[]{:S(2)}) %all-to-all-start) | async-done | bytes 327712 | tf_op jit(solution)/shard_map/reduce/all_to_all | solution.py:576
  98.1 0.3 sum_shares.1
  98.4 0.7 broadcast_in_dim.3
  99.1 6.6 %all-to-all-start.1 = ((f32[256,1,128]{2,1,0:T(1,128)}), f32[256,1,128]{2,1,0:T(1,128)S(1)}, u32[]{:S(2)}, u32[]{:S(2)}) async-start(f32[256,1,128]{2,1,0:T(1,128)} %broadcast_in_dim.3), calls=%async_computation.1 | async-start | bytes 262144 | tf_op jit(solution)/shard_map/norm/all_to_all | solution.py:581
  105.8 1.3 %collective-permute-start.12 = (f32[4,512]{1,0:T(4,128)S(1)}, f32[4,512]{1,0:T(4,128)S(1)}, u32[]{:S(2)}, u32[]{:S(2)}) collective-permute-start(f32[4,512]{1,0:T(4,128)S(1)} %slice.74.mats), channel_id=1, source_target_pairs={{0,3},{1,2},{2,1},{3,0},{4,7},{5,6},{6,5},{7,4},{8,11},{9,10},{10,... | collective-permute-start | bytes 24584 | tf_op jit(solution)/shard_map/norm/ppermute | solution.py:459
  107.1 0.4 collective-permute-start.11
  107.4 0.5 collective-permute-start.10
  107.9 6.7 %collective-permute-done.8.lo = bf16[2,272,512]{2,1,0:T(8,128)(2,1)S(1)} collective-permute-done((bf16[2,272,512]{2,1,0:T(8,128)(2,1)S(1)}, bf16[2,272,512]{2,1,0:T(8,128)(2,1)S(1)}, u32[]{:S(2)}, u32[]{:S(2)}) %collective-permute-start.8) | collective-permute-done | bytes 557088 | tf_op jit(solution)/shard_map/reduce/ppermute | solution.py:455
  114.7 4.3 %collective-permute-done.9.hi = bf16[2,272,512]{2,1,0:T(8,128)(2,1)S(1)} collective-permute-done((bf16[2,272,512]{2,1,0:T(8,128)(2,1)S(1)}, bf16[2,272,512]{2,1,0:T(8,128)(2,1)S(1)}, u32[]{:S(2)}, u32[]{:S(2)}) %collective-permute-start.9) | collective-permute-done | bytes 557088 | tf_op jit(solution)/shard_map/reduce/ppermute | solution.py:455
  119.0 0.8 copy-done.12
  119.8 5.6 %adjoint_outer.1 = bf16[8,256,512]{2,1,0:T(8,128)(2,1)} custom-call(bf16[4,256,512]{2,1,0:T(8,128)(2,1)} %get-tuple-element.39.mid, bf16[4,16,512]{2,1,0:T(8,128)(2,1)} %copy-done.5, bf16[4,256,512]{2,1,0:T(8,128)(2,1)} %get-tuple-element.42.end, bf16[4,16,512]{2,1,0:T(8,128)(2,1)} %copy-done.4, ...), custom_call_target="tpu_custom_call", output_to_operand_aliasing={{}: (9, {})} | custom-call | flops 1811939328 | bytes 3145728 | tf_op jit(solution)/shard_map/adjoint_outer/pallas_call | solution.py:419
  125.5 1.5 %scaled.1 = (f32[8,512]{1,0:T(8,128)}, f32[512,8]{1,0:T(8,128)S(1)}, f32[8,9]{1,0:T(8,128)}) custom-call(s32[2]{0:T(128)S(1)} %pad_add_fusion.flags, f32[256,1,128]{2,1,0:T(1,128)S(1)} %all-to-all-done.1.every, f32[4,512]{1,0:T(4,128)S(1)} %slice.74.mats, f32[4,512]{1,0:T(4,128)S(1)} %collective-permute-done.10.near, ...), custom_call_target="tpu_custom_call" | custom-call | tf_op jit(solution)/shard_map/norm/scaled/pallas_call | solution.py:509
  127.1 0.7 copy.26
  (67 shorter events, 0.8 us)
Async XLA Ops:
  0.6 4.1 %copy-start.19 = (s32[512,5]{0,1:T(8,128)S(1)}, s32[512,5]{0,1:T(8,128)}, u32[]{:S(2)}) copy-start(s32[512,5]{0,1:T(8,128)} %param.14) | copy-start | bytes 30724
  0.6 4.3 %copy-start.15 = (s32[512,5,9]{0,1,2:T(8,128)S(1)}, s32[512,5,9]{0,1,2:T(8,128)}, u32[]{:S(2)}) copy-start(s32[512,5,9]{0,1,2:T(8,128)} %param.13) | copy-start | bytes 276484
  1.6 3.8 %collective-permute-start.1 = (bf16[8,8,512]{2,1,0:T(8,128)(2,1)S(1)}, bf16[8,8,512]{2,1,0:T(8,128)(2,1)S(1)}, u32[]{:S(2)}, u32[]{:S(2)}) collective-permute-start(bf16[8,8,512]{2,1,0:T(8,128)(2,1)S(1)} %get-tuple-element.73), channel_id=1, source_target_pairs={{0,1},{1,2},{2,3},{3,0},{4,5},{5,6},{6,7},{7,4},{8,9},{9,10},{10,1... | collective-permute-start | bytes 196616 | tf_op jit(solution)/shard_map/input_halo/ppermute | solution.py:444
  1.7 3.7 %collective-permute-start = (bf16[8,8,512]{2,1,0:T(8,128)(2,1)S(1)}, bf16[8,8,512]{2,1,0:T(8,128)(2,1)S(1)}, u32[]{:S(2)}, u32[]{:S(2)}) collective-permute-start(bf16[8,8,512]{2,1,0:T(8,128)(2,1)S(1)} %get-tuple-element.74), channel_id=1, source_target_pairs={{0,3},{1,0},{2,1},{3,2},{4,7},{5,4},{6,5},{7,6},{8,11},{9,8},{10,9... | collective-permute-start | bytes 196616 | tf_op jit(solution)/shard_map/input_halo/ppermute | solution.py:443
  5.3 12.6 %copy-start.16 = (f32[512,5,9]{0,1,2:T(8,128)S(1)}, f32[512,5,9]{0,1,2:T(8,128)}, u32[]{:S(2)}) copy-start(f32[512,5,9]{0,1,2:T(8,128)} %param.12) | copy-start | bytes 276484
  5.4 12.8 %copy-start.17 = (bf16[8,16,512]{2,1,0:T(8,128)(2,1)}, bf16[8,16,512]{2,1,0:T(8,128)(2,1)S(1)}, u32[]{:S(2)}) copy-start(bf16[8,16,512]{2,1,0:T(8,128)(2,1)S(1)} %constant_dynamic-update-slice_fusion.side) | copy-start | bytes 393220
  5.4 12.9 %copy-start.8 = (bf16[60,2048]{1,0:T(8,128)(2,1)S(1)}, bf16[60,2048]{1,0:T(8,128)(2,1)}, u32[]{:S(2)}) copy-start(bf16[60,2048]{1,0:T(8,128)(2,1)} %constant.47.clone.pick) | copy-start | bytes 737284
  5.5 29.8 %collective-permute-start.2 = (bf16[2,272,512]{2,1,0:T(8,128)(2,1)S(1)}, bf16[2,272,512]{2,1,0:T(8,128)(2,1)S(1)}, u32[]{:S(2)}, u32[]{:S(2)}) collective-permute-start(bf16[2,272,512]{2,1,0:T(8,128)(2,1)S(1)} %pad_maximum_fusion), channel_id=1, source_target_pairs={{0,4},{4,8},{8,12},{12,16},{16,20},{20,24},{24,28},{28,32},{32,36}... | collective-permute-start | bytes 1671176 | tf_op jit(solution)/shard_map/input_halo/ppermute | solution.py:455
  10.8 30.6 %collective-permute-start.3 = (bf16[2,272,512]{2,1,0:T(8,128)(2,1)S(1)}, bf16[2,272,512]{2,1,0:T(8,128)(2,1)S(1)}, u32[]{:S(2)}, u32[]{:S(2)}) collective-permute-start(bf16[2,272,512]{2,1,0:T(8,128)(2,1)S(1)} %pad_maximum_fusion.1), channel_id=1, source_target_pairs={{4,0},{8,4},{12,8},{16,12},{20,16},{24,20},{28,24},{32,28},{36,32}... | collective-permute-start | bytes 1671176 | tf_op jit(solution)/shard_map/input_halo/ppermute | solution.py:455
  19.3 0.8 copy-start.6
  20.1 11.8 %copy-start.7 = (bf16[60,2048]{1,0:T(8,128)(2,1)S(1)}, bf16[60,2048]{1,0:T(8,128)(2,1)}, u32[]{:S(2)}) copy-start(bf16[60,2048]{1,0:T(8,128)(2,1)} %constant.48.clone.pick) | copy-start | bytes 737284
  32.9 30.3 %copy-start.2 = (bf16[4,288,192]{2,1,0:T(8,128)(2,1)}, bf16[4,288,192]{2,1,0:T(8,128)(2,1)S(1)}, u32[]{:S(2)}) copy-start(bf16[4,288,192]{2,1,0:T(8,128)(2,1)S(1)} %band_adjoint.1.band) | copy-start | bytes 1327108
  35.3 6.1 %copy-start.20 = (bf16[2,272,512]{2,1,0:T(8,128)(2,1)}, bf16[2,272,512]{2,1,0:T(8,128)(2,1)S(1)}, u32[]{:S(2)}) copy-start(bf16[2,272,512]{2,1,0:T(8,128)(2,1)S(1)} %collective-permute-done.2.lo) | copy-start | bytes 1671172
  41.4 0.8 copy-start.21
  42.2 14.8 %copy-start.18 = (bf16[4,16,512]{2,1,0:T(8,128)(2,1)S(1)}, bf16[4,16,512]{2,1,0:T(8,128)(2,1)}, u32[]{:S(2)}) copy-start(bf16[4,16,512]{2,1,0:T(8,128)(2,1)} %get-tuple-element.41) | copy-start | bytes 196612
  57.0 3.8 %collective-permute-start.5 = (bf16[8,8,512]{2,1,0:T(8,128)(2,1)S(1)}, bf16[8,8,512]{2,1,0:T(8,128)(2,1)S(1)}, u32[]{:S(2)}, u32[]{:S(2)}) collective-permute-start(bf16[8,8,512]{2,1,0:T(8,128)(2,1)S(1)} %get-tuple-element.81), channel_id=1, source_target_pairs={{0,1},{1,2},{2,3},{3,0},{4,5},{5,6},{6,7},{7,4},{8,9},{9,10},{10,1... | collective-permute-start | bytes 196616 | tf_op jit(solution)/shard_map/grad_halo/ppermute | solution.py:444
  57.2 3.5 %collective-permute-start.4 = (bf16[8,8,512]{2,1,0:T(8,128)(2,1)S(1)}, bf16[8,8,512]{2,1,0:T(8,128)(2,1)S(1)}, u32[]{:S(2)}, u32[]{:S(2)}) collective-permute-start(bf16[8,8,512]{2,1,0:T(8,128)(2,1)S(1)} %get-tuple-element.82), channel_id=1, source_target_pairs={{0,3},{1,0},{2,1},{3,2},{4,7},{5,4},{6,5},{7,6},{8,11},{9,8},{10,9... | collective-permute-start | bytes 196616 | tf_op jit(solution)/shard_map/grad_halo/ppermute | solution.py:443
  58.8 2.3 %collective-permute-start.6 = (bf16[512,640]{1,0:T(8,128)(2,1)}, bf16[512,640]{1,0:T(8,128)(2,1)S(1)}, u32[]{:S(2)}, u32[]{:S(2)}) collective-permute-start(bf16[512,640]{1,0:T(8,128)(2,1)} %get-tuple-element.44), channel_id=1, source_target_pairs={{0,1},{1,0},{2,3},{3,2},{4,5},{5,4},{6,7},{7,6},{8,9},{9,8},{10,11... | collective-permute-start | bytes 1966088 | tf_op jit(solution)/shard_map/reduce/ppermute | solution.py:459
  58.8 2.3 %copy-start.10 = (f32[512,640]{1,0:T(8,128)S(1)}, f32[512,640]{1,0:T(8,128)}, u32[]{:S(2)}) copy-start(f32[512,640]{1,0:T(8,128)} %get-tuple-element.43) | copy-start | bytes 3932164
  60.8 2.4 %copy-start.4 = (bf16[4,16,512]{2,1,0:T(8,128)(2,1)}, bf16[4,16,512]{2,1,0:T(8,128)(2,1)S(1)}, u32[]{:S(2)}) copy-start(bf16[4,16,512]{2,1,0:T(8,128)(2,1)S(1)} %get-tuple-element.79.end_side) | copy-start | bytes 196612
  60.8 2.4 %copy-start.5 = (bf16[4,16,512]{2,1,0:T(8,128)(2,1)}, bf16[4,16,512]{2,1,0:T(8,128)(2,1)S(1)}, u32[]{:S(2)}) copy-start(bf16[4,16,512]{2,1,0:T(8,128)(2,1)S(1)} %get-tuple-element.80.mid_side) | copy-start | bytes 196612
  61.1 2.1 %copy-start.3 = (bf16[4,256,512]{2,1,0:T(8,128)(2,1)S(1)}, bf16[4,256,512]{2,1,0:T(8,128)(2,1)}, u32[]{:S(2)}) copy-start(bf16[4,256,512]{2,1,0:T(8,128)(2,1)} %get-tuple-element.39.mid) | copy-start | bytes 3145732
  61.2 2.0 %copy-start.1 = (bf16[8,256,512]{2,1,0:T(8,128)(2,1)S(1)}, bf16[8,256,512]{2,1,0:T(8,128)(2,1)}, u32[]{:S(2)}) copy-start(bf16[8,256,512]{2,1,0:T(8,128)(2,1)} %cot.7) | copy-start | bytes 6291460
  61.5 2.3 %copy-start = (bf16[4,256,512]{2,1,0:T(8,128)(2,1)S(1)}, bf16[4,256,512]{2,1,0:T(8,128)(2,1)}, u32[]{:S(2)}) copy-start(bf16[4,256,512]{2,1,0:T(8,128)(2,1)} %get-tuple-element.42.end) | copy-start | bytes 3145732
  61.5 2.3 %copy-start.9 = (f32[512,9]{0,1:T(8,128)S(1)}, f32[512,9]{0,1:T(8,128)}, u32[]{:S(2)}) copy-start(f32[512,9]{0,1:T(8,128)} %param.15) | copy-start | bytes 55300
  61.5 10.1 %collective-permute-start.7 = (bf16[64,4,640]{2,1,0:T(4,128)(2,1)S(1)}, bf16[64,4,640]{2,1,0:T(4,128)(2,1)S(1)}, u32[]{:S(2)}, u32[]{:S(2)}) collective-permute-start(bf16[64,4,640]{2,1,0:T(4,128)(2,1)S(1)} %select_convert_fusion), channel_id=1, source_target_pairs={{0,2},{1,3},{2,0},{3,1},{4,6},{5,7},{6,4},{7,5},{8,10},{9,11},{10,... | collective-permute-start | bytes 983048 | tf_op jit(solution)/shard_map/reduce/ppermute | solution.py:459
  67.6 14.9 %copy-start.14 = (bf16[2,272,512]{2,1,0:T(8,128)(2,1)S(1)}, bf16[2,272,512]{2,1,0:T(8,128)(2,1)}, u32[]{:S(2)}) copy-start(bf16[2,272,512]{2,1,0:T(8,128)(2,1)} %get-tuple-element.48) | copy-start | bytes 1671172
  67.6 19.8 %copy-start.13 = (bf16[2,272,512]{2,1,0:T(8,128)(2,1)S(1)}, bf16[2,272,512]{2,1,0:T(8,128)(2,1)}, u32[]{:S(2)}) copy-start(bf16[2,272,512]{2,1,0:T(8,128)(2,1)} %get-tuple-element.49) | copy-start | bytes 1671172
  72.5 25.5 %all-to-all-start = ((bf16[64,4,640]{2,1,0:T(4,128)(2,1)}), bf16[64,4,640]{2,1,0:T(4,128)(2,1)S(1)}, u32[]{:S(2)}, u32[]{:S(2)}) async-start(bf16[64,4,640]{2,1,0:T(4,128)(2,1)} %add_convert_fusion), calls=%async_computation | async-start | bytes 655360 | tf_op jit(solution)/shard_map/reduce/all_to_all | solution.py:576
  82.5 32.2 %collective-permute-start.8 = (bf16[2,272,512]{2,1,0:T(8,128)(2,1)S(1)}, bf16[2,272,512]{2,1,0:T(8,128)(2,1)S(1)}, u32[]{:S(2)}, u32[]{:S(2)}) collective-permute-start(bf16[2,272,512]{2,1,0:T(8,128)(2,1)S(1)} %copy-done.14), channel_id=1, source_target_pairs={{0,4},{4,8},{8,12},{12,16},{16,20},{20,24},{24,28},{28,32},{32,36}... | collective-permute-start | bytes 1671176 | tf_op jit(solution)/shard_map/reduce/ppermute | solution.py:455
  87.4 31.7 %collective-permute-start.9 = (bf16[2,272,512]{2,1,0:T(8,128)(2,1)S(1)}, bf16[2,272,512]{2,1,0:T(8,128)(2,1)S(1)}, u32[]{:S(2)}, u32[]{:S(2)}) collective-permute-start(bf16[2,272,512]{2,1,0:T(8,128)(2,1)S(1)} %copy-done.13), channel_id=1, source_target_pairs={{4,0},{8,4},{12,8},{16,12},{20,16},{24,20},{28,24},{32,28},{36,32}... | collective-permute-start | bytes 1671176 | tf_op jit(solution)/shard_map/reduce/ppermute | solution.py:455
  99.1 26.4 %all-to-all-start.1 = ((f32[256,1,128]{2,1,0:T(1,128)}), f32[256,1,128]{2,1,0:T(1,128)S(1)}, u32[]{:S(2)}, u32[]{:S(2)}) async-start(f32[256,1,128]{2,1,0:T(1,128)} %broadcast_in_dim.3), calls=%async_computation.1 | async-start | bytes 262144 | tf_op jit(solution)/shard_map/norm/all_to_all | solution.py:581
  105.8 19.7 %collective-permute-start.12 = (f32[4,512]{1,0:T(4,128)S(1)}, f32[4,512]{1,0:T(4,128)S(1)}, u32[]{:S(2)}, u32[]{:S(2)}) collective-permute-start(f32[4,512]{1,0:T(4,128)S(1)} %slice.74.mats), channel_id=1, source_target_pairs={{0,3},{1,2},{2,1},{3,0},{4,7},{5,6},{6,5},{7,4},{8,11},{9,10},{10,... | collective-permute-start | bytes 24584 | tf_op jit(solution)/shard_map/norm/ppermute | solution.py:459
  107.1 18.4 %collective-permute-start.11 = (f32[4,512]{1,0:T(4,128)S(1)}, f32[4,512]{1,0:T(4,128)S(1)}, u32[]{:S(2)}, u32[]{:S(2)}) collective-permute-start(f32[4,512]{1,0:T(4,128)S(1)} %slice.74.mats), channel_id=1, source_target_pairs={{0,1},{1,0},{2,3},{3,2},{4,5},{5,4},{6,7},{7,6},{8,9},{9,8},{10,11... | collective-permute-start | bytes 24584 | tf_op jit(solution)/shard_map/norm/ppermute | solution.py:459
  107.4 18.0 %collective-permute-start.10 = (f32[4,512]{1,0:T(4,128)S(1)}, f32[4,512]{1,0:T(4,128)S(1)}, u32[]{:S(2)}, u32[]{:S(2)}) collective-permute-start(f32[4,512]{1,0:T(4,128)S(1)} %slice.74.mats), channel_id=1, source_target_pairs={{0,2},{1,3},{2,0},{3,1},{4,6},{5,7},{6,4},{7,5},{8,10},{9,11},{10,... | collective-permute-start | bytes 24584 | tf_op jit(solution)/shard_map/norm/ppermute | solution.py:459
  114.7 4.3 %copy-start.11 = (bf16[2,272,512]{2,1,0:T(8,128)(2,1)}, bf16[2,272,512]{2,1,0:T(8,128)(2,1)S(1)}, u32[]{:S(2)}) copy-start(bf16[2,272,512]{2,1,0:T(8,128)(2,1)S(1)} %collective-permute-done.8.lo) | copy-start | bytes 1671172
  119.0 0.8 copy-start.12

commit v4 on v3

--- a/solution.py
+++ b/solution.py
@@ -563,7 +563,6 @@
         gside = exchange_columns(edge[:, :HALF], edge[:, HALF:], panels)
         end_side, mid_side = gside[: 2 * PAIR], gside[2 * PAIR :]
         ends = beside(gf_end[:PAIR], end_side[:PAIR]), beside(gf_end[PAIR:], end_side[PAIR:])
-    back = adjoint_inner(gf_mid, mid_side, gf_end, end_side, band_adj, filt, cotangent)
     with jax.named_scope("reduce"):
         lanes, half = chans + 128, per // 2
         total = (keep + swap(give, panels, 1).astype(F32)).reshape(bands, per, lanes)
@@ -571,9 +570,12 @@
         kept = jnp.where(upper, total[:, half:], total[:, :half])
         give = jnp.where(upper, total[:, :half], total[:, half:]).astype(BF)
         part = (kept + swap(give, panels, 2).astype(F32)).astype(BF)
-        part, back, ends = lax.optimization_barrier((part, back, ends))
+        part, ends = lax.optimization_barrier((part, ends))
         halos = exchange_rows(*ends, bands)
         spread = lax.all_to_all(part, "lat", 0, 0)
+        halos, gf_mid = lax.optimization_barrier((halos, gf_mid))
+        back = adjoint_inner(gf_mid, mid_side, gf_end, end_side, band_adj, filt, cotangent)
+        spread, back = lax.optimization_barrier((spread, back))
     with jax.named_scope("norm"):
         share, square = sum_shares(spread, chans, BASIS * per, panels)
         mats = share[:, :chans]

time: 128 us -> 143 us (1.12); the launches traced: 128 us -> 141 us
  waiting for transfers between devices: 29.6 us -> 36.9 us
  local copies, waits for them, and re-layouts: 9.89 us -> 13.6 us
  starting transfers between devices: 45.7 us -> 48.1 us
    all_to_all x1, waiting for transfers between devices: 5.22 us -> 0.01 us  [local(): spread = lax.all_to_all(part, 'lat', 0, 0)]
    ppermute x5, waiting for transfers between devices: 4.31 us -> 8.71 us  [swap(): return lax.ppermute(a, 'lon', [(i, i ^ bits) for i in range(count)])]
    all_to_all x1, waiting for transfers between devices: 0.01 us -> 4.09 us  [local(): lax.all_to_all(jnp.broadcast_to(square, (bands * panels, 1, 128)), ('lat'...]
    ppermute x4, waiting for transfers between devices: 19.5 us -> 23.4 us  [exchange_rows(): return (lax.ppermute(last, 'lat', up), lax.ppermute(first, 'lat', down))]
    all_to_all x1, starting transfers between devices: 6.57 us -> 10.4 us  [local(): lax.all_to_all(jnp.broadcast_to(square, (bands * panels, 1, 128)), ('lat'...]
    unnamed x48 -> x42, local copies, waits for them, and re-layouts: 4.61 us -> 7.62 us
    all_to_all x1, starting transfers between devices: 9.92 us -> 8.27 us  [local(): spread = lax.all_to_all(part, 'lat', 0, 0)]
  transfers between devices with their start and end apart: 15 -> 15, of which waited for: 8 -> 7; matrix products, arithmetic and copies ran while one was open for 4% -> 4% of each run, Pallas kernels for 18% -> 16%
where the time goes in v4:
time: 143 us; the launch traced here: 141 us
  starting transfers between devices  48.1 us (34%)
  Pallas kernels  38.9 us (27%)
  waiting for transfers between devices  36.9 us (26%)
  local copies, waits for them, and re-layouts  13.6 us (10%)
  other arithmetic  2.56 us (2%)
    ppermute x4, waiting for transfers between devices, exchange_rows(): return (lax.ppermute(last, 'lat', up), lax.ppermute(first, 'lat', down))  23.4 us
    ppermute x4, starting transfers between devices, exchange_rows(): return (lax.ppermute(last, 'lat', up), lax.ppermute(first, 'lat', down))  22.9 us
    pallas_call x1, Pallas kernels, mixer_outer(): pl.pallas_call(functools.partial(outer_kernel, per), grid=(2,), in_specs=...  13.9 us
    pallas_call x1, Pallas kernels, mixer_inner(): pl.pallas_call(inner_kernel, grid=(2,), in_specs=[whole(x.shape), whole(s...  11.8 us
    all_to_all x1, starting transfers between devices, local(): lax.all_to_all(jnp.broadcast_to(square, (bands * panels, 1, 128)), ('lat'...  10.4 us
    ppermute x5, waiting for transfers between devices, swap(): return lax.ppermute(a, 'lon', [(i, i ^ bits) for i in range(count)])  8.71 us
    all_to_all x1, starting transfers between devices, local(): spread = lax.all_to_all(part, 'lat', 0, 0)  8.27 us
    unnamed x42, local copies, waits for them, and re-layouts  7.62 us
  transfers between devices with their start and end apart: 15, of which 7 were waited for; matrix products, arithmetic and copies ran while one was open for 4% of the time, Pallas kernels for 16%

profile of v4, /device:TPU:2, one launch (start us, length us, event | category | flops | bytes accessed | tf_op | source)
XLA Modules:
  0.0 141.1 jit_solution(7661089769126922677)
XLA Ops:
  0.7 0.9 fusion.1
  1.7 1.7 %collective-permute-start = (bf16[8,8,512]{2,1,0:T(8,128)(2,1)S(1)}, bf16[8,8,512]{2,1,0:T(8,128)(2,1)S(1)}, u32[]{:S(2)}, u32[]{:S(2)}) collective-permute-start(bf16[8,8,512]{2,1,0:T(8,128)(2,1)S(1)} %get-tuple-element.82), channel_id=1, source_target_pairs={{0,3},{1,0},{2,1},{3,2},{4,7},{5,4},{6,5},{7,6},{8,11},{9,8},{10,9... | collective-permute-start | bytes 196616 | tf_op jit(solution)/shard_map/input_halo/ppermute | solution.py:443
  3.4 1.3 fusion
  5.1 0.1 copy.28
  5.5 5.2 %collective-permute-start.2 = (bf16[2,272,512]{2,1,0:T(8,128)(2,1)S(1)}, bf16[2,272,512]{2,1,0:T(8,128)(2,1)S(1)}, u32[]{:S(2)}, u32[]{:S(2)}) collective-permute-start(bf16[2,272,512]{2,1,0:T(8,128)(2,1)S(1)} %pad_maximum_fusion), channel_id=1, source_target_pairs={{0,4},{4,8},{8,12},{12,16},{16,20},{20,24},{24,28},{28,32},{32,36}... | collective-permute-start | bytes 1671176 | tf_op jit(solution)/shard_map/input_halo/ppermute | solution.py:455
  10.8 7.2 %collective-permute-start.3 = (bf16[2,272,512]{2,1,0:T(8,128)(2,1)S(1)}, bf16[2,272,512]{2,1,0:T(8,128)(2,1)S(1)}, u32[]{:S(2)}, u32[]{:S(2)}) collective-permute-start(bf16[2,272,512]{2,1,0:T(8,128)(2,1)S(1)} %pad_maximum_fusion.1), channel_id=1, source_target_pairs={{4,0},{8,4},{12,8},{16,12},{20,16},{24,20},{28,24},{32,28},{36,32}... | collective-permute-start | bytes 1671176 | tf_op jit(solution)/shard_map/input_halo/ppermute | solution.py:455
  18.0 0.1 copy.27
  18.3 1.0 band_forward.1.band
  19.3 0.8 copy-done.6
  20.1 11.8 %mixer_inner.1 = (bf16[8,256,512]{2,1,0:T(8,128)(2,1)}, bf16[4,256,512]{2,1,0:T(8,128)(2,1)}, bf16[4,16,512]{2,1,0:T(8,128)(2,1)}, f32[512,512]{1,0:T(8,128)}, f32[512,512]{1,0:T(8,128)}, /*index=5*/f32[72,512]{1,0:T(8,128)}) custom-call(bf16[8,256,512]{2,1,0:T(8,128)(2,1)} %x.9, bf16[8,16,512]{2,1,0:T(8,128)(2,1)} %copy-done.14, ...), custom_call_target="tpu_custom_call" | custom-call | flops 5033164800 | bytes 5242880 | tf_op jit(solution)/shard_map/mixer_inner/pallas_call | solution.py:330
  31.9 3.4 %collective-permute-done.2.lo = bf16[2,272,512]{2,1,0:T(8,128)(2,1)S(1)} collective-permute-done((bf16[2,272,512]{2,1,0:T(8,128)(2,1)S(1)}, bf16[2,272,512]{2,1,0:T(8,128)(2,1)S(1)}, u32[]{:S(2)}, u32[]{:S(2)}) %collective-permute-start.2) | collective-permute-done | bytes 557088 | tf_op jit(solution)/shard_map/input_halo/ppermute | solution.py:455
  35.3 6.1 %collective-permute-done.3.hi = bf16[2,272,512]{2,1,0:T(8,128)(2,1)S(1)} collective-permute-done((bf16[2,272,512]{2,1,0:T(8,128)(2,1)S(1)}, bf16[2,272,512]{2,1,0:T(8,128)(2,1)S(1)}, u32[]{:S(2)}, u32[]{:S(2)}) %collective-permute-start.3) | collective-permute-done | bytes 557088 | tf_op jit(solution)/shard_map/input_halo/ppermute | solution.py:455
  41.4 0.8 copy-done.18
  42.2 13.9 %mixer_outer.1 = (bf16[8,256,512]{2,1,0:T(8,128)(2,1)}, bf16[4,256,512]{2,1,0:T(8,128)(2,1)}, bf16[4,16,512]{2,1,0:T(8,128)(2,1)}, f32[512,640]{1,0:T(8,128)}, bf16[512,640]{1,0:T(8,128)(2,1)}) custom-call(s32[1]{0:T(128)} %bitcast.odd, bf16[8,256,512]{2,1,0:T(8,128)(2,1)} %x.9, bf16[8,16,512]{2,1,0:T(8,128)(2,1)} %copy-done.14, ...), custom_call_target="tpu_custom_call", output_to_operand_aliasing={{0}: (10, {})} | custom-call | flops 5033164800 | bytes 5242880 | tf_op jit(solution)/shard_map/mixer_outer/pallas_call | solution.py:359
  56.1 0.8 constant_dynamic-update-slice_fusion.3
  57.0 0.1 collective-permute-start.4
  57.1 0.5 collective-permute-start.7
  57.6 1.4 collective-permute-start.6
  59.0 1.3 fusion.2
  60.2 0.6 collective-permute-done.6
  61.1 0.2 select_convert_fusion
  61.3 0.6 collective-permute-start.5
  61.9 1.1 pad_maximum_fusion.2
  63.0 8.7 %collective-permute-done.5 = bf16[64,4,640]{2,1,0:T(4,128)(2,1)S(1)} collective-permute-done((bf16[64,4,640]{2,1,0:T(4,128)(2,1)S(1)}, bf16[64,4,640]{2,1,0:T(4,128)(2,1)S(1)}, u32[]{:S(2)}, u32[]{:S(2)}) %collective-permute-start.5) | collective-permute-done | bytes 327712 | tf_op jit(solution)/shard_map/reduce/ppermute | solution.py:459
  71.7 1.0 add_convert_fusion
  72.7 2.0 %collective-permute-start.8 = (bf16[2,272,512]{2,1,0:T(8,128)(2,1)}, bf16[2,272,512]{2,1,0:T(8,128)(2,1)}, u32[]{:S(2)}, u32[]{:S(2)}) collective-permute-start(bf16[2,272,512]{2,1,0:T(8,128)(2,1)} %get-tuple-element.48), channel_id=1, source_target_pairs={{0,4},{4,8},{8,12},{12,16},{16,20},{20,24},{24,28},{28,32},{32,36}... | collective-permute-start | bytes 1671176 | tf_op jit(solution)/shard_map/reduce/ppermute | solution.py:455
  74.7 8.4 %collective-permute-start.9 = (bf16[2,272,512]{2,1,0:T(8,128)(2,1)}, bf16[2,272,512]{2,1,0:T(8,128)(2,1)}, u32[]{:S(2)}, u32[]{:S(2)}) collective-permute-start(bf16[2,272,512]{2,1,0:T(8,128)(2,1)} %get-tuple-element.49), channel_id=1, source_target_pairs={{4,0},{8,4},{12,8},{16,12},{20,16},{24,20},{28,24},{32,28},{36,32}... | collective-permute-start | bytes 1671176 | tf_op jit(solution)/shard_map/reduce/ppermute | solution.py:455
  83.2 8.3 %all-to-all-start = ((bf16[64,4,640]{2,1,0:T(4,128)(2,1)}), bf16[64,4,640]{2,1,0:T(4,128)(2,1)S(1)}, u32[]{:S(2)}, u32[]{:S(2)}) async-start(bf16[64,4,640]{2,1,0:T(4,128)(2,1)} %add_convert_fusion), calls=%async_computation | async-start | bytes 655360 | tf_op jit(solution)/shard_map/reduce/all_to_all | solution.py:575
  91.5 0.9 copy-done.7
  92.4 1.0 band_adjoint.1.band
  93.4 0.9 fusion.3
  94.3 8.2 %collective-permute-done.8.lo = bf16[2,272,512]{2,1,0:T(8,128)(2,1)} collective-permute-done((bf16[2,272,512]{2,1,0:T(8,128)(2,1)}, bf16[2,272,512]{2,1,0:T(8,128)(2,1)}, u32[]{:S(2)}, u32[]{:S(2)}) %collective-permute-start.8) | collective-permute-done | bytes 557088 | tf_op jit(solution)/shard_map/reduce/ppermute | solution.py:455
  102.5 5.7 %collective-permute-done.9.hi = bf16[2,272,512]{2,1,0:T(8,128)(2,1)} collective-permute-done((bf16[2,272,512]{2,1,0:T(8,128)(2,1)}, bf16[2,272,512]{2,1,0:T(8,128)(2,1)}, u32[]{:S(2)}, u32[]{:S(2)}) %collective-permute-start.9) | collective-permute-done | bytes 557088 | tf_op jit(solution)/shard_map/reduce/ppermute | solution.py:455
  108.2 1.2 copy-done.3
  109.4 0.8 copy-done.9
  110.2 3.8 %adjoint_inner.1.partial_out = bf16[8,256,512]{2,1,0:T(8,128)(2,1)} custom-call(bf16[4,256,512]{2,1,0:T(8,128)(2,1)S(1)} %copy-done.3, bf16[4,16,512]{2,1,0:T(8,128)(2,1)S(1)} %get-tuple-element.86.mid_side, bf16[4,256,512]{2,1,0:T(8,128)(2,1)S(1)} %copy-done, bf16[4,16,512]{2,1,0:T(8,128)(2,1)S(1)} %get-tuple-element.85.end_side, ...), custom_call_target="tpu_custom_call" | custom-call | flops 1811939328 | bytes 3145728 | tf_op jit(solution)/shard_map/reduce/adjoint_inner/pallas_call | solution.py:399
  114.0 0.8 copy-done.2
  114.8 0.6 copy-done.5
  115.4 0.3 sum_shares.1
  115.7 0.7 broadcast_in_dim.3
  116.4 10.4 %all-to-all-start.1 = ((f32[256,1,128]{2,1,0:T(1,128)}), f32[256,1,128]{2,1,0:T(1,128)S(1)}, u32[]{:S(2)}, u32[]{:S(2)}) async-start(f32[256,1,128]{2,1,0:T(1,128)} %broadcast_in_dim.3), calls=%async_computation.1 | async-start | bytes 262144 | tf_op jit(solution)/shard_map/norm/all_to_all | solution.py:583
  126.9 1.3 collective-permute-start.12
  128.2 0.4 collective-permute-start.11
  128.5 0.6 collective-permute-start.10
  129.1 5.6 %adjoint_outer.1 = bf16[8,256,512]{2,1,0:T(8,128)(2,1)} custom-call(bf16[4,256,512]{2,1,0:T(8,128)(2,1)} %get-tuple-element.51.mid, bf16[4,16,512]{2,1,0:T(8,128)(2,1)} %copy-done.5, bf16[4,256,512]{2,1,0:T(8,128)(2,1)} %get-tuple-element.45.end, bf16[4,16,512]{2,1,0:T(8,128)(2,1)} %copy-done.4, ...), custom_call_target="tpu_custom_call", output_to_operand_aliasing={{}: (9, {})} | custom-call | flops 1811939328 | bytes 3145728 | tf_op jit(solution)/shard_map/adjoint_outer/pallas_call | solution.py:419
  134.8 4.1 %all-to-all-done.1.every = f32[256,1,128]{2,1,0:T(1,128)S(1)} async-done(((f32[256,1,128]{2,1,0:T(1,128)}), f32[256,1,128]{2,1,0:T(1,128)S(1)}, u32[]{:S(2)}, u32[]{:S(2)}) %all-to-all-start.1) | async-done | bytes 131104 | tf_op jit(solution)/shard_map/norm/all_to_all | solution.py:583
  138.9 1.5 %scaled.1 = (f32[8,512]{1,0:T(8,128)}, f32[512,8]{1,0:T(8,128)S(1)}, f32[8,9]{1,0:T(8,128)}) custom-call(s32[2]{0:T(128)S(1)} %pad_add_fusion.flags, f32[256,1,128]{2,1,0:T(1,128)S(1)} %all-to-all-done.1.every, f32[4,512]{1,0:T(4,128)S(1)} %slice.74.mats, f32[4,512]{1,0:T(4,128)S(1)} %collective-permute-done.10.near, ...), custom_call_target="tpu_custom_call" | custom-call | tf_op jit(solution)/shard_map/norm/scaled/pallas_call | solution.py:509
  140.4 0.7 copy.26
  (61 shorter events, 1.2 us)
Async XLA Ops:
  0.6 4.1 %copy-start.16 = (s32[512,5]{0,1:T(8,128)S(1)}, s32[512,5]{0,1:T(8,128)}, u32[]{:S(2)}) copy-start(s32[512,5]{0,1:T(8,128)} %param.14) | copy-start | bytes 30724
  0.6 4.3 %copy-start.12 = (s32[512,5,9]{0,1,2:T(8,128)S(1)}, s32[512,5,9]{0,1,2:T(8,128)}, u32[]{:S(2)}) copy-start(s32[512,5,9]{0,1,2:T(8,128)} %param.13) | copy-start | bytes 276484
  1.6 3.8 %collective-permute-start.1 = (bf16[8,8,512]{2,1,0:T(8,128)(2,1)S(1)}, bf16[8,8,512]{2,1,0:T(8,128)(2,1)S(1)}, u32[]{:S(2)}, u32[]{:S(2)}) collective-permute-start(bf16[8,8,512]{2,1,0:T(8,128)(2,1)S(1)} %get-tuple-element.81), channel_id=1, source_target_pairs={{0,1},{1,2},{2,3},{3,0},{4,5},{5,6},{6,7},{7,4},{8,9},{9,10},{10,1... | collective-permute-start | bytes 196616 | tf_op jit(solution)/shard_map/input_halo/ppermute | solution.py:444
  1.7 3.7 %collective-permute-start = (bf16[8,8,512]{2,1,0:T(8,128)(2,1)S(1)}, bf16[8,8,512]{2,1,0:T(8,128)(2,1)S(1)}, u32[]{:S(2)}, u32[]{:S(2)}) collective-permute-start(bf16[8,8,512]{2,1,0:T(8,128)(2,1)S(1)} %get-tuple-element.82), channel_id=1, source_target_pairs={{0,3},{1,0},{2,1},{3,2},{4,7},{5,4},{6,5},{7,6},{8,11},{9,8},{10,9... | collective-permute-start | bytes 196616 | tf_op jit(solution)/shard_map/input_halo/ppermute | solution.py:443
  5.3 12.6 %copy-start.13 = (f32[512,5,9]{0,1,2:T(8,128)S(1)}, f32[512,5,9]{0,1,2:T(8,128)}, u32[]{:S(2)}) copy-start(f32[512,5,9]{0,1,2:T(8,128)} %param.12) | copy-start | bytes 276484
  5.4 12.8 %copy-start.14 = (bf16[8,16,512]{2,1,0:T(8,128)(2,1)}, bf16[8,16,512]{2,1,0:T(8,128)(2,1)S(1)}, u32[]{:S(2)}) copy-start(bf16[8,16,512]{2,1,0:T(8,128)(2,1)S(1)} %constant_dynamic-update-slice_fusion.side) | copy-start | bytes 393220
  5.4 12.9 %copy-start.8 = (bf16[60,2048]{1,0:T(8,128)(2,1)S(1)}, bf16[60,2048]{1,0:T(8,128)(2,1)}, u32[]{:S(2)}) copy-start(bf16[60,2048]{1,0:T(8,128)(2,1)} %constant.47.clone.pick) | copy-start | bytes 737284
  5.5 29.8 %collective-permute-start.2 = (bf16[2,272,512]{2,1,0:T(8,128)(2,1)S(1)}, bf16[2,272,512]{2,1,0:T(8,128)(2,1)S(1)}, u32[]{:S(2)}, u32[]{:S(2)}) collective-permute-start(bf16[2,272,512]{2,1,0:T(8,128)(2,1)S(1)} %pad_maximum_fusion), channel_id=1, source_target_pairs={{0,4},{4,8},{8,12},{12,16},{16,20},{20,24},{24,28},{28,32},{32,36}... | collective-permute-start | bytes 1671176 | tf_op jit(solution)/shard_map/input_halo/ppermute | solution.py:455
  10.8 30.6 %collective-permute-start.3 = (bf16[2,272,512]{2,1,0:T(8,128)(2,1)S(1)}, bf16[2,272,512]{2,1,0:T(8,128)(2,1)S(1)}, u32[]{:S(2)}, u32[]{:S(2)}) collective-permute-start(bf16[2,272,512]{2,1,0:T(8,128)(2,1)S(1)} %pad_maximum_fusion.1), channel_id=1, source_target_pairs={{4,0},{8,4},{12,8},{16,12},{20,16},{24,20},{28,24},{32,28},{36,32}... | collective-permute-start | bytes 1671176 | tf_op jit(solution)/shard_map/input_halo/ppermute | solution.py:455
  19.3 0.8 copy-start.6
  35.3 6.1 %copy-start.17 = (bf16[2,272,512]{2,1,0:T(8,128)(2,1)}, bf16[2,272,512]{2,1,0:T(8,128)(2,1)S(1)}, u32[]{:S(2)}) copy-start(bf16[2,272,512]{2,1,0:T(8,128)(2,1)S(1)} %collective-permute-done.2.lo) | copy-start | bytes 1671172
  41.4 0.8 copy-start.18
  42.2 14.9 %copy-start.15 = (bf16[4,16,512]{2,1,0:T(8,128)(2,1)S(1)}, bf16[4,16,512]{2,1,0:T(8,128)(2,1)}, u32[]{:S(2)}) copy-start(bf16[4,16,512]{2,1,0:T(8,128)(2,1)} %get-tuple-element.47) | copy-start | bytes 196612
  57.0 4.0 %collective-permute-start.4 = (bf16[512,640]{1,0:T(8,128)(2,1)}, bf16[512,640]{1,0:T(8,128)(2,1)S(1)}, u32[]{:S(2)}, u32[]{:S(2)}) collective-permute-start(bf16[512,640]{1,0:T(8,128)(2,1)} %get-tuple-element.44), channel_id=1, source_target_pairs={{0,1},{1,0},{2,3},{3,2},{4,5},{5,4},{6,7},{7,6},{8,9},{9,8},{10,11... | collective-permute-start | bytes 1966088 | tf_op jit(solution)/shard_map/reduce/ppermute | solution.py:459
  57.1 3.8 %copy-start.10 = (f32[512,640]{1,0:T(8,128)S(1)}, f32[512,640]{1,0:T(8,128)}, u32[]{:S(2)}) copy-start(f32[512,640]{1,0:T(8,128)} %get-tuple-element.43) | copy-start | bytes 3932164
  57.1 3.8 %collective-permute-start.7 = (bf16[8,8,512]{2,1,0:T(8,128)(2,1)S(1)}, bf16[8,8,512]{2,1,0:T(8,128)(2,1)S(1)}, u32[]{:S(2)}, u32[]{:S(2)}) collective-permute-start(bf16[8,8,512]{2,1,0:T(8,128)(2,1)S(1)} %get-tuple-element.89), channel_id=1, source_target_pairs={{0,1},{1,2},{2,3},{3,0},{4,5},{5,6},{6,7},{7,4},{8,9},{9,10},{10,1... | collective-permute-start | bytes 196616 | tf_op jit(solution)/shard_map/grad_halo/ppermute | solution.py:444
  57.6 3.3 %collective-permute-start.6 = (bf16[8,8,512]{2,1,0:T(8,128)(2,1)S(1)}, bf16[8,8,512]{2,1,0:T(8,128)(2,1)S(1)}, u32[]{:S(2)}, u32[]{:S(2)}) collective-permute-start(bf16[8,8,512]{2,1,0:T(8,128)(2,1)S(1)} %get-tuple-element.90), channel_id=1, source_target_pairs={{0,3},{1,0},{2,1},{3,2},{4,7},{5,4},{6,5},{7,6},{8,11},{9,8},{10,9... | collective-permute-start | bytes 196616 | tf_op jit(solution)/shard_map/grad_halo/ppermute | solution.py:443
  60.9 11.8 %copy-start.11 = (bf16[8,16,512]{2,1,0:T(8,128)(2,1)}, bf16[8,16,512]{2,1,0:T(8,128)(2,1)S(1)}, u32[]{:S(2)}) copy-start(bf16[8,16,512]{2,1,0:T(8,128)(2,1)S(1)} %constant_dynamic-update-slice_fusion.4) | copy-start | bytes 393220
  61.3 10.4 %collective-permute-start.5 = (bf16[64,4,640]{2,1,0:T(4,128)(2,1)S(1)}, bf16[64,4,640]{2,1,0:T(4,128)(2,1)S(1)}, u32[]{:S(2)}, u32[]{:S(2)}) collective-permute-start(bf16[64,4,640]{2,1,0:T(4,128)(2,1)S(1)} %select_convert_fusion), channel_id=1, source_target_pairs={{0,2},{1,3},{2,0},{3,1},{4,6},{5,7},{6,4},{7,5},{8,10},{9,11},{10,... | collective-permute-start | bytes 983048 | tf_op jit(solution)/shard_map/reduce/ppermute | solution.py:459
  71.7 36.5 %copy-start.1 = (bf16[8,256,512]{2,1,0:T(8,128)(2,1)S(1)}, bf16[8,256,512]{2,1,0:T(8,128)(2,1)}, u32[]{:S(2)}) copy-start(bf16[8,256,512]{2,1,0:T(8,128)(2,1)} %cot.7) | copy-start | bytes 6291460
  72.7 35.5 %copy-start = (bf16[4,256,512]{2,1,0:T(8,128)(2,1)S(1)}, bf16[4,256,512]{2,1,0:T(8,128)(2,1)}, u32[]{:S(2)}) copy-start(bf16[4,256,512]{2,1,0:T(8,128)(2,1)} %get-tuple-element.45.end) | copy-start | bytes 3145732
  72.7 29.8 %collective-permute-start.8 = (bf16[2,272,512]{2,1,0:T(8,128)(2,1)}, bf16[2,272,512]{2,1,0:T(8,128)(2,1)}, u32[]{:S(2)}, u32[]{:S(2)}) collective-permute-start(bf16[2,272,512]{2,1,0:T(8,128)(2,1)} %get-tuple-element.48), channel_id=1, source_target_pairs={{0,4},{4,8},{8,12},{12,16},{16,20},{20,24},{24,28},{28,32},{32,36}... | collective-permute-start | bytes 1671176 | tf_op jit(solution)/shard_map/reduce/ppermute | solution.py:455
  74.7 33.5 %collective-permute-start.9 = (bf16[2,272,512]{2,1,0:T(8,128)(2,1)}, bf16[2,272,512]{2,1,0:T(8,128)(2,1)}, u32[]{:S(2)}, u32[]{:S(2)}) collective-permute-start(bf16[2,272,512]{2,1,0:T(8,128)(2,1)} %get-tuple-element.49), channel_id=1, source_target_pairs={{4,0},{8,4},{12,8},{16,12},{20,16},{24,20},{28,24},{32,28},{36,32}... | collective-permute-start | bytes 1671176 | tf_op jit(solution)/shard_map/reduce/ppermute | solution.py:455
  83.2 32.2 %all-to-all-start = ((bf16[64,4,640]{2,1,0:T(4,128)(2,1)}), bf16[64,4,640]{2,1,0:T(4,128)(2,1)S(1)}, u32[]{:S(2)}, u32[]{:S(2)}) async-start(bf16[64,4,640]{2,1,0:T(4,128)(2,1)} %add_convert_fusion), calls=%async_computation | async-start | bytes 655360 | tf_op jit(solution)/shard_map/reduce/all_to_all | solution.py:575
  91.5 1.0 copy-start.7
  94.3 19.7 %copy-start.4 = (bf16[4,16,512]{2,1,0:T(8,128)(2,1)}, bf16[4,16,512]{2,1,0:T(8,128)(2,1)S(1)}, u32[]{:S(2)}) copy-start(bf16[4,16,512]{2,1,0:T(8,128)(2,1)S(1)} %get-tuple-element.85.end_side) | copy-start | bytes 196612
  108.2 1.2 copy-start.3
  109.4 0.8 copy-start.9
  114.0 0.8 copy-start.2
  114.8 0.6 copy-start.5
  116.4 22.4 %all-to-all-start.1 = ((f32[256,1,128]{2,1,0:T(1,128)}), f32[256,1,128]{2,1,0:T(1,128)S(1)}, u32[]{:S(2)}, u32[]{:S(2)}) async-start(f32[256,1,128]{2,1,0:T(1,128)} %broadcast_in_dim.3), calls=%async_computation.1 | async-start | bytes 262144 | tf_op jit(solution)/shard_map/norm/all_to_all | solution.py:583
  126.9 7.8 %collective-permute-start.12 = (f32[4,512]{1,0:T(4,128)S(1)}, f32[4,512]{1,0:T(4,128)S(1)}, u32[]{:S(2)}, u32[]{:S(2)}) collective-permute-start(f32[4,512]{1,0:T(4,128)S(1)} %slice.74.mats), channel_id=1, source_target_pairs={{0,3},{1,2},{2,1},{3,0},{4,7},{5,6},{6,5},{7,4},{8,11},{9,10},{10,... | collective-permute-start | bytes 24584 | tf_op jit(solution)/shard_map/norm/ppermute | solution.py:459
  128.2 6.6 %collective-permute-start.11 = (f32[4,512]{1,0:T(4,128)S(1)}, f32[4,512]{1,0:T(4,128)S(1)}, u32[]{:S(2)}, u32[]{:S(2)}) collective-permute-start(f32[4,512]{1,0:T(4,128)S(1)} %slice.74.mats), channel_id=1, source_target_pairs={{0,1},{1,0},{2,3},{3,2},{4,5},{5,4},{6,7},{7,6},{8,9},{9,8},{10,11... | collective-permute-start | bytes 24584 | tf_op jit(solution)/shard_map/norm/ppermute | solution.py:459
  128.5 6.2 %collective-permute-start.10 = (f32[4,512]{1,0:T(4,128)S(1)}, f32[4,512]{1,0:T(4,128)S(1)}, u32[]{:S(2)}, u32[]{:S(2)}) collective-permute-start(f32[4,512]{1,0:T(4,128)S(1)} %slice.74.mats), channel_id=1, source_target_pairs={{0,2},{1,3},{2,0},{3,1},{4,6},{5,7},{6,4},{7,5},{8,10},{9,11},{10,... | collective-permute-start | bytes 24584 | tf_op jit(solution)/shard_map/norm/ppermute | solution.py:459
